TPU v7x, 32 devices: a whole 2x2x4 slice. The times are simulated.
32 devices in a mesh: section: 8 (over y, x, core), peer: 4 (over z).
Axes of the slice: x: 2, y: 2, z: 4, core: 2. Of those that a mesh axis runs over, the one named last changes fastest.
Arguments:
- inputs: bfloat16 [8, 4, 128, 5120], P('section', 'peer'), may hold values from -6 to 6
- out_grad: bfloat16 [8, 4, 128, 5120], P('section', 'peer'), may hold values from -6 to 6
- gains: float32 [8, 5120], P('section'), may hold values from 0.1 to 1.9
- down_proj: bfloat16 [8, 5120, 128], P('section'), may hold values from -0.078125 to 0.078125
- up_proj: bfloat16 [8, 128, 5120], P('section'), may hold values from -0.5 to 0.5
- wiring: int32 [8, 4, 4], replicated, may hold values from 0 to 2, as said below
- pair_mask: int32 [8], replicated, may hold values from 1 to 3
Outputs:
- next_inputs: bfloat16 [8, 4, 128, 5120], P('section', 'peer')
- returned_grad: bfloat16 [8, 4, 128, 5120], P('section', 'peer')
- grad_down: float32 [8, 4, 5120, 128], P('section', 'peer')
- grad_up: float32 [8, 4, 128, 5120], P('section', 'peer')
Inputs may be any that keep to these rules, and one draw needn't show every extreme that they name: For each section, every row and every column of wiring sums to 4; entries are 0, 1 or 2, and 2 occurs in every row and every column. `pair_mask`: 4 is a power of two; each section's mask is nonzero.
All inputs are finite; a program needn't handle non-finite values.
Results may differ from a plain program's by a relative error of at most 0.006.
Values may be sent and summed in bfloat16 or wider, within the bound.
No kernel may reach another device: no remote copies, remote signals or barrier semaphores. Data moves between devices by JAX's collectives and lax.ppermute only.
A program may use at most 128 MiB of HBM per device.

v0:
```python
import functools

import jax
import jax.numpy as jnp
from jax import lax
from jax.experimental import pallas as pl
from jax.experimental.pallas import tpu as pltpu
from jax.sharding import PartitionSpec as P

CAP = 2
TILE = 512
CHUNKS = (2, 2, 2, 2, 2)
STAGES = (((0, 1, 2), (0, 1)), ((3, 4), (2, 3)), ((), (4,)))
DEPTH = 1
F32, BF16 = jnp.float32, jnp.bfloat16


def passed_along(block, axis, distance):
    devices = range(lax.axis_size(axis))
    route = [((i - distance) % len(devices), i) for i in devices]
    return lax.ppermute(block, axis, route)


def swapped(block, axis, mask):
    count = lax.axis_size(axis)
    return lax.ppermute(block, axis, [(i, i ^ mask) for i in range(count) if i ^ mask < count])


def after(value, *others):
    return lax.optimization_barrier((value, *others))[0]


def dot(a, b, dims):
    return lax.dot_general(a, b, (dims, ((), ())), preferred_element_type=F32)


PIECE = 1024
FREE = pl.CostEstimate(flops=0, bytes_accessed=0, transcendentals=0)
ROOM = pltpu.CompilerParams(vmem_limit_bytes=32 * 2**20)
SMEM = pl.BlockSpec(memory_space=pltpu.SMEM)


def open_kernel(widths, wiring_ref, mask_ref, g_ref, x_ref, dy_ref, down_ref, up_ref, plan_ref, choice_ref, low_ref,
                high_ref, *refs):
    outs = refs[: len(widths)]
    x_scr, dy_scr, down_scr, up_scr, extra, in_sems, out_sems, extra_sem = refs[len(widths) :]
    rows, width = x_ref.shape
    rank = up_ref.shape[0]
    pieces = [slice(i, i + PIECE) for i in range(0, width, PIECE)]
    loads = []
    for i, at in enumerate(pieces):
        pairs = ((x_ref.at[:, at], x_scr.at[:, at]), (dy_ref.at[:, at], dy_scr.at[:, at]),
                 (down_ref.at[at, :], down_scr.at[at, :]), (up_ref.at[:, at], up_scr.at[:, at]))
        loads.append([pltpu.make_async_copy(s, t, in_sems.at[4 * i + n]) for n, (s, t) in enumerate(pairs)])
    for some in loads:
        for copy in some:
            copy.start()
    stores, first = [], 0
    for c, cols in enumerate(widths):
        for n, scr in enumerate((x_scr, dy_scr)):
            to = outs[c].at[pl.ds(n * rows, rows), :]
            stores.append((first + cols, pltpu.make_async_copy(scr.at[:, pl.ds(first, cols)], to, out_sems.at[2 * c + n])))
        first += cols

    section, peer = lax.axis_index("section"), lax.axis_index("peer")
    count = wiring_ref.shape[0]
    before = lax.rem(section + count - 1, count)
    mask = mask_ref[section]
    match = peer ^ mask
    other = peer ^ jnp.where(mask >= 2, 1, 2)

    def sources(back, q):
        at = [jnp.int32(0)] * 4
        block = [jnp.int32(0)] * 4
        cum = jnp.int32(0)
        for i in range(4):
            first = jnp.int32(0)
            for j in range(4):
                if back:
                    first += jnp.where(j < q, wiring_ref[before, j, i], 0)
                else:
                    first += jnp.where(j < q, wiring_ref[section, i, j], 0)
            amount = wiring_ref[before, q, i] if back else wiring_ref[section, i, q]
            for k in range(4):
                inside = (cum <= k) & (k < cum + amount)
                at[k] = jnp.where(inside, i, at[k])
                block[k] = jnp.where(inside, first + k - cum, block[k])
            cum += amount
        held = [((a == peer) | (a == match)).astype(jnp.int32) for a in at]
        index = [jnp.where(a == peer, b, 4 + b) for a, b in zip(at, block)]
        return held, index

    for n, back in enumerate((False, True)):
        held, index = sources(back, other)
        order = jnp.int32(0)
        orders = []
        for k in range(4):
            orders.append(order)
            order += held[k]
        for j in range(4):
            pick = jnp.int32(0)
            for k in range(4):
                pick += jnp.where((held[k] == 1) & (orders[k] == j), index[k], 0)
            plan_ref[4 * n + j] = pick
        held, index = sources(back, peer)
        order = jnp.int32(0)
        for k in range(4):
            plan_ref[8 + 4 * n + k] = jnp.where(held[k] == 1, index[k], 8 + order)
            order += 1 - held[k]
    twos = jnp.int32(0)
    for at in (section, before):
        for i in range(4):
            for j in range(4):
                twos += jnp.where(wiring_ref[at, i, j] == 2, 1, 0)
    choice_ref[0] = mask - 1 + jnp.where(twos > 8, 3, 0)

    square = jnp.zeros((rows, 1), F32)
    pre = jnp.zeros((rows, rank), F32)
    dact = jnp.zeros((rows, rank), F32)
    for some, at in zip(loads, pieces):
        for copy in some:
            copy.wait()
        for end, copy in stores:
            if at.start < end <= at.stop:
                copy.start()
        x = x_scr[:, at].astype(F32)
        square += jnp.sum(x * x, axis=1, keepdims=True)
        pre += dot((x * g_ref[:, at]).astype(BF16), down_scr[at, :], ((1,), (0,)))
        dact += dot(dy_scr[:, at], up_scr[:, at], ((1,), (1,)))
    rinv = lax.rsqrt(square / width + 1e-05)
    v = pre * rinv
    sig = jax.nn.sigmoid(v)
    act = (v * sig).astype(BF16)
    dpre = (dact * sig * (1.0 + v * (1.0 - sig))).astype(BF16)
    inner = jnp.sum(dpre.astype(F32) * v, axis=1, keepdims=True) / width
    weight = rinv * rinv * inner
    low_ref[:rows, :] = act
    low_ref[rows:, :] = dpre
    lane = lax.broadcasted_iota(jnp.int32, (rows, rows), 1)
    high = jnp.where(lane == 0, rinv, weight).T[:8, :]
    high_ref[...] = high
    bands = widths[0] // rank
    band = 2 * rows // bands
    for j in range(bands):
        from_ref = act if (j + 1) * band <= rows else dpre
        start = j * band % rows
        extra[:band, j * rank : (j + 1) * rank] = from_ref[start : start + band, :]
    rest = high
    parts = []
    for _ in range(3):
        part = rest.astype(BF16)
        parts.append(part)
        rest = rest - part.astype(F32)
    extra[band:, :] = jnp.zeros_like(extra[band:, :])
    extra[band : band + 16, 0:rows] = jnp.concatenate([parts[0], parts[1]], axis=0)
    extra[band : band + 16, rows : 2 * rows] = jnp.concatenate([parts[2], parts[2]], axis=0)
    last = pltpu.make_async_copy(extra, outs[0].at[pl.ds(2 * rows, band + 16), :], extra_sem)
    last.start()
    for _, copy in stores:
        copy.wait()
    last.wait()


def make_open(widths, wiring, pair_mask, g, x, dy, down, up):
    rows, width = x.shape
    rank = up.shape[0]
    band = 2 * rows * rank // widths[0]
    hbm = pl.BlockSpec(memory_space=pl.ANY)
    vmem = pl.BlockSpec(memory_space=pltpu.VMEM)
    tall = [2 * rows + band + 16] + [2 * rows] * (len(widths) - 1)
    return pl.pallas_call(
        functools.partial(open_kernel, widths),
        out_shape=[
            jax.ShapeDtypeStruct((16,), jnp.int32),
            jax.ShapeDtypeStruct((1,), jnp.int32),
            jax.ShapeDtypeStruct((2 * rows, rank), BF16),
            jax.ShapeDtypeStruct((8, rows), F32),
        ] + [jax.ShapeDtypeStruct((n, cols), BF16) for n, cols in zip(tall, widths)],
        in_specs=[SMEM, SMEM, vmem, hbm, hbm, hbm, hbm],
        out_specs=[SMEM, SMEM, vmem, vmem] + [hbm] * len(widths),
        scratch_shapes=[
            pltpu.VMEM((rows, width), BF16), pltpu.VMEM((rows, width), BF16),
            pltpu.VMEM((width, rank), BF16), pltpu.VMEM((rank, width), BF16),
            pltpu.VMEM((band + 16, widths[0]), BF16),
            pltpu.SemaphoreType.DMA((4 * (width // PIECE),)), pltpu.SemaphoreType.DMA((2 * len(widths),)),
            pltpu.SemaphoreType.DMA,
        ],
        compiler_params=ROOM,
        cost_estimate=FREE,
        name="open",
    )(wiring, pair_mask, g, x, dy, down, up)


def unpack_kernel(got_ref, low_ref, high_ref):
    rows2, rank = low_ref.shape
    bands = got_ref.shape[1] // rank
    band = rows2 // bands
    rows = rows2 // 2
    for j in range(bands):
        low_ref[j * band : (j + 1) * band, :] = got_ref[rows2 : rows2 + band, j * rank : (j + 1) * rank]
    parts = got_ref[rows2 + band : rows2 + band + 16, :].astype(F32)
    high_ref[...] = parts[0:8, 0:rows] + parts[8:16, 0:rows] + parts[0:8, rows : 2 * rows]


def make_unpack(got, low, high):
    vmem = pl.BlockSpec(memory_space=pltpu.VMEM)
    return pl.pallas_call(
        unpack_kernel,
        out_shape=(jax.ShapeDtypeStruct(low.shape, BF16), jax.ShapeDtypeStruct(high.shape, F32)),
        in_specs=[vmem],
        out_specs=(vmem, vmem),
        compiler_params=ROOM,
        cost_estimate=FREE,
        name="unpack",
    )(got)


def whole(shape):
    return pl.BlockSpec(shape, lambda i: (0,) * len(shape))


def column(rows, first=0):
    return pl.BlockSpec((rows, TILE), lambda i: (0, first + i))


def chunk(rows, start, end):
    return pl.BlockSpec((rows, TILE), lambda i: (0, jnp.clip(i - start, 0, end - start - 1)))


def rows_kernel(cap, blk, plan_ref, x_ref, dy_ref, got_ref, low_ref, low2_ref, high_ref, high2_ref, up_ref, down_ref,
                g_ref, send_ref, keep_f_ref, keep_b_ref, out_scr, dx_scr):
    rows = x_ref.shape[0]
    for half in range(2):
        part = pl.ds(half * rows, rows)
        x = (x_ref[...] if half == 0 else got_ref[:rows, :]).astype(F32)
        dy = (dy_ref[...] if half == 0 else got_ref[rows:, :]).astype(F32)
        low = low_ref if half == 0 else low2_ref
        stat = (high_ref if half == 0 else high2_ref)[...].T
        out = x + dot(low[:rows, :], up_ref[...], ((1,), (0,)))
        out_scr[part, :] = out.astype(BF16)
        dn = dot(low[rows:, :], down_ref[...], ((1,), (1,))) * g_ref[...]
        dx = dy + stat[:, 0:1] * dn - x * stat[:, 1:2]
        dx_scr[part, :] = dx.astype(BF16)

    def block_of(scr, index):
        return scr[pl.ds(pl.multiple_of(index * blk, blk), blk), :]

    for n, scr in enumerate((out_scr, dx_scr)):
        for j in range(cap):
            send_ref[pl.ds((n * cap + j) * blk, blk), :] = block_of(scr, plan_ref[4 * n + j])
    for n, (scr, keep_ref) in enumerate(((out_scr, keep_f_ref), (dx_scr, keep_b_ref))):
        for k in range(4):
            keep_ref[pl.ds(k * blk, blk), :] = block_of(scr, jnp.minimum(plan_ref[8 + 4 * n + k], 7))


def make_rows(cap, first, tiles, plan, x, dy, got, low, low2, high, high2, up, down, g):
    rows, width = x.shape
    rank = up.shape[0]
    blk = rows // 4
    cols = tiles * TILE
    return pl.pallas_call(
        functools.partial(rows_kernel, cap, blk),
        grid=(tiles,),
        out_shape=(
            jax.ShapeDtypeStruct((2 * cap * blk, cols), BF16),
            jax.ShapeDtypeStruct((rows, cols), BF16),
            jax.ShapeDtypeStruct((rows, cols), BF16),
        ),
        in_specs=[
            SMEM, column(rows, first), column(rows, first), column(2 * rows),
            whole(low.shape), whole(low.shape), whole(high.shape), whole(high.shape),
            column(rank, first), pl.BlockSpec((TILE, rank), lambda i: (first + i, 0)), column(1, first),
        ],
        out_specs=(column(2 * cap * blk), column(rows), column(rows)),
        scratch_shapes=[pltpu.VMEM((2 * rows, TILE), BF16), pltpu.VMEM((2 * rows, TILE), BF16)],
        compiler_params=ROOM,
        cost_estimate=FREE,
        name="rows",
    )(plan, x, dy, got, low, low2, high, high2, up, down, g)


def merge_kernel(cap, blk, spans, plan_ref, *refs):
    outs, sems = refs[-3:-1], refs[-1]
    waits = []
    for c, (first, cols) in enumerate(spans):
        keeps, got = refs[3 * c : 3 * c + 2], refs[3 * c + 2]
        for n in range(2):
            for k in range(4):
                index = plan_ref[8 + 4 * n + k]
                rows = pl.ds(k * blk, blk)
                to = outs[n].at[rows, pl.ds(first, cols)]
                sem = sems.at[8 * c + 4 * n + k]
                row = pl.multiple_of((n * cap + jnp.clip(index - 8, 0, cap - 1)) * blk, blk)
                here = pltpu.make_async_copy(keeps[n].at[rows, :], to, sem)
                there = pltpu.make_async_copy(got.at[pl.ds(row, blk), :], to, sem)

                @pl.when(index < 8)
                def _():
                    here.start()

                @pl.when(index >= 8)
                def _():
                    there.start()

                waits.append(here)
    for copy in waits:
        copy.wait()


def make_merge(cap, plan, parts):
    rows = parts[0][0].shape[0]
    spans, first = [], 0
    for keep_f, _, _ in parts:
        spans.append((first, keep_f.shape[1]))
        first += keep_f.shape[1]
    hbm = pl.BlockSpec(memory_space=pl.ANY)
    return pl.pallas_call(
        functools.partial(merge_kernel, cap, rows // 4, tuple(spans)),
        out_shape=(jax.ShapeDtypeStruct((rows, first), BF16),) * 2,
        in_specs=[SMEM] + [hbm] * (3 * len(parts)),
        out_specs=(hbm, hbm),
        scratch_shapes=[pltpu.SemaphoreType.DMA((8 * len(parts),))],
        compiler_params=ROOM,
        cost_estimate=FREE,
        name="merge",
    )(plan, *[array for part in parts for array in part])


def join_kernel(places, *refs):
    count = len(places)
    sems = refs[-1]
    outs = refs[-3:-1]
    parts = refs[-3 - 2 * count : -3]
    copies = []
    for n in range(2):
        for i, (first, cols) in enumerate(places):
            copies.append(
                pltpu.make_async_copy(parts[n * count + i], outs[n].at[:, pl.ds(first, cols)], sems.at[n * count + i])
            )
    for copy in copies:
        copy.start()
    for copy in copies:
        copy.wait()


def make_join(width, first, nexts, returns, into=()):
    rows = nexts[0].shape[0]
    places = []
    for part in nexts:
        places.append((first, part.shape[1]))
        first += part.shape[1]
    hbm = pl.BlockSpec(memory_space=pl.ANY)
    return pl.pallas_call(
        functools.partial(join_kernel, tuple(places)),
        out_shape=(jax.ShapeDtypeStruct((rows, width), BF16),) * 2,
        in_specs=[hbm] * (len(into) + 2 * len(nexts)),
        out_specs=(hbm, hbm),
        scratch_shapes=[pltpu.SemaphoreType.DMA((2 * len(nexts),))],
        input_output_aliases={i: i for i in range(len(into))},
        compiler_params=ROOM,
        cost_estimate=FREE,
        name="join",
    )(*into, *nexts, *returns)


def grads_kernel(starts, x_ref, dy_ref, *refs):
    got_refs = refs[: len(starts) - 1]
    low_ref, low2_ref, high_ref, high2_ref, g_ref = refs[len(starts) - 1 : len(starts) + 4]
    gup_ref, gdown_ref, x_scr, dy_scr, act_scr, dpre_scr, rinv_scr = refs[-7:]
    step = pl.program_id(0)
    rows = x_ref.shape[0]

    @pl.when(step == 0)
    def _():
        for half, (low, high) in enumerate(((low_ref, high_ref), (low2_ref, high2_ref))):
            part = pl.ds(half * rows, rows)
            act_scr[part, :] = (low[:rows, :].astype(F32) * 0.5).astype(BF16)
            dpre_scr[part, :] = (low[rows:, :].astype(F32) * 0.5).astype(BF16)
            rinv_scr[part, :] = high[...].T[:, 0:1]

    dy_scr[:rows, :] = dy_ref[...]
    x_scr[:rows, :] = x_ref[...]
    for c, got_ref in enumerate(got_refs):

        @pl.when((step >= starts[c]) & (step < starts[c + 1]))
        def _():
            x_scr[rows:, :] = got_ref[:rows, :]
            dy_scr[rows:, :] = got_ref[rows:, :]

    gup_ref[...] = dot(act_scr[...], dy_scr[...], ((0,), (0,)))
    normed = (x_scr[...].astype(F32) * rinv_scr[...] * g_ref[...]).astype(BF16)
    gdown_ref[...] = dot(normed, dpre_scr[...], ((0,), (0,)))


def make_grads(first, x, dy, got, low, low2, high, high2, g, into=()):
    rows, width = x.shape
    rank = low.shape[1]
    starts = [0]
    for block in got:
        starts.append(starts[-1] + block.shape[1] // TILE)

    def kernel(*refs):
        grads_kernel(tuple(starts), *refs[len(into):])

    return pl.pallas_call(
        kernel,
        grid=(starts[-1],),
        out_shape=(jax.ShapeDtypeStruct((rank, width), F32), jax.ShapeDtypeStruct((width, rank), F32)),
        in_specs=[pl.BlockSpec(memory_space=pl.ANY)] * len(into)
        + [column(rows, first), column(rows, first)] + [chunk(2 * rows, s, e) for s, e in zip(starts[:-1], starts[1:])]
        + [whole(low.shape), whole(low.shape), whole(high.shape), whole(high.shape), column(1, first)],
        out_specs=(column(rank, first), pl.BlockSpec((TILE, rank), lambda i: (first + i, 0))),
        scratch_shapes=[
            pltpu.VMEM((2 * rows, TILE), BF16), pltpu.VMEM((2 * rows, TILE), BF16),
            pltpu.VMEM((2 * rows, rank), BF16), pltpu.VMEM((2 * rows, rank), BF16), pltpu.VMEM((2 * rows, 1), F32),
        ],
        input_output_aliases={i: i for i in range(len(into))},
        compiler_params=ROOM,
        cost_estimate=FREE,
        name="grads",
    )(*into, x, dy, *got, low, low2, high, high2, g)


def four_peers(inputs, out_grad, gains, down_proj, up_proj, wiring, pair_mask):
    x, dy, down, up = inputs[0, 0], out_grad[0, 0], down_proj[0], up_proj[0]
    width = x.shape[1]
    count = len(CHUNKS)
    early = count - 1
    starts = [sum(CHUNKS[:c]) for c in range(count + 1)]
    plan, choice, low, high, *outs = make_open(
        [n * TILE for n in CHUNKS], wiring, pair_mask, gains, x, dy, down, up
    )
    choice = choice[0]

    def stage(number, cap, mask, state):
        exchange, route = STAGES[number]
        if number == 0:
            held = {}
        else:
            low2, high2, held, grads = state
        held, parts, backs, sent = dict(held), [], {}, plan

        def send_on(c):
            ready = [source[d] for source, d in ((held, c - DEPTH), (backs, c - DEPTH - 1)) if d in source]
            held[c] = swapped(after(outs[c], *ready) if ready else outs[c], "peer", mask)

        waiting = list(exchange)
        while waiting and (waiting[0] < exchange[0] + DEPTH):
            send_on(waiting.pop(0))
        if number == 0:
            low2, high2 = make_unpack(held[0], low, high)
        common = (low, low2, high, high2)
        for c in route:
            send, keep_f, keep_b = make_rows(
                cap, starts[c], CHUNKS[c], after(plan, sent), x, dy, held[c], *common, up, down, gains
            )
            backs[c] = swapped(send, "peer", 1 if mask >= 2 else 2)
            parts.append((keep_f, keep_b, backs[c]))
            sent = send
            if waiting:
                send_on(waiting.pop(0))
        while waiting:
            send_on(waiting.pop(0))
        if number == 0:
            grads = ()
        elif number == 1:
            grads = make_grads(0, after(x, sent), dy, [held[c] for c in range(early)], *common, gains)
        merged = make_merge(cap, after(plan, sent), parts)
        return merged, (low2, high2) if number == 0 else (), {c: held[c] for c in exchange}, grads

    state = None
    nexts, returns = [], []
    for number in range(len(STAGES)):
        branches = [functools.partial(stage, number, cap, m) for cap in (3, 4) for m in (1, 2, 3)]
        (f, b), made, arrived, grads = lax.switch(choice, branches, state)
        if number == 0:
            low2, high2 = made
            held = {}
        held = {**held, **arrived}
        state = (low2, high2, held, grads)
        if number:
            f, b = after(f, nexts[-1], returns[-1]), after(b, nexts[-1], returns[-1])
        nexts.append(passed_along(f, "section", 1))
        returns.append(passed_along(b, "section", -1))
    grad_up, grad_down = make_grads(
        starts[early], after(x, f, b), dy, [held[c] for c in range(early, count)], low, low2, high, high2, gains, into=grads
    )
    joined = make_join(width, 0, [after(nexts[0], f, b), *nexts[1:-1]], returns[:-1])
    done = sum(part.shape[1] for part in nexts[:-1])
    next_rows, return_rows = make_join(width, done, nexts[-1:], returns[-1:], into=joined)
    return next_rows[None, None], return_rows[None, None], grad_down[None, None], grad_up[None, None]


def adapter(x, dy, g, down, up):
    xf = x.astype(F32)
    rinv = lax.rsqrt(jnp.mean(xf * xf, axis=-1, keepdims=True) + 1e-05)
    normed = (xf * rinv * g).astype(BF16)
    pre = dot(normed, down, ((1,), (0,)))
    sig = jax.nn.sigmoid(pre)
    act = (pre * sig).astype(BF16)
    dact = dot(dy, up, ((1,), (1,)))
    dpre = (dact * sig * (1.0 + pre * (1.0 - sig))).astype(BF16)
    inner = jnp.sum(dpre.astype(F32) * pre, axis=-1, keepdims=True) / x.shape[1]
    return act, dpre, rinv, rinv * rinv * inner


def layer(x, dy, g, down, up):
    xf = x.astype(F32)
    act, dpre, rinv, weight = adapter(x, dy, g, down, up)
    normed = (xf * rinv * g).astype(BF16)
    out = (xf + dot(act, up, ((1,), (0,)))).astype(BF16)
    gup = dot(act, dy, ((0,), (0,))).astype(BF16)
    gdown = dot(normed, dpre, ((0,), (0,))).astype(BF16)
    dnorm = dot(dpre, down, ((1,), (1,))) * g
    dx = (dy.astype(F32) + rinv * dnorm - xf * weight).astype(BF16)
    return (out, dx, gdown, gup)


def pack_blocks(blocks, counts_vec, first_vec, slots):
    peers = counts_vec.shape[0]
    nblocks = blocks.shape[0]
    place = jnp.arange(slots, dtype=jnp.int32)
    source = first_vec[:, None] + place[None, :]
    valid = place[None, :] < counts_vec[:, None]
    select = (source[:, :, None] == jnp.arange(nblocks, dtype=jnp.int32)[None, None, :]) & valid[:, :, None]
    select = select.astype(BF16).reshape(peers * slots, nblocks)
    return jnp.dot(select, blocks, preferred_element_type=F32).astype(BF16)


def unpack_blocks(received, counts_vec, first_vec, slots, nblocks):
    place = jnp.arange(slots, dtype=jnp.int32)
    target = (first_vec[:, None] + place[None, :]).reshape(-1)
    valid = (place[None, :] < counts_vec[:, None]).reshape(-1)
    select = (target[None, :] == jnp.arange(nblocks, dtype=jnp.int32)[:, None]) & valid[None, :]
    return jnp.dot(select.astype(BF16), received, preferred_element_type=F32).astype(BF16)


def any_peers(inputs, out_grad, gains, down_proj, up_proj, wiring, pair_mask):
    sections = lax.axis_size("section")
    nblocks = lax.axis_size("peer")
    section = lax.axis_index("section")
    peer = lax.axis_index("peer")
    x = inputs[0, 0]
    rows, width = x.shape
    out, dx, gdown, gup = layer(x, out_grad[0, 0], gains[0], down_proj[0], up_proj[0])
    blk_rows = rows // nblocks
    here = lax.dynamic_index_in_dim(wiring, section, 0, keepdims=False)
    before = lax.dynamic_index_in_dim(wiring, (section + sections - 1) % sections, 0, keepdims=False)
    here_start = jnp.cumsum(here, axis=1) - here
    before_col = jnp.cumsum(before, axis=0) - before
    out_blocks = out.reshape(nblocks, blk_rows * width)
    dx_blocks = dx.reshape(nblocks, blk_rows * width)
    fwd_buf = pack_blocks(out_blocks, here[peer], here_start[peer], CAP)
    back_buf = pack_blocks(dx_blocks, before[:, peer], before_col[:, peer], CAP)
    moved = passed_along(fwd_buf, "section", 1)
    got_fwd = lax.all_to_all(moved, "peer", split_axis=0, concat_axis=0, tiled=True)
    next_rows = unpack_blocks(got_fwd, before[:, peer], before_col[:, peer], CAP, nblocks)
    moved_back = passed_along(back_buf, "section", -1)
    got_back = lax.all_to_all(moved_back, "peer", split_axis=0, concat_axis=0, tiled=True)
    return_rows = unpack_blocks(got_back, here[peer], here_start[peer], CAP, nblocks)
    mask_value = pair_mask[section]
    other_down, other_up = (gdown, gup)
    for bit in range(nblocks.bit_length() - 1):
        swapped_down, swapped_up = swapped((other_down, other_up), "peer", 1 << bit)
        take = jnp.bitwise_and(jnp.right_shift(mask_value, bit), 1) == 1
        other_down = jnp.where(take, swapped_down, other_down)
        other_up = jnp.where(take, swapped_up, other_up)
    grad_down = (gdown.astype(F32) + other_down.astype(F32)) * 0.5
    grad_up = (gup.astype(F32) + other_up.astype(F32)) * 0.5
    return (
        next_rows.reshape(1, 1, rows, width),
        return_rows.reshape(1, 1, rows, width),
        grad_down[None, None],
        grad_up[None, None],
    )


def solution(mesh):
    whole = P("section", "peer", None, None)
    return jax.shard_map(
        four_peers if mesh.shape["peer"] == 4 else any_peers,
        mesh=mesh,
        in_specs=(whole, whole, P("section", None), P("section", None, None), P("section", None, None), P(), P()),
        out_specs=(whole,) * 4,
        check_vma=False,
    )
```

profile of v0, /device:TPU:1, one launch (start us, length us, event | category | flops | bytes accessed | tf_op | source)
XLA Modules:
  0.0 161.8 jit_solution(11959384839442456259)
XLA Ops:
  0.6 0.8 copy.15.wiring_ref
  1.4 0.0 copy-start
  1.4 0.7 copy-done
  2.1 0.0 copy-start.1
  2.1 0.0 copy-start.35
  2.1 5.4 %open.1 = (s32[16]{0:T(128)S(1)}, s32[1]{0:T(128)}, bf16[256,128]{1,0:T(8,128)(2,1)S(1)}, f32[8,128]{1,0:T(8,128)S(1)}, bf16[304,1024]{1,0:T(8,128)(2,1)S(1)}, /...) custom-call(s32[8,4,4]{2,1,0:T(4,128)S(1)} %copy.15.wiring_ref, ...), custom_call_target="tpu_custom_call" | custom-call | tf_op jit(solution)/shard_map/open/pallas_call | solution.py:171
  8.2 0.0 copy-done.1
  8.2 0.0 copy-done.2
  8.2 0.0 copy-done.9
  8.2 0.0 copy-done.16
  8.2 0.0 copy-done.35
  8.2 65.0 %conditional.3 = (bf16[128,2048]{1,0:T(8,128)(2,1)}, bf16[128,2048]{1,0:T(8,128)(2,1)}, bf16[256,128]{1,0:T(8,128)(2,1)}, f32[8,128]{1,0:T(8,128)}, bf16[304,102...) conditional(s32[]{:T(128)} %bitcast.4, (s32[16]{0:T(128)S(1)}, ...), branch_computations={%region_0.0_spmd, %region_1.0_spmd, %region_2.0_spmd, %region_3.0_... | conditional | bytes 13369628 | solution.py:475
  8.3 4.2 %collective-permute-start.10 = (bf16[304,1024]{1,0:T(8,128)(2,1)S(1)}, bf16[304,1024]{1,0:T(8,128)(2,1)S(1)}, u32[]{:S(2)}, u32[]{:S(2)}) collective-permute-start(bf16[304,1024]{1,0:T(8,128)(2,1)S(1)} %get-tuple-element.500), channel_id=1, source_target_pairs={{0,3},{1,2},{2,1},{3,0},{4,7},{5,6},{6,5},{7,4},{8,11},{9,10},{10,... | collective-permute-start | bytes 1867784 | tf_op jit(solution)/shard_map/cond/branch_2_fun/ppermute | solution.py:26
  12.5 13.1 %collective-permute-done.10.got_ref = bf16[304,1024]{1,0:T(8,128)(2,1)S(1)} collective-permute-done((bf16[304,1024]{1,0:T(8,128)(2,1)S(1)}, bf16[304,1024]{1,0:T(8,128)(2,1)S(1)}, u32[]{:S(2)}, u32[]{:S(2)}) %collective-permute-start.10) | collective-permute-done | bytes 622624 | tf_op jit(solution)/shard_map/cond/branch_2_fun/ppermute | solution.py:26
  25.6 3.6 %collective-permute-start.11 = (bf16[256,1024]{1,0:T(8,128)(2,1)S(1)}, bf16[256,1024]{1,0:T(8,128)(2,1)}, u32[]{:S(2)}, u32[]{:S(2)}) collective-permute-start(bf16[256,1024]{1,0:T(8,128)(2,1)S(1)} %get-tuple-element.511), channel_id=1, source_target_pairs={{0,3},{1,2},{2,1},{3,0},{4,7},{5,6},{6,5},{7,4},{8,11},{9,10},{10,... | collective-permute-start | bytes 1572872 | tf_op jit(solution)/shard_map/cond/branch_2_fun/ppermute | solution.py:26
  29.2 0.6 unpack.8
  29.8 1.8 %rows.34 = (bf16[192,1024]{1,0:T(8,128)(2,1)S(1)}, bf16[128,1024]{1,0:T(8,128)(2,1)S(1)}, bf16[128,1024]{1,0:T(8,128)(2,1)S(1)}) custom-call(s32[16]{0:T(128)S(1)} %get-tuple-element.513.plan_ref, bf16[128,5120]{1,0:T(8,128)(2,1)S(1)} %get-tuple-element.498.x_ref, bf16[128,5120]{1,0:T(8,128)(2,1)S(1)} %get-tuple-element.499.dy_ref, ...), custom_call_target="tpu_custom_call" | custom-call | tf_op jit(solution)/shard_map/cond/branch_2_fun/rows/pallas_call | solution.py:261
  31.7 0.0 copy-done.25
  31.7 0.1 collective-permute-start.12
  31.7 17.1 %collective-permute-done.12.refs_2_ = bf16[192,1024]{1,0:T(8,128)(2,1)S(1)} collective-permute-done((bf16[192,1024]{1,0:T(8,128)(2,1)S(1)}, bf16[192,1024]{1,0:T(8,128)(2,1)S(1)}, u32[]{:S(2)}, u32[]{:S(2)}) %collective-permute-start.12) | collective-permute-done | bytes 393248 | tf_op jit(solution)/shard_map/cond/branch_2_fun/ppermute | solution.py:26
  48.8 0.0 collective-permute-done.11.got_ref
  48.8 3.7 %collective-permute-start.14 = (bf16[256,1024]{1,0:T(8,128)(2,1)S(1)}, bf16[256,1024]{1,0:T(8,128)(2,1)}, u32[]{:S(2)}, u32[]{:S(2)}) collective-permute-start(bf16[256,1024]{1,0:T(8,128)(2,1)S(1)} %get-tuple-element.521), channel_id=1, source_target_pairs={{0,3},{1,2},{2,1},{3,0},{4,7},{5,6},{6,5},{7,4},{8,11},{9,10},{10,... | collective-permute-start | bytes 1572872 | tf_op jit(solution)/shard_map/cond/branch_2_fun/ppermute | solution.py:26
  52.5 1.9 %rows.35 = (bf16[192,1024]{1,0:T(8,128)(2,1)S(1)}, bf16[128,1024]{1,0:T(8,128)(2,1)S(1)}, bf16[128,1024]{1,0:T(8,128)(2,1)S(1)}) custom-call(s32[16]{0:T(128)S(1)} %get-tuple-element.513.plan_ref, bf16[128,5120]{1,0:T(8,128)(2,1)S(1)} %get-tuple-element.498.x_ref, bf16[128,5120]{1,0:T(8,128)(2,1)S(1)} %get-tuple-element.499.dy_ref, ...), custom_call_target="tpu_custom_call" | custom-call | tf_op jit(solution)/shard_map/cond/branch_2_fun/rows/pallas_call | solution.py:261
  54.5 0.1 collective-permute-start.13
  54.5 17.1 %collective-permute-done.13.refs_5_ = bf16[192,1024]{1,0:T(8,128)(2,1)S(1)} collective-permute-done((bf16[192,1024]{1,0:T(8,128)(2,1)S(1)}, bf16[192,1024]{1,0:T(8,128)(2,1)S(1)}, u32[]{:S(2)}, u32[]{:S(2)}) %collective-permute-start.13) | collective-permute-done | bytes 393248 | tf_op jit(solution)/shard_map/cond/branch_2_fun/ppermute | solution.py:26
  71.6 1.6 %merge.20 = (bf16[128,2048]{1,0:T(8,128)(2,1)}, bf16[128,2048]{1,0:T(8,128)(2,1)}) custom-call(s32[16]{0:T(128)S(1)} %get-tuple-element.513.plan_ref, bf16[128,1024]{1,0:T(8,128)(2,1)S(1)} %get-tuple-element.514.refs_0_, bf16[128,1024]{1,0:T(8,128)(2,1)S(1)} %get-tuple-element.515.refs_1_, bf16[192,1024]{1,0:T(8,128)(2,1)S(1)} %collective-permute-done.12.refs_2_, ...), custom_call_target="tpu_custom_call" | custom-call | tf_op jit(solution)/shard_map/cond/branch_2_fun/merge/pallas_call | solution.py:317
  73.3 0.0 collective-permute-done.14
  73.3 14.3 %collective-permute-start.60 = (bf16[128,2048]{1,0:T(8,128)(2,1)}, bf16[128,2048]{1,0:T(8,128)(2,1)S(1)}, u32[]{:S(2)}, u32[]{:S(2)}) collective-permute-start(bf16[128,2048]{1,0:T(8,128)(2,1)} %get-tuple-element.928), channel_id=1, source_target_pairs={{28,0},{0,4},{4,8},{8,12},{12,16},{16,20},{20,24},{24,28},{29,1},{... | collective-permute-start | bytes 1572872 | tf_op jit(solution)/shard_map/ppermute | solution.py:21
  87.6 0.0 collective-permute-start.61
  87.6 38.1 %conditional.4 = (bf16[128,2048]{1,0:T(8,128)(2,1)}, bf16[128,2048]{1,0:T(8,128)(2,1)}, bf16[256,1024]{1,0:T(8,128)(2,1)}, f32[128,5120]{1,0:T(8,128)}, f32[5120,128]{1,0:T(8,128)}) conditional(s32[]{:T(128)} %bitcast.4, (s32[16]{0:T(128)S(1)}, bf16[128,5120]{1,0:T(8,128)(2,1)S(1)}, bf16[128,5120]{1,0:T(8,128)(2,1)}, ...), branch_computations={%region_6.0_spmd, %region_7.0_spmd, %region_8.0_spmd, %region_9.0_... | conditional | bytes 26607928 | solution.py:475
  87.6 3.6 %collective-permute-start.38 = (bf16[256,1024]{1,0:T(8,128)(2,1)S(1)}, bf16[256,1024]{1,0:T(8,128)(2,1)S(1)}, u32[]{:S(2)}, u32[]{:S(2)}) collective-permute-start(bf16[256,1024]{1,0:T(8,128)(2,1)S(1)} %get-tuple-element.677), channel_id=1, source_target_pairs={{0,3},{1,2},{2,1},{3,0},{4,7},{5,6},{6,5},{7,4},{8,11},{9,10},{10,... | collective-permute-start | bytes 1572872 | tf_op jit(solution)/shard_map/cond/branch_2_fun/ppermute | solution.py:26
  91.2 2.2 %rows.46 = (bf16[192,1024]{1,0:T(8,128)(2,1)S(1)}, bf16[128,1024]{1,0:T(8,128)(2,1)S(1)}, bf16[128,1024]{1,0:T(8,128)(2,1)S(1)}) custom-call(s32[16]{0:T(128)S(1)} %get-tuple-element.679.plan_ref, bf16[128,5120]{1,0:T(8,128)(2,1)S(1)} %get-tuple-element.688.x_ref.refs_0_, bf16[128,5120]{1,0:T(8,128)(2,1)} %get-tuple-element.665.dy_ref.refs_1_, ...), custom_call_target="tpu_custom_call" | custom-call | tf_op jit(solution)/shard_map/cond/branch_2_fun/rows/pallas_call | solution.py:261
  93.4 0.1 collective-permute-start.39
  93.5 10.5 %collective-permute-done.39.refs_2_ = bf16[192,1024]{1,0:T(8,128)(2,1)S(1)} collective-permute-done((bf16[192,1024]{1,0:T(8,128)(2,1)S(1)}, bf16[192,1024]{1,0:T(8,128)(2,1)S(1)}, u32[]{:S(2)}, u32[]{:S(2)}) %collective-permute-start.39) | collective-permute-done | bytes 393248 | tf_op jit(solution)/shard_map/cond/branch_2_fun/ppermute | solution.py:26
  104.0 0.0 collective-permute-done.38.got_ref.refs_5_
  104.0 3.0 %collective-permute-start.41 = (bf16[256,1024]{1,0:T(8,128)(2,1)S(1)}, bf16[256,1024]{1,0:T(8,128)(2,1)}, u32[]{:S(2)}, u32[]{:S(2)}) collective-permute-start(bf16[256,1024]{1,0:T(8,128)(2,1)S(1)} %get-tuple-element.687), channel_id=1, source_target_pairs={{0,3},{1,2},{2,1},{3,0},{4,7},{5,6},{6,5},{7,4},{8,11},{9,10},{10,... | collective-permute-start | bytes 1572872 | tf_op jit(solution)/shard_map/cond/branch_2_fun/ppermute | solution.py:26
  107.0 0.0 copy-done.5
  107.0 0.0 copy-done.12
  107.0 0.0 copy-done.19
  107.0 1.9 %rows.47 = (bf16[192,1024]{1,0:T(8,128)(2,1)S(1)}, bf16[128,1024]{1,0:T(8,128)(2,1)S(1)}, bf16[128,1024]{1,0:T(8,128)(2,1)S(1)}) custom-call(s32[16]{0:T(128)S(1)} %get-tuple-element.679.plan_ref, bf16[128,5120]{1,0:T(8,128)(2,1)S(1)} %get-tuple-element.688.x_ref.refs_0_, bf16[128,5120]{1,0:T(8,128)(2,1)S(1)} %copy-done.5, ...), custom_call_target="tpu_custom_call" | custom-call | tf_op jit(solution)/shard_map/cond/branch_2_fun/rows/pallas_call | solution.py:261
  108.9 0.1 collective-permute-start.40
  108.9 0.0 copy-done.31
  108.9 7.2 %grads.9 = (f32[128,5120]{1,0:T(8,128)}, f32[5120,128]{1,0:T(8,128)}) custom-call(bf16[128,5120]{1,0:T(8,128)(2,1)S(1)} %get-tuple-element.688.x_ref.refs_0_, bf16[128,5120]{1,0:T(8,128)(2,1)S(1)} %copy-done.5, bf16[304,1024]{1,0:T(8,128)(2,1)S(1)} %copy-done.31, bf16[256,1024]{1,0:T(8,128)(2,1)} %get-tuple-element.690.refs_3_, ...), custom_call_target="tpu_custom_call" | custom-call | tf_op jit(solution)/shard_map/cond/branch_2_fun/grads/pallas_call | solution.py:405
  116.1 7.6 %collective-permute-done.40.refs_5_ = bf16[192,1024]{1,0:T(8,128)(2,1)S(1)} collective-permute-done((bf16[192,1024]{1,0:T(8,128)(2,1)S(1)}, bf16[192,1024]{1,0:T(8,128)(2,1)S(1)}, u32[]{:S(2)}, u32[]{:S(2)}) %collective-permute-start.40) | collective-permute-done | bytes 393248 | tf_op jit(solution)/shard_map/cond/branch_2_fun/ppermute | solution.py:26
  123.7 1.7 %merge.26 = (bf16[128,2048]{1,0:T(8,128)(2,1)}, bf16[128,2048]{1,0:T(8,128)(2,1)}) custom-call(s32[16]{0:T(128)S(1)} %get-tuple-element.679.plan_ref, bf16[128,1024]{1,0:T(8,128)(2,1)S(1)} %get-tuple-element.680.refs_0_, bf16[128,1024]{1,0:T(8,128)(2,1)S(1)} %get-tuple-element.681.refs_1_, bf16[192,1024]{1,0:T(8,128)(2,1)S(1)} %collective-permute-done.39.refs_2_, ...), custom_call_target="tpu_custom_call" | custom-call | tf_op jit(solution)/shard_map/cond/branch_2_fun/merge/pallas_call | solution.py:317
  125.4 0.0 collective-permute-done.41
  125.6 0.0 collective-permute-done.60.refs_0_
  125.7 0.0 collective-permute-done.61.refs_2_
  125.7 3.5 %collective-permute-start.63 = (bf16[128,2048]{1,0:T(8,128)(2,1)}, bf16[128,2048]{1,0:T(8,128)(2,1)S(1)}, u32[]{:S(2)}, u32[]{:S(2)}) collective-permute-start(bf16[128,2048]{1,0:T(8,128)(2,1)} %get-tuple-element.942), channel_id=1, source_target_pairs={{4,0},{8,4},{12,8},{16,12},{20,16},{24,20},{28,24},{0,28},{5,1},{9... | collective-permute-start | bytes 1572872 | tf_op jit(solution)/shard_map/ppermute | solution.py:21
  129.2 9.7 %collective-permute-start.62 = (bf16[128,2048]{1,0:T(8,128)(2,1)}, bf16[128,2048]{1,0:T(8,128)(2,1)S(1)}, u32[]{:S(2)}, u32[]{:S(2)}) collective-permute-start(bf16[128,2048]{1,0:T(8,128)(2,1)} %get-tuple-element.940), channel_id=1, source_target_pairs={{28,0},{0,4},{4,8},{8,12},{12,16},{16,20},{20,24},{24,28},{29,1},{... | collective-permute-start | bytes 1572872 | tf_op jit(solution)/shard_map/ppermute | solution.py:21
  138.9 10.2 %conditional.5 = ((bf16[128,1024]{1,0:T(8,128)(2,1)}, bf16[128,1024]{1,0:T(8,128)(2,1)})) conditional(s32[]{:T(128)} %bitcast.4, (s32[16]{0:T(128)S(1)}, bf16[128,5120]{1,0:T(8,128)(2,1)S(1)}, bf16[128,5120]{1,0:T(8,128)(2,1)}, bf16[256,1024]{1,0:T(8,128)(2,1)}, bf16[256,128]{1,0:T(8,128)(2,1)S(1)}, ...), branch_computations={%region_12.0_spmd, %region_13.0_spmd, %region_14.0_spmd, %region_1... | conditional | bytes 2097200 | solution.py:475
  138.9 2.1 %rows.56 = (bf16[192,1024]{1,0:T(8,128)(2,1)S(1)}, bf16[128,1024]{1,0:T(8,128)(2,1)S(1)}, bf16[128,1024]{1,0:T(8,128)(2,1)S(1)}) custom-call(s32[16]{0:T(128)S(1)} %get-tuple-element.831.plan_ref, bf16[128,5120]{1,0:T(8,128)(2,1)S(1)} %get-tuple-element.820.x_ref, bf16[128,5120]{1,0:T(8,128)(2,1)} %get-tuple-element.821.dy_ref, ...), custom_call_target="tpu_custom_call" | custom-call | tf_op jit(solution)/shard_map/cond/branch_2_fun/rows/pallas_call | solution.py:261
  140.9 0.1 collective-permute-start.56
  141.0 6.6 %collective-permute-done.56.refs_2_ = bf16[192,1024]{1,0:T(8,128)(2,1)S(1)} collective-permute-done((bf16[192,1024]{1,0:T(8,128)(2,1)S(1)}, bf16[192,1024]{1,0:T(8,128)(2,1)S(1)}, u32[]{:S(2)}, u32[]{:S(2)}) %collective-permute-start.56) | collective-permute-done | bytes 393248 | tf_op jit(solution)/shard_map/cond/branch_2_fun/ppermute | solution.py:26
  147.6 1.4 merge.32
  149.0 2.6 %collective-permute-done.63.refs_3_ = bf16[128,2048]{1,0:T(8,128)(2,1)S(1)} collective-permute-done((bf16[128,2048]{1,0:T(8,128)(2,1)}, bf16[128,2048]{1,0:T(8,128)(2,1)S(1)}, u32[]{:S(2)}, u32[]{:S(2)}) %collective-permute-start.63) | collective-permute-done | bytes 524320 | tf_op jit(solution)/shard_map/ppermute | solution.py:21
  151.6 0.0 collective-permute-done.62.refs_1_
  151.6 3.0 %collective-permute-start.64 = (bf16[128,1024]{1,0:T(8,128)(2,1)}, bf16[128,1024]{1,0:T(8,128)(2,1)S(1)}, u32[]{:S(2)}, u32[]{:S(2)}) collective-permute-start(bf16[128,1024]{1,0:T(8,128)(2,1)} %get-tuple-element.943), channel_id=1, source_target_pairs={{28,0},{0,4},{4,8},{8,12},{12,16},{16,20},{20,24},{24,28},{29,1},{... | collective-permute-start | bytes 786440 | tf_op jit(solution)/shard_map/ppermute | solution.py:21
  154.6 0.0 collective-permute-start.65
  154.6 2.8 %grads.13 = (f32[128,5120]{1,0:T(8,128)}, f32[5120,128]{1,0:T(8,128)}) custom-call(f32[128,5120]{1,0:T(8,128)} %get-tuple-element.951.refs_0_, f32[5120,128]{1,0:T(8,128)} %get-tuple-element.952.refs_1_, bf16[128,5120]{1,0:T(8,128)(2,1)S(1)} %bitcast.28, bf16[128,5120]{1,0:T(8,128)(2,1)} %bitcast.42, ...), custom_call_target="tpu_custom_call", output_to_operand_aliasing={{0}: (0, {}), {1}: (1, {})} | custom-call | tf_op jit(solution)/shard_map/grads/pallas_call | solution.py:405
  157.4 1.3 join.2
  158.8 0.0 collective-permute-done.64.refs_2_
  158.8 2.1 %collective-permute-done.65.refs_3_ = bf16[128,1024]{1,0:T(8,128)(2,1)S(1)} collective-permute-done((bf16[128,1024]{1,0:T(8,128)(2,1)}, bf16[128,1024]{1,0:T(8,128)(2,1)S(1)}, u32[]{:S(2)}, u32[]{:S(2)}) %collective-permute-start.65) | collective-permute-done | bytes 262176 | tf_op jit(solution)/shard_map/ppermute | solution.py:21
  160.8 0.8 join.3
  (8 shorter events, 0.0 us)
Async XLA Ops:
  1.4 0.7 copy-start
  2.1 6.1 %copy-start.1 = (bf16[1,1,128,5120]{3,2,1,0:T(8,128)(2,1)S(1)}, bf16[1,1,128,5120]{3,2,1,0:T(8,128)(2,1)}, u32[]{:S(2)}) copy-start(bf16[1,1,128,5120]{3,2,1,0:T(8,128)(2,1)} %param.25) | copy-start | bytes 3932164
  2.1 6.1 %copy-start.2 = (bf16[1,1,128,5120]{3,2,1,0:T(8,128)(2,1)S(1)}, bf16[1,1,128,5120]{3,2,1,0:T(8,128)(2,1)}, u32[]{:S(2)}) copy-start(bf16[1,1,128,5120]{3,2,1,0:T(8,128)(2,1)} %param.26) | copy-start | bytes 3932164
  2.1 6.1 %copy-start.9 = (bf16[1,5120,128]{2,1,0:T(8,128)(2,1)S(1)}, bf16[1,5120,128]{2,1,0:T(8,128)(2,1)}, u32[]{:S(2)}) copy-start(bf16[1,5120,128]{2,1,0:T(8,128)(2,1)} %param.28) | copy-start | bytes 3932164
  2.1 6.1 %copy-start.16 = (bf16[1,128,5120]{2,1,0:T(8,128)(2,1)S(1)}, bf16[1,128,5120]{2,1,0:T(8,128)(2,1)}, u32[]{:S(2)}) copy-start(bf16[1,128,5120]{2,1,0:T(8,128)(2,1)} %param.29) | copy-start | bytes 3932164
  2.1 6.1 %copy-start.35 = (f32[1,5120]{1,0:T(1,128)S(1)}, f32[1,5120]{1,0:T(1,128)}, u32[]{:S(2)}) copy-start(f32[1,5120]{1,0:T(1,128)} %refs_9_.1) | copy-start | bytes 61444
  8.3 17.3 %collective-permute-start.10 = (bf16[304,1024]{1,0:T(8,128)(2,1)S(1)}, bf16[304,1024]{1,0:T(8,128)(2,1)S(1)}, u32[]{:S(2)}, u32[]{:S(2)}) collective-permute-start(bf16[304,1024]{1,0:T(8,128)(2,1)S(1)} %get-tuple-element.500), channel_id=1, source_target_pairs={{0,3},{1,2},{2,1},{3,0},{4,7},{5,6},{6,5},{7,4},{8,11},{9,10},{10,... | collective-permute-start | bytes 1867784 | tf_op jit(solution)/shard_map/cond/branch_2_fun/ppermute | solution.py:26
  25.6 6.1 %copy-start.25 = (bf16[304,1024]{1,0:T(8,128)(2,1)}, bf16[304,1024]{1,0:T(8,128)(2,1)S(1)}, u32[]{:S(2)}) copy-start(bf16[304,1024]{1,0:T(8,128)(2,1)S(1)} %collective-permute-done.10.got_ref) | copy-start | bytes 1867780 | tf_op jit(solution)/shard_map/cond
  25.6 23.3 %collective-permute-start.11 = (bf16[256,1024]{1,0:T(8,128)(2,1)S(1)}, bf16[256,1024]{1,0:T(8,128)(2,1)}, u32[]{:S(2)}, u32[]{:S(2)}) collective-permute-start(bf16[256,1024]{1,0:T(8,128)(2,1)S(1)} %get-tuple-element.511), channel_id=1, source_target_pairs={{0,3},{1,2},{2,1},{3,0},{4,7},{5,6},{6,5},{7,4},{8,11},{9,10},{10,... | collective-permute-start | bytes 1572872 | tf_op jit(solution)/shard_map/cond/branch_2_fun/ppermute | solution.py:26
  31.7 17.2 %collective-permute-start.12 = (bf16[192,1024]{1,0:T(8,128)(2,1)S(1)}, bf16[192,1024]{1,0:T(8,128)(2,1)S(1)}, u32[]{:S(2)}, u32[]{:S(2)}) collective-permute-start(bf16[192,1024]{1,0:T(8,128)(2,1)S(1)} %get-tuple-element.508), channel_id=1, source_target_pairs={{0,1},{1,0},{2,3},{3,2},{4,5},{5,4},{6,7},{7,6},{8,9},{9,8},{10,11... | collective-permute-start | bytes 1179656 | tf_op jit(solution)/shard_map/cond/branch_2_fun/ppermute | solution.py:26
  48.8 24.5 %collective-permute-start.14 = (bf16[256,1024]{1,0:T(8,128)(2,1)S(1)}, bf16[256,1024]{1,0:T(8,128)(2,1)}, u32[]{:S(2)}, u32[]{:S(2)}) collective-permute-start(bf16[256,1024]{1,0:T(8,128)(2,1)S(1)} %get-tuple-element.521), channel_id=1, source_target_pairs={{0,3},{1,2},{2,1},{3,0},{4,7},{5,6},{6,5},{7,4},{8,11},{9,10},{10,... | collective-permute-start | bytes 1572872 | tf_op jit(solution)/shard_map/cond/branch_2_fun/ppermute | solution.py:26
  54.5 17.2 %collective-permute-start.13 = (bf16[192,1024]{1,0:T(8,128)(2,1)S(1)}, bf16[192,1024]{1,0:T(8,128)(2,1)S(1)}, u32[]{:S(2)}, u32[]{:S(2)}) collective-permute-start(bf16[192,1024]{1,0:T(8,128)(2,1)S(1)} %get-tuple-element.512), channel_id=1, source_target_pairs={{0,1},{1,0},{2,3},{3,2},{4,5},{5,4},{6,7},{7,6},{8,9},{9,8},{10,11... | collective-permute-start | bytes 1179656 | tf_op jit(solution)/shard_map/cond/branch_2_fun/ppermute | solution.py:26
  73.3 52.4 %collective-permute-start.60 = (bf16[128,2048]{1,0:T(8,128)(2,1)}, bf16[128,2048]{1,0:T(8,128)(2,1)S(1)}, u32[]{:S(2)}, u32[]{:S(2)}) collective-permute-start(bf16[128,2048]{1,0:T(8,128)(2,1)} %get-tuple-element.928), channel_id=1, source_target_pairs={{28,0},{0,4},{4,8},{8,12},{12,16},{16,20},{20,24},{24,28},{29,1},{... | collective-permute-start | bytes 1572872 | tf_op jit(solution)/shard_map/ppermute | solution.py:21
  87.6 38.1 %collective-permute-start.61 = (bf16[128,2048]{1,0:T(8,128)(2,1)}, bf16[128,2048]{1,0:T(8,128)(2,1)S(1)}, u32[]{:S(2)}, u32[]{:S(2)}) collective-permute-start(bf16[128,2048]{1,0:T(8,128)(2,1)} %get-tuple-element.939), channel_id=1, source_target_pairs={{4,0},{8,4},{12,8},{16,12},{20,16},{24,20},{28,24},{0,28},{5,1},{9... | collective-permute-start | bytes 1572872 | tf_op jit(solution)/shard_map/ppermute | solution.py:21
  87.6 16.4 %collective-permute-start.38 = (bf16[256,1024]{1,0:T(8,128)(2,1)S(1)}, bf16[256,1024]{1,0:T(8,128)(2,1)S(1)}, u32[]{:S(2)}, u32[]{:S(2)}) collective-permute-start(bf16[256,1024]{1,0:T(8,128)(2,1)S(1)} %get-tuple-element.677), channel_id=1, source_target_pairs={{0,3},{1,2},{2,1},{3,0},{4,7},{5,6},{6,5},{7,4},{8,11},{9,10},{10,... | collective-permute-start | bytes 1572872 | tf_op jit(solution)/shard_map/cond/branch_2_fun/ppermute | solution.py:26
  91.2 15.8 %copy-start.5 = (bf16[128,5120]{1,0:T(8,128)(2,1)S(1)}, bf16[128,5120]{1,0:T(8,128)(2,1)}, u32[]{:S(2)}) copy-start(bf16[128,5120]{1,0:T(8,128)(2,1)} %get-tuple-element.665.dy_ref.refs_1_) | copy-start | bytes 3932164 | tf_op jit(solution)/shard_map/cond
  91.2 15.8 %copy-start.12 = (bf16[5120,128]{1,0:T(8,128)(2,1)S(1)}, bf16[5120,128]{1,0:T(8,128)(2,1)}, u32[]{:S(2)}) copy-start(bf16[5120,128]{1,0:T(8,128)(2,1)} %get-tuple-element.672.down_ref) | copy-start | bytes 3932164 | tf_op jit(solution)/shard_map/cond
  91.2 15.8 %copy-start.19 = (bf16[128,5120]{1,0:T(8,128)(2,1)S(1)}, bf16[128,5120]{1,0:T(8,128)(2,1)}, u32[]{:S(2)}) copy-start(bf16[128,5120]{1,0:T(8,128)(2,1)} %get-tuple-element.671.up_ref) | copy-start | bytes 3932164 | tf_op jit(solution)/shard_map/cond
  93.4 10.6 %collective-permute-start.39 = (bf16[192,1024]{1,0:T(8,128)(2,1)S(1)}, bf16[192,1024]{1,0:T(8,128)(2,1)S(1)}, u32[]{:S(2)}, u32[]{:S(2)}) collective-permute-start(bf16[192,1024]{1,0:T(8,128)(2,1)S(1)} %get-tuple-element.674), channel_id=1, source_target_pairs={{0,1},{1,0},{2,3},{3,2},{4,5},{5,4},{6,7},{7,6},{8,9},{9,8},{10,11... | collective-permute-start | bytes 1179656 | tf_op jit(solution)/shard_map/cond/branch_2_fun/ppermute | solution.py:26
  104.0 4.9 %copy-start.31 = (bf16[304,1024]{1,0:T(8,128)(2,1)S(1)}, bf16[304,1024]{1,0:T(8,128)(2,1)}, u32[]{:S(2)}) copy-start(bf16[304,1024]{1,0:T(8,128)(2,1)} %get-tuple-element.689.refs_2_) | copy-start | bytes 1867780 | tf_op jit(solution)/shard_map/cond
  104.0 21.4 %collective-permute-start.41 = (bf16[256,1024]{1,0:T(8,128)(2,1)S(1)}, bf16[256,1024]{1,0:T(8,128)(2,1)}, u32[]{:S(2)}, u32[]{:S(2)}) collective-permute-start(bf16[256,1024]{1,0:T(8,128)(2,1)S(1)} %get-tuple-element.687), channel_id=1, source_target_pairs={{0,3},{1,2},{2,1},{3,0},{4,7},{5,6},{6,5},{7,4},{8,11},{9,10},{10,... | collective-permute-start | bytes 1572872 | tf_op jit(solution)/shard_map/cond/branch_2_fun/ppermute | solution.py:26
  108.9 14.9 %collective-permute-start.40 = (bf16[192,1024]{1,0:T(8,128)(2,1)S(1)}, bf16[192,1024]{1,0:T(8,128)(2,1)S(1)}, u32[]{:S(2)}, u32[]{:S(2)}) collective-permute-start(bf16[192,1024]{1,0:T(8,128)(2,1)S(1)} %get-tuple-element.678), channel_id=1, source_target_pairs={{0,1},{1,0},{2,3},{3,2},{4,5},{5,4},{6,7},{7,6},{8,9},{9,8},{10,11... | collective-permute-start | bytes 1179656 | tf_op jit(solution)/shard_map/cond/branch_2_fun/ppermute | solution.py:26
  125.7 25.9 %collective-permute-start.63 = (bf16[128,2048]{1,0:T(8,128)(2,1)}, bf16[128,2048]{1,0:T(8,128)(2,1)S(1)}, u32[]{:S(2)}, u32[]{:S(2)}) collective-permute-start(bf16[128,2048]{1,0:T(8,128)(2,1)} %get-tuple-element.942), channel_id=1, source_target_pairs={{4,0},{8,4},{12,8},{16,12},{20,16},{24,20},{28,24},{0,28},{5,1},{9... | collective-permute-start | bytes 1572872 | tf_op jit(solution)/shard_map/ppermute | solution.py:21
  129.2 22.4 %collective-permute-start.62 = (bf16[128,2048]{1,0:T(8,128)(2,1)}, bf16[128,2048]{1,0:T(8,128)(2,1)S(1)}, u32[]{:S(2)}, u32[]{:S(2)}) collective-permute-start(bf16[128,2048]{1,0:T(8,128)(2,1)} %get-tuple-element.940), channel_id=1, source_target_pairs={{28,0},{0,4},{4,8},{8,12},{12,16},{16,20},{20,24},{24,28},{29,1},{... | collective-permute-start | bytes 1572872 | tf_op jit(solution)/shard_map/ppermute | solution.py:21
  140.9 6.7 %collective-permute-start.56 = (bf16[192,1024]{1,0:T(8,128)(2,1)S(1)}, bf16[192,1024]{1,0:T(8,128)(2,1)S(1)}, u32[]{:S(2)}, u32[]{:S(2)}) collective-permute-start(bf16[192,1024]{1,0:T(8,128)(2,1)S(1)} %get-tuple-element.830), channel_id=1, source_target_pairs={{0,1},{1,0},{2,3},{3,2},{4,5},{5,4},{6,7},{7,6},{8,9},{9,8},{10,11... | collective-permute-start | bytes 1179656 | tf_op jit(solution)/shard_map/cond/branch_2_fun/ppermute | solution.py:26
  151.6 7.2 %collective-permute-start.64 = (bf16[128,1024]{1,0:T(8,128)(2,1)}, bf16[128,1024]{1,0:T(8,128)(2,1)S(1)}, u32[]{:S(2)}, u32[]{:S(2)}) collective-permute-start(bf16[128,1024]{1,0:T(8,128)(2,1)} %get-tuple-element.943), channel_id=1, source_target_pairs={{28,0},{0,4},{4,8},{8,12},{12,16},{16,20},{20,24},{24,28},{29,1},{... | collective-permute-start | bytes 786440 | tf_op jit(solution)/shard_map/ppermute | solution.py:21
  154.6 6.2 %collective-permute-start.65 = (bf16[128,1024]{1,0:T(8,128)(2,1)}, bf16[128,1024]{1,0:T(8,128)(2,1)S(1)}, u32[]{:S(2)}, u32[]{:S(2)}) collective-permute-start(bf16[128,1024]{1,0:T(8,128)(2,1)} %get-tuple-element.945), channel_id=1, source_target_pairs={{4,0},{8,4},{12,8},{16,12},{20,16},{24,20},{28,24},{0,28},{5,1},{9... | collective-permute-start | bytes 786440 | tf_op jit(solution)/shard_map/ppermute | solution.py:21
where the time goes:
time: 164 us; the launch traced here: 162 us
  waiting for transfers between devices  76.6 us (47%)
  starting transfers between devices  49 us (30%)
  Pallas kernels  32.7 us (20%)
    ppermute x10, waiting for transfers between devices, swapped(): lax.ppermute(block, axis, [(i, i ^ mask) for i in range(count) if i ^ mas...  72 us
    ppermute x6, starting transfers between devices, passed_along(): return lax.ppermute(block, axis, route)  30.5 us
    ppermute x10, starting transfers between devices, swapped(): lax.ppermute(block, axis, [(i, i ^ mask) for i in range(count) if i ^ mas...  18.5 us
    pallas_call x2, Pallas kernels, make_grads(): pl.pallas_call(kernel, grid=(starts[-1],), out_shape=(jax.ShapeDtypeStruc...  9.94 us
    pallas_call x5, Pallas kernels, make_rows(): pl.pallas_call(functools.partial(rows_kernel, cap, blk), grid=(tiles,), o...  9.86 us
    pallas_call x1, Pallas kernels, make_open(): pl.pallas_call(functools.partial(open_kernel, widths), out_shape=[jax.Sha...  5.42 us
    pallas_call x3, Pallas kernels, make_merge(): pl.pallas_call(functools.partial(merge_kernel, cap, rows // 4, tuple(span...  4.71 us
    ppermute x6, waiting for transfers between devices, passed_along(): return lax.ppermute(block, axis, route)  4.63 us
  transfers between devices with their start and end apart: 16, of which 8 were waited for; matrix products, arithmetic and copies ran while one was open for 0% of the time, Pallas kernels for 16%

commit v1 on v0

--- a/solution.py
+++ b/solution.py
@@ -9,9 +9,9 @@
 
 CAP = 2
 TILE = 512
-CHUNKS = (2, 2, 2, 2, 2)
+CHUNKS = (2, 2, 3, 2, 1)
 STAGES = (((0, 1, 2), (0, 1)), ((3, 4), (2, 3)), ((), (4,)))
-DEPTH = 1
+DEPTH, LAG = 2, 3
 F32, BF16 = jnp.float32, jnp.bfloat16
 
 
@@ -42,8 +42,8 @@
 
 def open_kernel(widths, wiring_ref, mask_ref, g_ref, x_ref, dy_ref, down_ref, up_ref, plan_ref, choice_ref, low_ref,
                 high_ref, *refs):
-    outs = refs[: len(widths)]
-    x_scr, dy_scr, down_scr, up_scr, extra, in_sems, out_sems, extra_sem = refs[len(widths) :]
+    outs, late_ref = refs[: len(widths)], refs[len(widths)]
+    x_scr, dy_scr, down_scr, up_scr, extra, in_sems, out_sems, extra_sems = refs[len(widths) + 1 :]
     rows, width = x_ref.shape
     rank = up_ref.shape[0]
     pieces = [slice(i, i + PIECE) for i in range(0, width, PIECE)]
@@ -55,13 +55,6 @@
     for some in loads:
         for copy in some:
             copy.start()
-    stores, first = [], 0
-    for c, cols in enumerate(widths):
-        for n, scr in enumerate((x_scr, dy_scr)):
-            to = outs[c].at[pl.ds(n * rows, rows), :]
-            stores.append((first + cols, pltpu.make_async_copy(scr.at[:, pl.ds(first, cols)], to, out_sems.at[2 * c + n])))
-        first += cols
-
     section, peer = lax.axis_index("section"), lax.axis_index("peer")
     count = wiring_ref.shape[0]
     before = lax.rem(section + count - 1, count)
@@ -113,6 +106,37 @@
             for j in range(4):
                 twos += jnp.where(wiring_ref[at, i, j] == 2, 1, 0)
     choice_ref[0] = mask - 1 + jnp.where(twos > 8, 3, 0)
+    for n, (owner, to) in enumerate(((peer, match), (match, peer))):
+        wanted, cum = [jnp.int32(0)] * 4, jnp.int32(0)
+        for q in range(4):
+            amount = wiring_ref[before, q, owner]
+            near = ((q == to) | (q == (to ^ jnp.where(mask >= 2, 1, 2)))).astype(jnp.int32)
+            for k in range(4):
+                wanted[k] = jnp.where((cum <= k) & (k < cum + amount), near, wanted[k])
+            cum += amount
+        total = sum(wanted)
+        ahead, behind = jnp.int32(0), jnp.int32(0)
+        slots = []
+        for k in range(4):
+            slots.append(jnp.where(wanted[k] == 1, ahead, total + behind))
+            ahead += wanted[k]
+            behind += 1 - wanted[k]
+        for j in range(4):
+            plan_ref[16 + 4 * n + j] = sum(jnp.where(slots[k] == j, k, 0) for k in range(4))
+
+    blk = rows // 4
+    stores, first = [], 0
+    for c, cols in enumerate(widths):
+        at = pl.ds(first, cols)
+        first += cols
+        sem = out_sems.at[4 * c]
+        stores.append((first, pltpu.make_async_copy(x_scr.at[:, at], outs[c].at[pl.ds(0, rows), :], sem)))
+        for j in range(3):
+            from_rows = pl.ds(pl.multiple_of(plan_ref[16 + j] * blk, blk), blk)
+            to = outs[c].at[pl.ds(rows + j * blk, blk), :]
+            stores.append((first, pltpu.make_async_copy(dy_scr.at[from_rows, at], to, out_sems.at[4 * c + 1 + j])))
+    from_rows = pl.ds(pl.multiple_of(plan_ref[19] * blk, blk), blk)
+    stores.append((width, pltpu.make_async_copy(dy_scr.at[from_rows, :], late_ref, extra_sems.at[1])))
 
     square = jnp.zeros((rows, 1), F32)
     pre = jnp.zeros((rows, rank), F32)
@@ -125,10 +149,12 @@
                 copy.start()
         x = x_scr[:, at].astype(F32)
         square += jnp.sum(x * x, axis=1, keepdims=True)
-        pre += dot((x * g_ref[:, at]).astype(BF16), down_scr[at, :], ((1,), (0,)))
         dact += dot(dy_scr[:, at], up_scr[:, at], ((1,), (1,)))
     rinv = lax.rsqrt(square / width + 1e-05)
-    v = pre * rinv
+    for at in pieces:
+        normed = (x_scr[:, at].astype(F32) * rinv * g_ref[:, at]).astype(BF16)
+        pre += dot(normed, down_scr[at, :], ((1,), (0,)))
+    v = pre
     sig = jax.nn.sigmoid(v)
     act = (v * sig).astype(BF16)
     dpre = (dact * sig * (1.0 + v * (1.0 - sig))).astype(BF16)
@@ -154,7 +180,7 @@
     extra[band:, :] = jnp.zeros_like(extra[band:, :])
     extra[band : band + 16, 0:rows] = jnp.concatenate([parts[0], parts[1]], axis=0)
     extra[band : band + 16, rows : 2 * rows] = jnp.concatenate([parts[2], parts[2]], axis=0)
-    last = pltpu.make_async_copy(extra, outs[0].at[pl.ds(2 * rows, band + 16), :], extra_sem)
+    last = pltpu.make_async_copy(extra, outs[0].at[pl.ds(rows + 3 * blk, band + 16), :], extra_sems.at[0])
     last.start()
     for _, copy in stores:
         copy.wait()
@@ -167,23 +193,25 @@
     band = 2 * rows * rank // widths[0]
     hbm = pl.BlockSpec(memory_space=pl.ANY)
     vmem = pl.BlockSpec(memory_space=pltpu.VMEM)
-    tall = [2 * rows + band + 16] + [2 * rows] * (len(widths) - 1)
+    sent = rows + 3 * (rows // 4)
+    tall = [sent + band + 16] + [sent] * (len(widths) - 1)
     return pl.pallas_call(
         functools.partial(open_kernel, widths),
         out_shape=[
-            jax.ShapeDtypeStruct((16,), jnp.int32),
+            jax.ShapeDtypeStruct((24,), jnp.int32),
             jax.ShapeDtypeStruct((1,), jnp.int32),
             jax.ShapeDtypeStruct((2 * rows, rank), BF16),
             jax.ShapeDtypeStruct((8, rows), F32),
-        ] + [jax.ShapeDtypeStruct((n, cols), BF16) for n, cols in zip(tall, widths)],
+        ] + [jax.ShapeDtypeStruct((n, cols), BF16) for n, cols in zip(tall, widths)]
+        + [jax.ShapeDtypeStruct((rows // 4, width), BF16)],
         in_specs=[SMEM, SMEM, vmem, hbm, hbm, hbm, hbm],
-        out_specs=[SMEM, SMEM, vmem, vmem] + [hbm] * len(widths),
+        out_specs=[SMEM, SMEM, vmem, vmem] + [hbm] * (len(widths) + 1),
         scratch_shapes=[
             pltpu.VMEM((rows, width), BF16), pltpu.VMEM((rows, width), BF16),
             pltpu.VMEM((width, rank), BF16), pltpu.VMEM((rank, width), BF16),
             pltpu.VMEM((band + 16, widths[0]), BF16),
-            pltpu.SemaphoreType.DMA((4 * (width // PIECE),)), pltpu.SemaphoreType.DMA((2 * len(widths),)),
-            pltpu.SemaphoreType.DMA,
+            pltpu.SemaphoreType.DMA((4 * (width // PIECE),)), pltpu.SemaphoreType.DMA((4 * len(widths),)),
+            pltpu.SemaphoreType.DMA((2,)),
         ],
         compiler_params=ROOM,
         cost_estimate=FREE,
@@ -196,9 +224,10 @@
     bands = got_ref.shape[1] // rank
     band = rows2 // bands
     rows = rows2 // 2
+    first = got_ref.shape[0] - band - 16
     for j in range(bands):
-        low_ref[j * band : (j + 1) * band, :] = got_ref[rows2 : rows2 + band, j * rank : (j + 1) * rank]
-    parts = got_ref[rows2 + band : rows2 + band + 16, :].astype(F32)
+        low_ref[j * band : (j + 1) * band, :] = got_ref[first : first + band, j * rank : (j + 1) * rank]
+    parts = got_ref[first + band :, :].astype(F32)
     high_ref[...] = parts[0:8, 0:rows] + parts[8:16, 0:rows] + parts[0:8, rows : 2 * rows]
 
 
@@ -219,28 +248,36 @@
     return pl.BlockSpec(shape, lambda i: (0,) * len(shape))
 
 
-def column(rows, first=0):
-    return pl.BlockSpec((rows, TILE), lambda i: (0, first + i))
-
-
-def chunk(rows, start, end):
-    return pl.BlockSpec((rows, TILE), lambda i: (0, jnp.clip(i - start, 0, end - start - 1)))
+def column(rows, first=0, tile=TILE):
+    return pl.BlockSpec((rows, tile), lambda i: (0, first + i))
+
+
+def chunk(rows, start, end, tile=TILE):
+    return pl.BlockSpec((rows, tile), lambda i: (0, jnp.clip(i - start, 0, end - start - 1)))
 
 
 def rows_kernel(cap, blk, plan_ref, x_ref, dy_ref, got_ref, low_ref, low2_ref, high_ref, high2_ref, up_ref, down_ref,
-                g_ref, send_ref, keep_f_ref, keep_b_ref, out_scr, dx_scr):
+                g_ref, *refs):
+    late_refs = refs[: cap - 3]
+    send_ref, keep_f_ref, keep_b_ref, out_scr, dx_scr, rest_scr = refs[cap - 3 :]
     rows = x_ref.shape[0]
     for half in range(2):
         part = pl.ds(half * rows, rows)
         x = (x_ref[...] if half == 0 else got_ref[:rows, :]).astype(F32)
-        dy = (dy_ref[...] if half == 0 else got_ref[rows:, :]).astype(F32)
         low = low_ref if half == 0 else low2_ref
         stat = (high_ref if half == 0 else high2_ref)[...].T
         out = x + dot(low[:rows, :], up_ref[...], ((1,), (0,)))
         out_scr[part, :] = out.astype(BF16)
         dn = dot(low[rows:, :], down_ref[...], ((1,), (1,))) * g_ref[...]
-        dx = dy + stat[:, 0:1] * dn - x * stat[:, 1:2]
-        dx_scr[part, :] = dx.astype(BF16)
+        rest = stat[:, 0:1] * dn - x * stat[:, 1:2]
+        if half == 0:
+            dx_scr[part, :] = (dy_ref[...].astype(F32) + rest).astype(BF16)
+        else:
+            rest_scr[...] = rest
+    for j in range(cap):
+        dy = late_refs[0][...] if j == 3 else got_ref[rows + j * blk : rows + (j + 1) * blk, :]
+        at = pl.multiple_of(plan_ref[20 + j] * blk, blk)
+        dx_scr[pl.ds(rows + at, blk), :] = (dy.astype(F32) + rest_scr[pl.ds(at, blk), :]).astype(BF16)
 
     def block_of(scr, index):
         return scr[pl.ds(pl.multiple_of(index * blk, blk), blk), :]
@@ -253,7 +290,7 @@
             keep_ref[pl.ds(k * blk, blk), :] = block_of(scr, jnp.minimum(plan_ref[8 + 4 * n + k], 7))
 
 
-def make_rows(cap, first, tiles, plan, x, dy, got, low, low2, high, high2, up, down, g):
+def make_rows(cap, first, tiles, plan, x, dy, got, low, low2, high, high2, up, down, g, late):
     rows, width = x.shape
     rank = up.shape[0]
     blk = rows // 4
@@ -267,16 +304,18 @@
             jax.ShapeDtypeStruct((rows, cols), BF16),
         ),
         in_specs=[
-            SMEM, column(rows, first), column(rows, first), column(2 * rows),
+            SMEM, column(rows, first), column(rows, first), column(rows + 3 * blk),
             whole(low.shape), whole(low.shape), whole(high.shape), whole(high.shape),
             column(rank, first), pl.BlockSpec((TILE, rank), lambda i: (first + i, 0)), column(1, first),
+        ] + [column(blk, first)] * (cap - 3),
+        out_specs=(column(2 * cap * blk), column(rows), column(rows)),
+        scratch_shapes=[
+            pltpu.VMEM((2 * rows, TILE), BF16), pltpu.VMEM((2 * rows, TILE), BF16), pltpu.VMEM((rows, TILE), F32)
         ],
-        out_specs=(column(2 * cap * blk), column(rows), column(rows)),
-        scratch_shapes=[pltpu.VMEM((2 * rows, TILE), BF16), pltpu.VMEM((2 * rows, TILE), BF16)],
         compiler_params=ROOM,
         cost_estimate=FREE,
         name="rows",
-    )(plan, x, dy, got, low, low2, high, high2, up, down, g)
+    )(plan, x, dy, got, low, low2, high, high2, up, down, g, *[late] * (cap - 3))
 
 
 def merge_kernel(cap, blk, spans, plan_ref, *refs):
@@ -363,71 +402,97 @@
     )(*into, *nexts, *returns)
 
 
-def grads_kernel(starts, x_ref, dy_ref, *refs):
-    got_refs = refs[: len(starts) - 1]
-    low_ref, low2_ref, high_ref, high2_ref, g_ref = refs[len(starts) - 1 : len(starts) + 4]
-    gup_ref, gdown_ref, x_scr, dy_scr, act_scr, dpre_scr, rinv_scr = refs[-7:]
-    step = pl.program_id(0)
+VMEM = pl.BlockSpec(memory_space=pltpu.VMEM)
+
+
+def grad_down_kernel(x_ref, low_ref, low2_ref, high_ref, high2_ref, g_ref, *refs):
+    got_refs, to_ref = refs[:-1], refs[-1]
     rows = x_ref.shape[0]
-
-    @pl.when(step == 0)
-    def _():
-        for half, (low, high) in enumerate(((low_ref, high_ref), (low2_ref, high2_ref))):
-            part = pl.ds(half * rows, rows)
-            act_scr[part, :] = (low[:rows, :].astype(F32) * 0.5).astype(BF16)
-            dpre_scr[part, :] = (low[rows:, :].astype(F32) * 0.5).astype(BF16)
-            rinv_scr[part, :] = high[...].T[:, 0:1]
-
-    dy_scr[:rows, :] = dy_ref[...]
-    x_scr[:rows, :] = x_ref[...]
-    for c, got_ref in enumerate(got_refs):
-
-        @pl.when((step >= starts[c]) & (step < starts[c + 1]))
-        def _():
-            x_scr[rows:, :] = got_ref[:rows, :]
-            dy_scr[rows:, :] = got_ref[rows:, :]
-
-    gup_ref[...] = dot(act_scr[...], dy_scr[...], ((0,), (0,)))
-    normed = (x_scr[...].astype(F32) * rinv_scr[...] * g_ref[...]).astype(BF16)
-    gdown_ref[...] = dot(normed, dpre_scr[...], ((0,), (0,)))
-
-
-def make_grads(first, x, dy, got, low, low2, high, high2, g, into=()):
-    rows, width = x.shape
-    rank = low.shape[1]
-    starts = [0]
-    for block in got:
-        starts.append(starts[-1] + block.shape[1] // TILE)
-
-    def kernel(*refs):
-        grads_kernel(tuple(starts), *refs[len(into):])
-
-    return pl.pallas_call(
-        kernel,
-        grid=(starts[-1],),
-        out_shape=(jax.ShapeDtypeStruct((rank, width), F32), jax.ShapeDtypeStruct((width, rank), F32)),
-        in_specs=[pl.BlockSpec(memory_space=pl.ANY)] * len(into)
-        + [column(rows, first), column(rows, first)] + [chunk(2 * rows, s, e) for s, e in zip(starts[:-1], starts[1:])]
-        + [whole(low.shape), whole(low.shape), whole(high.shape), whole(high.shape), column(1, first)],
-        out_specs=(column(rank, first), pl.BlockSpec((TILE, rank), lambda i: (first + i, 0))),
-        scratch_shapes=[
-            pltpu.VMEM((2 * rows, TILE), BF16), pltpu.VMEM((2 * rows, TILE), BF16),
-            pltpu.VMEM((2 * rows, rank), BF16), pltpu.VMEM((2 * rows, rank), BF16), pltpu.VMEM((2 * rows, 1), F32),
-        ],
-        input_output_aliases={i: i for i in range(len(into))},
-        compiler_params=ROOM,
-        cost_estimate=FREE,
-        name="grads",
-    )(*into, x, dy, *got, low, low2, high, high2, g)
+    dpre = [(low[rows:, :].astype(F32) * 0.5).astype(BF16) for low in (low_ref, low2_ref)]
+    rinv = [high[...].T[:, 0:1] for high in (high_ref, high2_ref)]
+    first = 0
+    for got_ref in got_refs:
+        at = slice(first, first + got_ref.shape[1])
+        first = at.stop
+        g = g_ref[:, at]
+        own = (x_ref[:, at].astype(F32) * rinv[0] * g).astype(BF16)
+        other = (got_ref[:rows, :].astype(F32) * rinv[1] * g).astype(BF16)
+        to_ref[at, :] = dot(own, dpre[0], ((0,), (0,))) + dot(other, dpre[1], ((0,), (0,)))
+
+
+def make_grad_down(x, got, low, low2, high, high2, g):
+    return pl.pallas_call(
+        grad_down_kernel,
+        out_shape=jax.ShapeDtypeStruct((x.shape[1], low.shape[1]), F32),
+        in_specs=[VMEM] * (6 + len(got)),
+        out_specs=VMEM,
+        compiler_params=ROOM,
+        cost_estimate=FREE,
+        name="grad_down",
+    )(x, low, low2, high, high2, g, *got)
+
+
+def turned_act(plan_ref, low2_ref, j, blk):
+    at = pl.ds(pl.multiple_of(plan_ref[20 + j] * blk, blk), blk)
+    return (low2_ref[at, :].astype(F32) * 0.5).T.astype(BF16)
+
+
+def grad_up_kernel(plan_ref, dy_ref, low_ref, low2_ref, *refs):
+    got_refs, to_ref = refs[:-1], refs[-1]
+    rows = dy_ref.shape[0]
+    blk = rows // 4
+    own = (low_ref[:rows, :].astype(F32) * 0.5).T.astype(BF16)
+    other = jnp.concatenate([turned_act(plan_ref, low2_ref, j, blk) for j in range(3)], axis=1)
+    first = 0
+    for got_ref in got_refs:
+        at = slice(first, first + got_ref.shape[1])
+        first = at.stop
+        to_ref[:, at] = dot(own, dy_ref[:, at], ((1,), (0,))) + dot(
+            other, got_ref[rows : rows + 3 * blk, :], ((1,), (0,))
+        )
+
+
+def make_grad_up(plan, dy, got, low, low2):
+    return pl.pallas_call(
+        grad_up_kernel,
+        out_shape=jax.ShapeDtypeStruct((low.shape[1], dy.shape[1]), F32),
+        in_specs=[SMEM] + [VMEM] * (3 + len(got)),
+        out_specs=VMEM,
+        compiler_params=ROOM,
+        cost_estimate=FREE,
+        name="grad_up",
+    )(plan, dy, low, low2, *got)
+
+
+def grad_up_late_kernel(plan_ref, so_far_ref, late_ref, low2_ref, to_ref):
+    blk = late_ref.shape[0]
+    act = turned_act(plan_ref, low2_ref, 3, blk)
+    to_ref[...] = so_far_ref[...] + dot(act, late_ref[...], ((1,), (0,)))
+
+
+def make_grad_up_late(plan, so_far, late, low2):
+    rank, width = so_far.shape
+    blk = late.shape[0]
+    tile = 2 * TILE
+    return pl.pallas_call(
+        grad_up_late_kernel,
+        grid=(width // tile,),
+        out_shape=jax.ShapeDtypeStruct((rank, width), F32),
+        in_specs=[SMEM, column(rank, 0, tile), column(blk, 0, tile), whole(low2.shape)],
+        out_specs=column(rank, 0, tile),
+        input_output_aliases={1: 0},
+        compiler_params=ROOM,
+        cost_estimate=FREE,
+        name="grad_up_late",
+    )(plan, so_far, late, low2)
 
 
 def four_peers(inputs, out_grad, gains, down_proj, up_proj, wiring, pair_mask):
     x, dy, down, up = inputs[0, 0], out_grad[0, 0], down_proj[0], up_proj[0]
     width = x.shape[1]
     count = len(CHUNKS)
-    early = count - 1
     starts = [sum(CHUNKS[:c]) for c in range(count + 1)]
-    plan, choice, low, high, *outs = make_open(
+    plan, choice, low, high, *outs, late = make_open(
         [n * TILE for n in CHUNKS], wiring, pair_mask, gains, x, dy, down, up
     )
     choice = choice[0]
@@ -436,12 +501,13 @@
         exchange, route = STAGES[number]
         if number == 0:
             held = {}
+            late2 = swapped(late, "peer", mask) if cap == 4 else late
         else:
-            low2, high2, held, grads = state
+            low2, high2, late2, held = state
         held, parts, backs, sent = dict(held), [], {}, plan
 
         def send_on(c):
-            ready = [source[d] for source, d in ((held, c - DEPTH), (backs, c - DEPTH - 1)) if d in source]
+            ready = [source[d] for source, d in ((held, c - DEPTH), (backs, c - LAG)) if d in source]
             held[c] = swapped(after(outs[c], *ready) if ready else outs[c], "peer", mask)
 
         waiting = list(exchange)
@@ -452,7 +518,7 @@
         common = (low, low2, high, high2)
         for c in route:
             send, keep_f, keep_b = make_rows(
-                cap, starts[c], CHUNKS[c], after(plan, sent), x, dy, held[c], *common, up, down, gains
+                cap, starts[c], CHUNKS[c], after(plan, sent), x, dy, held[c], *common, up, down, gains, late2
             )
             backs[c] = swapped(send, "peer", 1 if mask >= 2 else 2)
             parts.append((keep_f, keep_b, backs[c]))
@@ -461,30 +527,32 @@
                 send_on(waiting.pop(0))
         while waiting:
             send_on(waiting.pop(0))
-        if number == 0:
-            grads = ()
-        elif number == 1:
-            grads = make_grads(0, after(x, sent), dy, [held[c] for c in range(early)], *common, gains)
+        grads = ()
+        if number == len(STAGES) - 1 and cap == 3:
+            late2 = swapped(after(late, held[count - 1]), "peer", mask)
+        if number == len(STAGES) - 1:
+            blocks = [held[c] for c in range(count)]
+            up_grad = make_grad_up(after(plan, sent), dy, blocks, low, low2)
+            grads = up_grad, make_grad_down(after(x, up_grad), blocks, *common, gains)
         merged = make_merge(cap, after(plan, sent), parts)
-        return merged, (low2, high2) if number == 0 else (), {c: held[c] for c in exchange}, grads
+        return merged, (low2, high2) if number == 0 else (), late2, {c: held[c] for c in exchange}, grads
 
     state = None
     nexts, returns = [], []
     for number in range(len(STAGES)):
         branches = [functools.partial(stage, number, cap, m) for cap in (3, 4) for m in (1, 2, 3)]
-        (f, b), made, arrived, grads = lax.switch(choice, branches, state)
+        (f, b), made, late2, arrived, grads = lax.switch(choice, branches, state)
         if number == 0:
             low2, high2 = made
             held = {}
         held = {**held, **arrived}
-        state = (low2, high2, held, grads)
+        state = (low2, high2, late2, held)
         if number:
             f, b = after(f, nexts[-1], returns[-1]), after(b, nexts[-1], returns[-1])
         nexts.append(passed_along(f, "section", 1))
         returns.append(passed_along(b, "section", -1))
-    grad_up, grad_down = make_grads(
-        starts[early], after(x, f, b), dy, [held[c] for c in range(early, count)], low, low2, high, high2, gains, into=grads
-    )
+    so_far, grad_down = grads
+    grad_up = make_grad_up_late(plan, after(so_far, f, b), late2, low2)
     joined = make_join(width, 0, [after(nexts[0], f, b), *nexts[1:-1]], returns[:-1])
     done = sum(part.shape[1] for part in nexts[:-1])
     next_rows, return_rows = make_join(width, done, nexts[-1:], returns[-1:], into=joined)

time: 164 us -> 168 us (1.024)
  starting transfers between devices: 49 us -> 57.5 us
  waiting for transfers between devices: 76.6 us -> 68.8 us
  local copies, waits for them, and re-layouts: 1.49 us -> 3.25 us
    ppermute x6, starting transfers between devices: 30.5 us -> 35.9 us  [passed_along(): return lax.ppermute(block, axis, route)]
    ppermute x10 -> x11, waiting for transfers between devices: 72 us -> 67.2 us  [swapped(): lax.ppermute(block, axis, [(i, i ^ mask) for i in range(count) if i ^ mas...]
    ppermute x10 -> x11, starting transfers between devices: 18.5 us -> 21.7 us  [swapped(): lax.ppermute(block, axis, [(i, i ^ mask) for i in range(count) if i ^ mas...]
    ppermute x6, waiting for transfers between devices: 4.63 us -> 1.6 us  [passed_along(): return lax.ppermute(block, axis, route)]
    cond x10 -> x15, local copies, waits for them, and re-layouts: 0.02 us -> 1.76 us
    pallas_call x2 -> x3, Pallas kernels: 9.94 us -> 8.78 us  [the longest x1 3.64 us: make_grad_up_late(): pl.pallas_call(grad_up_late_kernel, grid=(width // tile,), out_shape=jax....]
  transfers between devices with their start and end apart: 16 -> 17, of which waited for: 8 -> 8; matrix products, arithmetic and copies ran while one was open for 0% -> 1% of each run, Pallas kernels for 16% -> 16%
where the time goes in v1:
time: 168 us; the launch traced here: 166 us
  waiting for transfers between devices  68.8 us (41%)
  starting transfers between devices  57.5 us (34%)
  Pallas kernels  33.9 us (20%)
  local copies, waits for them, and re-layouts  3.25 us (2%)
    ppermute x11, waiting for transfers between devices, swapped(): lax.ppermute(block, axis, [(i, i ^ mask) for i in range(count) if i ^ mas...  67.2 us
    ppermute x6, starting transfers between devices, passed_along(): return lax.ppermute(block, axis, route)  35.9 us
    ppermute x11, starting transfers between devices, swapped(): lax.ppermute(block, axis, [(i, i ^ mask) for i in range(count) if i ^ mas...  21.7 us
    pallas_call x5, Pallas kernels, make_rows(): pl.pallas_call(functools.partial(rows_kernel, cap, blk), grid=(tiles,), o...  11.2 us
    pallas_call x1, Pallas kernels, make_open(): pl.pallas_call(functools.partial(open_kernel, widths), out_shape=[jax.Sha...  6.51 us
    pallas_call x3, Pallas kernels, make_merge(): pl.pallas_call(functools.partial(merge_kernel, cap, rows // 4, tuple(span...  4.39 us
    pallas_call x1, Pallas kernels, make_grad_up_late(): pl.pallas_call(grad_up_late_kernel, grid=(width // tile,), out_shape=jax....  3.64 us
  transfers between devices with their start and end apart: 17, of which 8 were waited for; matrix products, arithmetic and copies ran while one was open for 1% of the time, Pallas kernels for 16%

profile of v1, /device:TPU:1, one launch (start us, length us, event | category | flops | bytes accessed | tf_op | source)
XLA Modules:
  0.0 165.5 jit_solution(4714527775408808890)
XLA Ops:
  0.6 0.8 copy.14.wiring_ref
  1.4 0.7 copy-done
  2.1 0.0 copy-start.48
  2.1 6.5 %open.1 = (s32[24]{0:T(128)S(1)}, s32[1]{0:T(128)}, bf16[256,128]{1,0:T(8,128)(2,1)S(1)}, f32[8,128]{1,0:T(8,128)S(1)}, bf16[272,1024]{1,0:T(8,128)(2,1)S(1)}, /...) custom-call(s32[8,4,4]{2,1,0:T(4,128)S(1)} %copy.14.wiring_ref, ...), custom_call_target="tpu_custom_call" | custom-call | tf_op jit(solution)/shard_map/open/pallas_call | solution.py:198
  9.3 62.9 %conditional.3 = (bf16[128,2048]{1,0:T(8,128)(2,1)}, bf16[128,2048]{1,0:T(8,128)(2,1)}, bf16[256,128]{1,0:T(8,128)(2,1)}, f32[8,128]{1,0:T(8,128)}, bf16[32,5120...) conditional(s32[]{:T(128)} %bitcast.10, (s32[24]{0:T(128)S(1)}, ...), branch_computations={%region_0.0_spmd, %region_1.0_spmd, %region_2.0_spmd, %region_3.0_... | conditional | bytes 14549324 | solution.py:544
  9.3 2.2 %collective-permute-start = (bf16[272,1024]{1,0:T(8,128)(2,1)S(1)}, bf16[272,1024]{1,0:T(8,128)(2,1)S(1)}, u32[]{:S(2)}, u32[]{:S(2)}) collective-permute-start(bf16[272,1024]{1,0:T(8,128)(2,1)S(1)} %get-tuple-element.481), channel_id=1, source_target_pairs={{0,1},{1,0},{2,3},{3,2},{4,5},{5,4},{6,7},{7,6},{8,9},{9,8},{10,11... | collective-permute-start | bytes 1671176 | tf_op jit(solution)/shard_map/cond/branch_0_fun/ppermute | solution.py:26
  11.5 0.1 collective-permute-start.1
  11.6 12.3 %collective-permute-done.got_ref = bf16[272,1024]{1,0:T(8,128)(2,1)S(1)} collective-permute-done((bf16[272,1024]{1,0:T(8,128)(2,1)S(1)}, bf16[272,1024]{1,0:T(8,128)(2,1)S(1)}, u32[]{:S(2)}, u32[]{:S(2)}) %collective-permute-start) | collective-permute-done | bytes 557088 | tf_op jit(solution)/shard_map/cond/branch_0_fun/ppermute | solution.py:26
  23.9 1.1 collective-permute-start.4
  25.0 0.6 unpack.6
  25.7 1.8 %rows.30 = (bf16[192,1024]{1,0:T(8,128)(2,1)S(1)}, bf16[128,1024]{1,0:T(8,128)(2,1)S(1)}, bf16[128,1024]{1,0:T(8,128)(2,1)S(1)}) custom-call(s32[24]{0:T(128)S(1)} %get-tuple-element.521.plan_ref, bf16[128,5120]{1,0:T(8,128)(2,1)S(1)} %get-tuple-element.479.x_ref, bf16[128,5120]{1,0:T(8,128)(2,1)S(1)} %get-tuple-element.480.dy_ref, ...), custom_call_target="tpu_custom_call" | custom-call | tf_op jit(solution)/shard_map/cond/branch_0_fun/rows/pallas_call | solution.py:298
  27.5 2.4 %collective-permute-start.2 = (bf16[192,1024]{1,0:T(8,128)(2,1)S(1)}, bf16[192,1024]{1,0:T(8,128)(2,1)S(1)}, u32[]{:S(2)}, u32[]{:S(2)}) collective-permute-start(bf16[192,1024]{1,0:T(8,128)(2,1)S(1)} %get-tuple-element.517), channel_id=1, source_target_pairs={{0,2},{1,3},{2,0},{3,1},{4,6},{5,7},{6,4},{7,5},{8,10},{9,11},{10,... | collective-permute-start | bytes 1179656 | tf_op jit(solution)/shard_map/cond/branch_0_fun/ppermute | solution.py:26
  29.9 12.4 %collective-permute-done.1.got_ref = bf16[224,1024]{1,0:T(8,128)(2,1)} collective-permute-done((bf16[224,1024]{1,0:T(8,128)(2,1)S(1)}, bf16[224,1024]{1,0:T(8,128)(2,1)}, u32[]{:S(2)}, u32[]{:S(2)}) %collective-permute-start.1) | collective-permute-done | bytes 458784 | tf_op jit(solution)/shard_map/cond/branch_0_fun/ppermute | solution.py:26
  42.2 1.9 %rows.31 = (bf16[192,1024]{1,0:T(8,128)(2,1)S(1)}, bf16[128,1024]{1,0:T(8,128)(2,1)S(1)}, bf16[128,1024]{1,0:T(8,128)(2,1)S(1)}) custom-call(s32[24]{0:T(128)S(1)} %get-tuple-element.521.plan_ref, bf16[128,5120]{1,0:T(8,128)(2,1)S(1)} %get-tuple-element.479.x_ref, bf16[128,5120]{1,0:T(8,128)(2,1)S(1)} %get-tuple-element.480.dy_ref, ...), custom_call_target="tpu_custom_call" | custom-call | tf_op jit(solution)/shard_map/cond/branch_0_fun/rows/pallas_call | solution.py:298
  44.1 1.2 collective-permute-start.3
  45.4 1.7 %copy.19 = bf16[32,5120]{1,0:T(8,128)(2,1)} copy(bf16[32,5120]{1,0:T(8,128)(2,1)} %get-tuple-element.1043) | data formatting | bytes 655360 | tf_op jit(solution)/shard_map/cond
  47.1 8.8 %collective-permute-done.2.refs_2_ = bf16[192,1024]{1,0:T(8,128)(2,1)S(1)} collective-permute-done((bf16[192,1024]{1,0:T(8,128)(2,1)S(1)}, bf16[192,1024]{1,0:T(8,128)(2,1)S(1)}, u32[]{:S(2)}, u32[]{:S(2)}) %collective-permute-start.2) | collective-permute-done | bytes 393248 | tf_op jit(solution)/shard_map/cond/branch_0_fun/ppermute | solution.py:26
  55.9 14.7 %collective-permute-done.3.refs_5_ = bf16[192,1024]{1,0:T(8,128)(2,1)S(1)} collective-permute-done((bf16[192,1024]{1,0:T(8,128)(2,1)S(1)}, bf16[192,1024]{1,0:T(8,128)(2,1)S(1)}, u32[]{:S(2)}, u32[]{:S(2)}) %collective-permute-start.3) | collective-permute-done | bytes 393248 | tf_op jit(solution)/shard_map/cond/branch_0_fun/ppermute | solution.py:26
  70.6 1.6 merge.18
  72.2 0.0 collective-permute-done.4
  72.3 22.9 %collective-permute-start.66 = (bf16[128,2048]{1,0:T(8,128)(2,1)}, bf16[128,2048]{1,0:T(8,128)(2,1)S(1)}, u32[]{:S(2)}, u32[]{:S(2)}) collective-permute-start(bf16[128,2048]{1,0:T(8,128)(2,1)} %get-tuple-element.1010), channel_id=1, source_target_pairs={{28,0},{0,4},{4,8},{8,12},{12,16},{16,20},{20,24},{24,28},{29,1},{... | collective-permute-start | bytes 1572872 | tf_op jit(solution)/shard_map/ppermute | solution.py:21
  95.1 0.0 collective-permute-start.67
  95.1 35.9 %conditional.4 = (bf16[128,2560]{1,0:T(8,128)(2,1)}, bf16[128,2560]{1,0:T(8,128)(2,1)}, bf16[224,1024]{1,0:T(8,128)(2,1)}, bf16[224,512]{1,0:T(8,128)(2,1)}) conditional(s32[]{:T(128)} %bitcast.10, (s32[24]{0:T(128)S(1)}, bf16[128,5120]{1,0:T(8,128)(2,1)}, bf16[128,5120]{1,0:T(8,128)(2,1)}, ...), branch_computations={%region_6.0_spmd, %region_7.0_spmd, %region_8.0_spmd, %region_9.0_... | conditional | bytes 28967216 | solution.py:544
  95.1 0.0 collective-permute-start.33
  95.1 0.0 copy-start.2
  95.1 0.0 copy-start.15
  95.1 0.0 copy-start.28
  95.2 0.0 copy-start.35
  95.2 3.9 %rows.42 = (bf16[192,1536]{1,0:T(8,128)(2,1)S(1)}, bf16[128,1536]{1,0:T(8,128)(2,1)S(1)}, bf16[128,1536]{1,0:T(8,128)(2,1)S(1)}) custom-call(s32[24]{0:T(128)S(1)} %get-tuple-element.677.plan_ref, bf16[128,5120]{1,0:T(8,128)(2,1)} %get-tuple-element.663.x_ref, bf16[128,5120]{1,0:T(8,128)(2,1)} %get-tuple-element.664.dy_ref, ...), custom_call_target="tpu_custom_call" | custom-call | tf_op jit(solution)/shard_map/cond/branch_0_fun/rows/pallas_call | solution.py:298
  99.0 5.4 %collective-permute-start.34 = (bf16[192,1536]{1,0:T(8,128)(2,1)S(1)}, bf16[192,1536]{1,0:T(8,128)(2,1)S(1)}, u32[]{:S(2)}, u32[]{:S(2)}) collective-permute-start(bf16[192,1536]{1,0:T(8,128)(2,1)S(1)} %get-tuple-element.673), channel_id=1, source_target_pairs={{0,2},{1,3},{2,0},{3,1},{4,6},{5,7},{6,4},{7,5},{8,10},{9,11},{10,... | collective-permute-start | bytes 1769480 | tf_op jit(solution)/shard_map/cond/branch_0_fun/ppermute | solution.py:26
  104.4 6.0 %collective-permute-done.33.got_ref = bf16[224,1024]{1,0:T(8,128)(2,1)} collective-permute-done((bf16[224,1024]{1,0:T(8,128)(2,1)}, bf16[224,1024]{1,0:T(8,128)(2,1)}, u32[]{:S(2)}, u32[]{:S(2)}) %collective-permute-start.33) | collective-permute-done | bytes 458784 | tf_op jit(solution)/shard_map/cond/branch_0_fun/ppermute | solution.py:26
  110.4 1.9 %rows.43 = (bf16[192,1024]{1,0:T(8,128)(2,1)S(1)}, bf16[128,1024]{1,0:T(8,128)(2,1)S(1)}, bf16[128,1024]{1,0:T(8,128)(2,1)S(1)}) custom-call(s32[24]{0:T(128)S(1)} %get-tuple-element.677.plan_ref, bf16[128,5120]{1,0:T(8,128)(2,1)S(1)} %copy-done.15, bf16[128,5120]{1,0:T(8,128)(2,1)S(1)} %copy-done.2, bf16[224,1024]{1,0:T(8,128)(2,1)} %collective-permute-done.33.got_ref, ...), custom_call_target="tpu_custom_call" | custom-call | tf_op jit(solution)/shard_map/cond/branch_0_fun/rows/pallas_call | solution.py:298
  112.4 1.8 %collective-permute-start.35 = (bf16[192,1024]{1,0:T(8,128)(2,1)S(1)}, bf16[192,1024]{1,0:T(8,128)(2,1)S(1)}, u32[]{:S(2)}, u32[]{:S(2)}) collective-permute-start(bf16[192,1024]{1,0:T(8,128)(2,1)S(1)} %get-tuple-element.676), channel_id=1, source_target_pairs={{0,2},{1,3},{2,0},{3,1},{4,6},{5,7},{6,4},{7,5},{8,10},{9,11},{10,... | collective-permute-start | bytes 1179656 | tf_op jit(solution)/shard_map/cond/branch_0_fun/ppermute | solution.py:26
  114.1 2.1 %collective-permute-start.36 = (bf16[224,512]{1,0:T(8,128)(2,1)S(1)}, bf16[224,512]{1,0:T(8,128)(2,1)}, u32[]{:S(2)}, u32[]{:S(2)}) collective-permute-start(bf16[224,512]{1,0:T(8,128)(2,1)S(1)} %get-tuple-element.685), channel_id=1, source_target_pairs={{0,1},{1,0},{2,3},{3,2},{4,5},{5,4},{6,7},{7,6},{8,9},{9,8},{10,11... | collective-permute-start | bytes 688136 | tf_op jit(solution)/shard_map/cond/branch_0_fun/ppermute | solution.py:26
  116.2 8.9 %collective-permute-done.34.refs_2_ = bf16[192,1536]{1,0:T(8,128)(2,1)S(1)} collective-permute-done((bf16[192,1536]{1,0:T(8,128)(2,1)S(1)}, bf16[192,1536]{1,0:T(8,128)(2,1)S(1)}, u32[]{:S(2)}, u32[]{:S(2)}) %collective-permute-start.34) | collective-permute-done | bytes 589856 | tf_op jit(solution)/shard_map/cond/branch_0_fun/ppermute | solution.py:26
  125.1 4.2 %collective-permute-done.35.refs_5_ = bf16[192,1024]{1,0:T(8,128)(2,1)S(1)} collective-permute-done((bf16[192,1024]{1,0:T(8,128)(2,1)S(1)}, bf16[192,1024]{1,0:T(8,128)(2,1)S(1)}, u32[]{:S(2)}, u32[]{:S(2)}) %collective-permute-start.35) | collective-permute-done | bytes 393248 | tf_op jit(solution)/shard_map/cond/branch_0_fun/ppermute | solution.py:26
  129.3 1.7 %merge.24 = (bf16[128,2560]{1,0:T(8,128)(2,1)}, bf16[128,2560]{1,0:T(8,128)(2,1)}) custom-call(s32[24]{0:T(128)S(1)} %get-tuple-element.677.plan_ref, bf16[128,1536]{1,0:T(8,128)(2,1)S(1)} %get-tuple-element.678.refs_0_, bf16[128,1536]{1,0:T(8,128)(2,1)S(1)} %get-tuple-element.679.refs_1_, bf16[192,1536]{1,0:T(8,128)(2,1)S(1)} %collective-permute-done.34.refs_2_, ...), custom_call_target="tpu_custom_call" | custom-call | tf_op jit(solution)/shard_map/cond/branch_0_fun/merge/pallas_call | solution.py:356
  131.0 0.0 collective-permute-done.36
  131.1 0.0 collective-permute-done.66.refs_0_
  131.1 0.0 collective-permute-done.67.refs_2_
  131.1 0.1 collective-permute-start.69
  131.1 8.9 %collective-permute-start.68 = (bf16[128,2560]{1,0:T(8,128)(2,1)}, bf16[128,2560]{1,0:T(8,128)(2,1)S(1)}, u32[]{:S(2)}, u32[]{:S(2)}) collective-permute-start(bf16[128,2560]{1,0:T(8,128)(2,1)} %get-tuple-element.1024), channel_id=1, source_target_pairs={{28,0},{0,4},{4,8},{8,12},{12,16},{16,20},{20,24},{24,28},{29,1},{... | collective-permute-start | bytes 1966088 | tf_op jit(solution)/shard_map/ppermute | solution.py:21
  140.0 0.0 copy-done.47
  140.0 13.7 %conditional.5 = (bf16[128,512]{1,0:T(8,128)(2,1)S(1)}, bf16[128,512]{1,0:T(8,128)(2,1)S(1)}, bf16[32,5120]{1,0:T(8,128)(2,1)}, f32[128,5120]{1,0:T(8,128)S(1)}, f32[1,1,5120,128]{3,2,1,0:T(8,128)S(1)}) conditional(s32[]{:T(128)} %bitcast.10, (s32[24]{0:T(128)S(1)}, bf16[128,5120]{1,0:T(8,128)(2,1)}, ...), branch_computations={%region_12.0_spmd, %region_13.0_spmd, %region_14.0_spmd, %region_1... | conditional | bytes 12583088 | solution.py:544
  140.0 0.0 collective-permute-start.58
  140.0 1.8 %rows.54 = (bf16[192,512]{1,0:T(8,128)(2,1)S(1)}, bf16[128,512]{1,0:T(8,128)(2,1)S(1)}, bf16[128,512]{1,0:T(8,128)(2,1)S(1)}) custom-call(s32[24]{0:T(128)S(1)} %get-tuple-element.827.plan_ref, bf16[128,5120]{1,0:T(8,128)(2,1)} %get-tuple-element.838.x_ref, bf16[128,5120]{1,0:T(8,128)(2,1)} %get-tuple-element.817.dy_ref, ...), custom_call_target="tpu_custom_call" | custom-call | tf_op jit(solution)/shard_map/cond/branch_0_fun/rows/pallas_call | solution.py:298
  141.8 5.4 %collective-permute-start.57 = (bf16[192,512]{1,0:T(8,128)(2,1)S(1)}, bf16[192,512]{1,0:T(8,128)(2,1)S(1)}, u32[]{:S(2)}, u32[]{:S(2)}) collective-permute-start(bf16[192,512]{1,0:T(8,128)(2,1)S(1)} %get-tuple-element.826), channel_id=1, source_target_pairs={{0,2},{1,3},{2,0},{3,1},{4,6},{5,7},{6,4},{7,5},{8,10},{9,11},{10,... | collective-permute-start | bytes 589832 | tf_op jit(solution)/shard_map/cond/branch_0_fun/ppermute | solution.py:26
  147.2 2.6 %grad_up.6 = f32[128,5120]{1,0:T(8,128)S(1)} custom-call(s32[24]{0:T(128)S(1)} %get-tuple-element.827.plan_ref, bf16[128,5120]{1,0:T(8,128)(2,1)S(1)} %copy-done.8, bf16[256,128]{1,0:T(8,128)(2,1)S(1)} %get-tuple-element.819.low_ref, bf16[256,128]{1,0:T(8,128)(2,1)} %get-tuple-element.820.low2_ref, bf16[272,1024]{1,0:T(8,128)(2,1)S(1)} %get-tuple-element.834.refs_0_, ...), custom_call_target="tpu_custom_call" | custom-call | tf_op jit(solution)/shard_map/cond/branch_0_fun/grad_up/pallas_call | solution.py:456
  149.8 0.0 copy-done.21
  149.8 2.6 %grad_down.6 = f32[5120,128]{1,0:T(8,128)S(1)} custom-call(bf16[128,5120]{1,0:T(8,128)(2,1)S(1)} %copy-done.21, bf16[256,128]{1,0:T(8,128)(2,1)S(1)} %get-tuple-element.819.low_ref, bf16[256,128]{1,0:T(8,128)(2,1)} %get-tuple-element.820.low2_ref, f32[8,128]{1,0:T(8,128)S(1)} %get-tuple-element.821.high_ref, f32[8,128]{1,0:T(8,128)} %get-tuple-element.822.high2_ref, ...), custom_call_target="tpu_custom_call" | custom-call | tf_op jit(solution)/shard_map/cond/branch_0_fun/grad_down/pallas_call | solution.py:424
  152.4 0.0 collective-permute-done.57.refs_2_
  152.4 1.1 merge.30
  153.4 0.0 collective-permute-done.58
  153.7 0.0 copy-start.50
  153.7 1.6 collective-permute-done.69.refs_3_
  155.3 0.0 collective-permute-done.68.refs_1_
  155.3 0.0 collective-permute-start.71
  155.3 4.1 %collective-permute-start.70 = (bf16[128,512]{1,0:T(8,128)(2,1)S(1)}, bf16[128,512]{1,0:T(8,128)(2,1)S(1)}, u32[]{:S(2)}, u32[]{:S(2)}) collective-permute-start(bf16[128,512]{1,0:T(8,128)(2,1)S(1)} %get-tuple-element.1027), channel_id=1, source_target_pairs={{28,0},{0,4},{4,8},{8,12},{12,16},{16,20},{20,24},{24,28},{29,1},{... | collective-permute-start | bytes 393224 | tf_op jit(solution)/shard_map/ppermute | solution.py:21
  159.3 3.6 %grad_up_late.1 = f32[128,5120]{1,0:T(8,128)S(1)} custom-call(s32[24]{0:T(128)S(1)} %get-tuple-element.1003.plan_ref, f32[128,5120]{1,0:T(8,128)S(1)} %get-tuple-element.1037.so_far_ref, bf16[32,5120]{1,0:T(8,128)(2,1)} %get-tuple-element.1038.late_ref, bf16[256,128]{1,0:T(8,128)(2,1)} %get-tuple-element.1012.low2_ref), custom_call_target="tpu_custom_call", output_to_operand_aliasing={{}: (1, {})} | custom-call | tf_op jit(solution)/shard_map/grad_up_late/pallas_call | solution.py:477
  163.0 0.0 copy-start.49
  163.0 1.5 join.2
  164.5 0.0 collective-permute-done.71.refs_3_
  164.5 0.0 collective-permute-done.70.refs_2_
  164.5 0.8 join.3
  (22 shorter events, 0.0 us)
Async XLA Ops:
  1.4 0.7 copy-start
  2.1 7.2 %copy-start.1 = (bf16[1,1,128,5120]{3,2,1,0:T(8,128)(2,1)S(1)}, bf16[1,1,128,5120]{3,2,1,0:T(8,128)(2,1)}, u32[]{:S(2)}) copy-start(bf16[1,1,128,5120]{3,2,1,0:T(8,128)(2,1)} %param.26) | copy-start | bytes 3932164
  2.1 7.2 %copy-start.14 = (bf16[1,1,128,5120]{3,2,1,0:T(8,128)(2,1)S(1)}, bf16[1,1,128,5120]{3,2,1,0:T(8,128)(2,1)}, u32[]{:S(2)}) copy-start(bf16[1,1,128,5120]{3,2,1,0:T(8,128)(2,1)} %param.25) | copy-start | bytes 3932164
  2.1 7.2 %copy-start.27 = (bf16[1,5120,128]{2,1,0:T(8,128)(2,1)S(1)}, bf16[1,5120,128]{2,1,0:T(8,128)(2,1)}, u32[]{:S(2)}) copy-start(bf16[1,5120,128]{2,1,0:T(8,128)(2,1)} %param.28) | copy-start | bytes 3932164
  2.1 7.2 %copy-start.34 = (bf16[1,128,5120]{2,1,0:T(8,128)(2,1)S(1)}, bf16[1,128,5120]{2,1,0:T(8,128)(2,1)}, u32[]{:S(2)}) copy-start(bf16[1,128,5120]{2,1,0:T(8,128)(2,1)} %param.29) | copy-start | bytes 3932164
  2.1 7.2 %copy-start.48 = (f32[1,5120]{1,0:T(1,128)S(1)}, f32[1,5120]{1,0:T(1,128)}, u32[]{:S(2)}) copy-start(f32[1,5120]{1,0:T(1,128)} %g_ref.1) | copy-start | bytes 61444
  9.3 14.5 %collective-permute-start = (bf16[272,1024]{1,0:T(8,128)(2,1)S(1)}, bf16[272,1024]{1,0:T(8,128)(2,1)S(1)}, u32[]{:S(2)}, u32[]{:S(2)}) collective-permute-start(bf16[272,1024]{1,0:T(8,128)(2,1)S(1)} %get-tuple-element.481), channel_id=1, source_target_pairs={{0,1},{1,0},{2,3},{3,2},{4,5},{5,4},{6,7},{7,6},{8,9},{9,8},{10,11... | collective-permute-start | bytes 1671176 | tf_op jit(solution)/shard_map/cond/branch_0_fun/ppermute | solution.py:26
  11.5 30.7 %collective-permute-start.1 = (bf16[224,1024]{1,0:T(8,128)(2,1)S(1)}, bf16[224,1024]{1,0:T(8,128)(2,1)}, u32[]{:S(2)}, u32[]{:S(2)}) collective-permute-start(bf16[224,1024]{1,0:T(8,128)(2,1)S(1)} %get-tuple-element.519), channel_id=1, source_target_pairs={{0,1},{1,0},{2,3},{3,2},{4,5},{5,4},{6,7},{7,6},{8,9},{9,8},{10,11... | collective-permute-start | bytes 1376264 | tf_op jit(solution)/shard_map/cond/branch_0_fun/ppermute | solution.py:26
  23.9 3.6 %copy-start.41 = (bf16[272,1024]{1,0:T(8,128)(2,1)}, bf16[272,1024]{1,0:T(8,128)(2,1)S(1)}, u32[]{:S(2)}) copy-start(bf16[272,1024]{1,0:T(8,128)(2,1)S(1)} %collective-permute-done.got_ref) | copy-start | bytes 1671172 | tf_op jit(solution)/shard_map/cond
  23.9 48.4 %collective-permute-start.4 = (bf16[224,1536]{1,0:T(8,128)(2,1)S(1)}, bf16[224,1536]{1,0:T(8,128)(2,1)}, u32[]{:S(2)}, u32[]{:S(2)}) collective-permute-start(bf16[224,1536]{1,0:T(8,128)(2,1)S(1)} %get-tuple-element.530), channel_id=1, source_target_pairs={{0,1},{1,0},{2,3},{3,2},{4,5},{5,4},{6,7},{7,6},{8,9},{9,8},{10,11... | collective-permute-start | bytes 2064392 | tf_op jit(solution)/shard_map/cond/branch_0_fun/ppermute | solution.py:26
  27.5 28.4 %collective-permute-start.2 = (bf16[192,1024]{1,0:T(8,128)(2,1)S(1)}, bf16[192,1024]{1,0:T(8,128)(2,1)S(1)}, u32[]{:S(2)}, u32[]{:S(2)}) collective-permute-start(bf16[192,1024]{1,0:T(8,128)(2,1)S(1)} %get-tuple-element.517), channel_id=1, source_target_pairs={{0,2},{1,3},{2,0},{3,1},{4,6},{5,7},{6,4},{7,5},{8,10},{9,11},{10,... | collective-permute-start | bytes 1179656 | tf_op jit(solution)/shard_map/cond/branch_0_fun/ppermute | solution.py:26
  44.1 26.5 %collective-permute-start.3 = (bf16[192,1024]{1,0:T(8,128)(2,1)S(1)}, bf16[192,1024]{1,0:T(8,128)(2,1)S(1)}, u32[]{:S(2)}, u32[]{:S(2)}) collective-permute-start(bf16[192,1024]{1,0:T(8,128)(2,1)S(1)} %get-tuple-element.520), channel_id=1, source_target_pairs={{0,2},{1,3},{2,0},{3,1},{4,6},{5,7},{6,4},{7,5},{8,10},{9,11},{10,... | collective-permute-start | bytes 1179656 | tf_op jit(solution)/shard_map/cond/branch_0_fun/ppermute | solution.py:26
  72.3 58.8 %collective-permute-start.66 = (bf16[128,2048]{1,0:T(8,128)(2,1)}, bf16[128,2048]{1,0:T(8,128)(2,1)S(1)}, u32[]{:S(2)}, u32[]{:S(2)}) collective-permute-start(bf16[128,2048]{1,0:T(8,128)(2,1)} %get-tuple-element.1010), channel_id=1, source_target_pairs={{28,0},{0,4},{4,8},{8,12},{12,16},{16,20},{20,24},{24,28},{29,1},{... | collective-permute-start | bytes 1572872 | tf_op jit(solution)/shard_map/ppermute | solution.py:21
  95.1 36.0 %collective-permute-start.67 = (bf16[128,2048]{1,0:T(8,128)(2,1)}, bf16[128,2048]{1,0:T(8,128)(2,1)S(1)}, u32[]{:S(2)}, u32[]{:S(2)}) collective-permute-start(bf16[128,2048]{1,0:T(8,128)(2,1)} %get-tuple-element.1023), channel_id=1, source_target_pairs={{4,0},{8,4},{12,8},{16,12},{20,16},{24,20},{28,24},{0,28},{5,1},{9... | collective-permute-start | bytes 1572872 | tf_op jit(solution)/shard_map/ppermute | solution.py:21
  95.1 44.9 %copy-start.47 = (bf16[272,1024]{1,0:T(8,128)(2,1)S(1)}, bf16[272,1024]{1,0:T(8,128)(2,1)}, u32[]{:S(2)}) copy-start(bf16[272,1024]{1,0:T(8,128)(2,1)} %get-tuple-element.1018) | copy-start | bytes 1671172
  95.1 15.3 %collective-permute-start.33 = (bf16[224,1024]{1,0:T(8,128)(2,1)}, bf16[224,1024]{1,0:T(8,128)(2,1)}, u32[]{:S(2)}, u32[]{:S(2)}) collective-permute-start(bf16[224,1024]{1,0:T(8,128)(2,1)} %get-tuple-element.675), channel_id=1, source_target_pairs={{0,1},{1,0},{2,3},{3,2},{4,5},{5,4},{6,7},{7,6},{8,9},{9,8},{10,11... | collective-permute-start | bytes 1376264 | tf_op jit(solution)/shard_map/cond/branch_0_fun/ppermute | solution.py:26
  95.1 15.3 %copy-start.2 = (bf16[128,5120]{1,0:T(8,128)(2,1)S(1)}, bf16[128,5120]{1,0:T(8,128)(2,1)}, u32[]{:S(2)}) copy-start(bf16[128,5120]{1,0:T(8,128)(2,1)} %get-tuple-element.664.dy_ref) | copy-start | bytes 3932164 | tf_op jit(solution)/shard_map/cond
  95.1 15.3 %copy-start.15 = (bf16[128,5120]{1,0:T(8,128)(2,1)S(1)}, bf16[128,5120]{1,0:T(8,128)(2,1)}, u32[]{:S(2)}) copy-start(bf16[128,5120]{1,0:T(8,128)(2,1)} %get-tuple-element.663.x_ref) | copy-start | bytes 3932164 | tf_op jit(solution)/shard_map/cond
  95.1 15.3 %copy-start.28 = (bf16[5120,128]{1,0:T(8,128)(2,1)S(1)}, bf16[5120,128]{1,0:T(8,128)(2,1)}, u32[]{:S(2)}) copy-start(bf16[5120,128]{1,0:T(8,128)(2,1)} %get-tuple-element.671.down_ref) | copy-start | bytes 3932164 | tf_op jit(solution)/shard_map/cond
  95.2 15.3 %copy-start.35 = (bf16[128,5120]{1,0:T(8,128)(2,1)S(1)}, bf16[128,5120]{1,0:T(8,128)(2,1)}, u32[]{:S(2)}) copy-start(bf16[128,5120]{1,0:T(8,128)(2,1)} %get-tuple-element.670.up_ref) | copy-start | bytes 3932164 | tf_op jit(solution)/shard_map/cond
  99.0 26.0 %collective-permute-start.34 = (bf16[192,1536]{1,0:T(8,128)(2,1)S(1)}, bf16[192,1536]{1,0:T(8,128)(2,1)S(1)}, u32[]{:S(2)}, u32[]{:S(2)}) collective-permute-start(bf16[192,1536]{1,0:T(8,128)(2,1)S(1)} %get-tuple-element.673), channel_id=1, source_target_pairs={{0,2},{1,3},{2,0},{3,1},{4,6},{5,7},{6,4},{7,5},{8,10},{9,11},{10,... | collective-permute-start | bytes 1769480 | tf_op jit(solution)/shard_map/cond/branch_0_fun/ppermute | solution.py:26
  112.4 16.9 %collective-permute-start.35 = (bf16[192,1024]{1,0:T(8,128)(2,1)S(1)}, bf16[192,1024]{1,0:T(8,128)(2,1)S(1)}, u32[]{:S(2)}, u32[]{:S(2)}) collective-permute-start(bf16[192,1024]{1,0:T(8,128)(2,1)S(1)} %get-tuple-element.676), channel_id=1, source_target_pairs={{0,2},{1,3},{2,0},{3,1},{4,6},{5,7},{6,4},{7,5},{8,10},{9,11},{10,... | collective-permute-start | bytes 1179656 | tf_op jit(solution)/shard_map/cond/branch_0_fun/ppermute | solution.py:26
  114.1 16.9 %collective-permute-start.36 = (bf16[224,512]{1,0:T(8,128)(2,1)S(1)}, bf16[224,512]{1,0:T(8,128)(2,1)}, u32[]{:S(2)}, u32[]{:S(2)}) collective-permute-start(bf16[224,512]{1,0:T(8,128)(2,1)S(1)} %get-tuple-element.685), channel_id=1, source_target_pairs={{0,1},{1,0},{2,3},{3,2},{4,5},{5,4},{6,7},{7,6},{8,9},{9,8},{10,11... | collective-permute-start | bytes 688136 | tf_op jit(solution)/shard_map/cond/branch_0_fun/ppermute | solution.py:26
  131.1 24.2 %collective-permute-start.69 = (bf16[128,2560]{1,0:T(8,128)(2,1)}, bf16[128,2560]{1,0:T(8,128)(2,1)S(1)}, u32[]{:S(2)}, u32[]{:S(2)}) collective-permute-start(bf16[128,2560]{1,0:T(8,128)(2,1)} %get-tuple-element.1026), channel_id=1, source_target_pairs={{4,0},{8,4},{12,8},{16,12},{20,16},{24,20},{28,24},{0,28},{5,1},{9... | collective-permute-start | bytes 1966088 | tf_op jit(solution)/shard_map/ppermute | solution.py:21
  131.1 24.1 %collective-permute-start.68 = (bf16[128,2560]{1,0:T(8,128)(2,1)}, bf16[128,2560]{1,0:T(8,128)(2,1)S(1)}, u32[]{:S(2)}, u32[]{:S(2)}) collective-permute-start(bf16[128,2560]{1,0:T(8,128)(2,1)} %get-tuple-element.1024), channel_id=1, source_target_pairs={{28,0},{0,4},{4,8},{8,12},{12,16},{16,20},{20,24},{24,28},{29,1},{... | collective-permute-start | bytes 1966088 | tf_op jit(solution)/shard_map/ppermute | solution.py:21
  140.0 13.4 %collective-permute-start.58 = (bf16[32,5120]{1,0:T(8,128)(2,1)}, bf16[32,5120]{1,0:T(8,128)(2,1)}, u32[]{:S(2)}, u32[]{:S(2)}) collective-permute-start(bf16[32,5120]{1,0:T(8,128)(2,1)} %get-tuple-element.833), channel_id=1, source_target_pairs={{0,1},{1,0},{2,3},{3,2},{4,5},{5,4},{6,7},{7,6},{8,9},{9,8},{10,11... | collective-permute-start | bytes 983048 | tf_op jit(solution)/shard_map/cond/branch_0_fun/ppermute | solution.py:26
  140.0 7.2 %copy-start.8 = (bf16[128,5120]{1,0:T(8,128)(2,1)S(1)}, bf16[128,5120]{1,0:T(8,128)(2,1)}, u32[]{:S(2)}) copy-start(bf16[128,5120]{1,0:T(8,128)(2,1)} %get-tuple-element.817.dy_ref) | copy-start | bytes 3932164 | tf_op jit(solution)/shard_map/cond
  141.8 10.6 %collective-permute-start.57 = (bf16[192,512]{1,0:T(8,128)(2,1)S(1)}, bf16[192,512]{1,0:T(8,128)(2,1)S(1)}, u32[]{:S(2)}, u32[]{:S(2)}) collective-permute-start(bf16[192,512]{1,0:T(8,128)(2,1)S(1)} %get-tuple-element.826), channel_id=1, source_target_pairs={{0,2},{1,3},{2,0},{3,1},{4,6},{5,7},{6,4},{7,5},{8,10},{9,11},{10,... | collective-permute-start | bytes 589832 | tf_op jit(solution)/shard_map/cond/branch_0_fun/ppermute | solution.py:26
  147.2 2.6 %copy-start.21 = (bf16[128,5120]{1,0:T(8,128)(2,1)S(1)}, bf16[128,5120]{1,0:T(8,128)(2,1)}, u32[]{:S(2)}) copy-start(bf16[128,5120]{1,0:T(8,128)(2,1)} %get-tuple-element.838.x_ref) | copy-start | bytes 3932164 | tf_op jit(solution)/shard_map/cond
  153.7 9.3 %copy-start.50 = (f32[1,1,5120,128]{3,2,1,0:T(8,128)}, f32[1,1,5120,128]{3,2,1,0:T(8,128)S(1)}, u32[]{:S(2)}) copy-start(f32[1,1,5120,128]{3,2,1,0:T(8,128)S(1)} %get-tuple-element.1000) | copy-start | bytes 7864324
  155.3 9.2 %collective-permute-start.71 = (bf16[128,512]{1,0:T(8,128)(2,1)S(1)}, bf16[128,512]{1,0:T(8,128)(2,1)S(1)}, u32[]{:S(2)}, u32[]{:S(2)}) collective-permute-start(bf16[128,512]{1,0:T(8,128)(2,1)S(1)} %get-tuple-element.1029), channel_id=1, source_target_pairs={{4,0},{8,4},{12,8},{16,12},{20,16},{24,20},{28,24},{0,28},{5,1},{9... | collective-permute-start | bytes 393224 | tf_op jit(solution)/shard_map/ppermute | solution.py:21
  155.3 9.2 %collective-permute-start.70 = (bf16[128,512]{1,0:T(8,128)(2,1)S(1)}, bf16[128,512]{1,0:T(8,128)(2,1)S(1)}, u32[]{:S(2)}, u32[]{:S(2)}) collective-permute-start(bf16[128,512]{1,0:T(8,128)(2,1)S(1)} %get-tuple-element.1027), channel_id=1, source_target_pairs={{28,0},{0,4},{4,8},{8,12},{12,16},{16,20},{20,24},{24,28},{29,1},{... | collective-permute-start | bytes 393224 | tf_op jit(solution)/shard_map/ppermute | solution.py:21
  163.0 2.3 %copy-start.49 = (f32[128,5120]{1,0:T(8,128)}, f32[128,5120]{1,0:T(8,128)S(1)}, u32[]{:S(2)}) copy-start(f32[128,5120]{1,0:T(8,128)S(1)} %grad_up_late.1) | copy-start | bytes 7864324

commit v2 on v1

--- a/solution.py
+++ b/solution.py
@@ -9,9 +9,9 @@
 
 CAP = 2
 TILE = 512
-CHUNKS = (2, 2, 3, 2, 1)
+CHUNKS = (2, 2, 2, 2, 2)
 STAGES = (((0, 1, 2), (0, 1)), ((3, 4), (2, 3)), ((), (4,)))
-DEPTH, LAG = 2, 3
+DEPTH, LAG = 1, 2
 F32, BF16 = jnp.float32, jnp.bfloat16
 
 
@@ -432,59 +432,73 @@
     )(x, low, low2, high, high2, g, *got)
 
 
-def turned_act(plan_ref, low2_ref, j, blk):
-    at = pl.ds(pl.multiple_of(plan_ref[20 + j] * blk, blk), blk)
-    return (low2_ref[at, :].astype(F32) * 0.5).T.astype(BF16)
-
-
-def grad_up_kernel(plan_ref, dy_ref, low_ref, low2_ref, *refs):
-    got_refs, to_ref = refs[:-1], refs[-1]
+def last_kernel(places, starts, plan_ref, low_ref, low2_ref, dy_ref, late_ref, *refs):
+    chunks, count = len(starts) - 1, len(places)
+    got_refs = refs[:chunks]
+    parts = refs[chunks : chunks + 2 * count]
+    to_ref, next_ref, return_ref = refs[chunks + 2 * count : chunks + 2 * count + 3]
+    dy_scr, other_scr, to_scr, part_sems, in_sems, out_sems = refs[chunks + 2 * count + 3 :]
     rows = dy_ref.shape[0]
     blk = rows // 4
+    loads, stores = [], []
+    for c, got_ref in enumerate(got_refs):
+        at = slice(starts[c], starts[c + 1])
+        pairs = (
+            (dy_ref.at[:, at], dy_scr.at[:, at]),
+            (got_ref.at[pl.ds(rows, 3 * blk), :], other_scr.at[pl.ds(0, 3 * blk), at]),
+            (late_ref.at[:, at], other_scr.at[pl.ds(3 * blk, blk), at]),
+        )
+        loads.append([pltpu.make_async_copy(x, y, in_sems.at[3 * c + n]) for n, (x, y) in enumerate(pairs)])
+        stores.append(pltpu.make_async_copy(to_scr.at[:, at], to_ref.at[:, at], out_sems.at[c]))
+    for some in loads:
+        for copy in some:
+            copy.start()
+    joins = []
+    for n, out_ref in enumerate((next_ref, return_ref)):
+        for i, (first, cols) in enumerate(places):
+            sem = part_sems.at[n * count + i]
+            joins.append(pltpu.make_async_copy(parts[n * count + i], out_ref.at[:, pl.ds(first, cols)], sem))
+    for copy in joins:
+        copy.start()
     own = (low_ref[:rows, :].astype(F32) * 0.5).T.astype(BF16)
-    other = jnp.concatenate([turned_act(plan_ref, low2_ref, j, blk) for j in range(3)], axis=1)
+    ats = [pl.ds(pl.multiple_of(plan_ref[20 + j] * blk, blk), blk) for j in range(4)]
+    other = jnp.concatenate([(low2_ref[at, :].astype(F32) * 0.5).T.astype(BF16) for at in ats], axis=1)
+    for c, some in enumerate(loads):
+        for copy in some:
+            copy.wait()
+        at = slice(starts[c], starts[c + 1])
+        to_scr[:, at] = dot(own, dy_scr[:, at], ((1,), (0,))) + dot(other, other_scr[:, at], ((1,), (0,)))
+        stores[c].start()
+    for copy in joins + stores:
+        copy.wait()
+
+
+def make_last(plan, dy, late, got, low, low2, nexts, returns):
+    rows, width = dy.shape
+    rank = low.shape[1]
+    starts, places = [0], []
+    for block in got:
+        starts.append(starts[-1] + block.shape[1])
     first = 0
-    for got_ref in got_refs:
-        at = slice(first, first + got_ref.shape[1])
-        first = at.stop
-        to_ref[:, at] = dot(own, dy_ref[:, at], ((1,), (0,))) + dot(
-            other, got_ref[rows : rows + 3 * blk, :], ((1,), (0,))
-        )
-
-
-def make_grad_up(plan, dy, got, low, low2):
+    for part in nexts:
+        places.append((first, part.shape[1]))
+        first += part.shape[1]
+    hbm = pl.BlockSpec(memory_space=pl.ANY)
+    routed = jax.ShapeDtypeStruct((rows, width), BF16)
     return pl.pallas_call(
-        grad_up_kernel,
-        out_shape=jax.ShapeDtypeStruct((low.shape[1], dy.shape[1]), F32),
-        in_specs=[SMEM] + [VMEM] * (3 + len(got)),
-        out_specs=VMEM,
+        functools.partial(last_kernel, tuple(places), tuple(starts)),
+        out_shape=(jax.ShapeDtypeStruct((rank, width), F32), routed, routed),
+        in_specs=[SMEM, VMEM, VMEM] + [hbm] * (2 + len(got) + 2 * len(nexts)),
+        out_specs=(hbm,) * 3,
+        scratch_shapes=[
+            pltpu.VMEM((rows, width), BF16), pltpu.VMEM((rows, width), BF16), pltpu.VMEM((rank, width), F32),
+            pltpu.SemaphoreType.DMA((2 * len(nexts),)), pltpu.SemaphoreType.DMA((3 * len(got),)),
+            pltpu.SemaphoreType.DMA((len(got),)),
+        ],
         compiler_params=ROOM,
         cost_estimate=FREE,
-        name="grad_up",
-    )(plan, dy, low, low2, *got)
-
-
-def grad_up_late_kernel(plan_ref, so_far_ref, late_ref, low2_ref, to_ref):
-    blk = late_ref.shape[0]
-    act = turned_act(plan_ref, low2_ref, 3, blk)
-    to_ref[...] = so_far_ref[...] + dot(act, late_ref[...], ((1,), (0,)))
-
-
-def make_grad_up_late(plan, so_far, late, low2):
-    rank, width = so_far.shape
-    blk = late.shape[0]
-    tile = 2 * TILE
-    return pl.pallas_call(
-        grad_up_late_kernel,
-        grid=(width // tile,),
-        out_shape=jax.ShapeDtypeStruct((rank, width), F32),
-        in_specs=[SMEM, column(rank, 0, tile), column(blk, 0, tile), whole(low2.shape)],
-        out_specs=column(rank, 0, tile),
-        input_output_aliases={1: 0},
-        compiler_params=ROOM,
-        cost_estimate=FREE,
-        name="grad_up_late",
-    )(plan, so_far, late, low2)
+        name="last",
+    )(plan, low, low2, dy, late, *got, *nexts, *returns)
 
 
 def four_peers(inputs, out_grad, gains, down_proj, up_proj, wiring, pair_mask):
@@ -532,8 +546,7 @@
             late2 = swapped(after(late, held[count - 1]), "peer", mask)
         if number == len(STAGES) - 1:
             blocks = [held[c] for c in range(count)]
-            up_grad = make_grad_up(after(plan, sent), dy, blocks, low, low2)
-            grads = up_grad, make_grad_down(after(x, up_grad), blocks, *common, gains)
+            grads = make_grad_down(after(x, sent), blocks, *common, gains)
         merged = make_merge(cap, after(plan, sent), parts)
         return merged, (low2, high2) if number == 0 else (), late2, {c: held[c] for c in exchange}, grads
 
@@ -541,7 +554,7 @@
     nexts, returns = [], []
     for number in range(len(STAGES)):
         branches = [functools.partial(stage, number, cap, m) for cap in (3, 4) for m in (1, 2, 3)]
-        (f, b), made, late2, arrived, grads = lax.switch(choice, branches, state)
+        (f, b), made, late2, arrived, grad_down = lax.switch(choice, branches, state)
         if number == 0:
             low2, high2 = made
             held = {}
@@ -551,9 +564,9 @@
             f, b = after(f, nexts[-1], returns[-1]), after(b, nexts[-1], returns[-1])
         nexts.append(passed_along(f, "section", 1))
         returns.append(passed_along(b, "section", -1))
-    so_far, grad_down = grads
-    grad_up = make_grad_up_late(plan, after(so_far, f, b), late2, low2)
-    joined = make_join(width, 0, [after(nexts[0], f, b), *nexts[1:-1]], returns[:-1])
+    grad_up, *joined = make_last(
+        plan, after(dy, f, b), late2, [held[c] for c in range(count)], low, low2, nexts[:-1], returns[:-1]
+    )
     done = sum(part.shape[1] for part in nexts[:-1])
     next_rows, return_rows = make_join(width, done, nexts[-1:], returns[-1:], into=joined)
     return next_rows[None, None], return_rows[None, None], grad_down[None, None], grad_up[None, None]

time: 168 us -> 169 us (level)
  the two profiles are of different devices: /device:TPU:1 before, /device:TPU:0 now
where the time goes in v2:
time: 169 us; the launch traced here: 168 us
  waiting for transfers between devices  86.6 us (51%)
  starting transfers between devices  45.2 us (27%)
  Pallas kernels  31 us (18%)
  local copies, waits for them, and re-layouts  3.23 us (2%)
    ppermute x11, waiting for transfers between devices, swapped(): lax.ppermute(block, axis, [(i, i ^ mask) for i in range(count) if i ^ mas...  82.8 us
    ppermute x6, starting transfers between devices, passed_along(): return lax.ppermute(block, axis, route)  23.8 us
    ppermute x11, starting transfers between devices, swapped(): lax.ppermute(block, axis, [(i, i ^ mask) for i in range(count) if i ^ mas...  21.4 us
    pallas_call x5, Pallas kernels, make_rows(): pl.pallas_call(functools.partial(rows_kernel, cap, blk), grid=(tiles,), o...  10.1 us
    pallas_call x1, Pallas kernels, make_open(): pl.pallas_call(functools.partial(open_kernel, widths), out_shape=[jax.Sha...  6 us
    pallas_call x1, Pallas kernels, make_last(): pl.pallas_call(functools.partial(last_kernel, tuple(places), tuple(starts...  5.06 us
    pallas_call x3, Pallas kernels, make_merge(): pl.pallas_call(functools.partial(merge_kernel, cap, rows // 4, tuple(span...  4.66 us
    ppermute x6, waiting for transfers between devices, passed_along(): return lax.ppermute(block, axis, route)  3.8 us
  transfers between devices with their start and end apart: 17, of which 11 were waited for; matrix products, arithmetic and copies ran while one was open for 1% of the time, Pallas kernels for 14%

profile of v2, /device:TPU:0, one launch (start us, length us, event | category | flops | bytes accessed | tf_op | source)
XLA Modules:
  0.0 167.8 jit_solution(11658067814887176220)
XLA Ops:
  0.6 0.8 copy.13.wiring_ref
  1.4 0.7 copy-done
  2.1 0.0 copy-start.23
  2.1 6.0 %open.1 = (s32[24]{0:T(128)S(1)}, s32[1]{0:T(128)}, bf16[256,128]{1,0:T(8,128)(2,1)S(1)}, f32[8,128]{1,0:T(8,128)S(1)}, bf16[272,1024]{1,0:T(8,128)(2,1)S(1)}, /...) custom-call(s32[8,4,4]{2,1,0:T(4,128)S(1)} %copy.13.wiring_ref, ...), custom_call_target="tpu_custom_call" | custom-call | tf_op jit(solution)/shard_map/open/pallas_call | solution.py:198
  8.8 0.0 copy-done.1
  8.8 0.0 copy-done.2
  8.8 0.0 copy-done.9
  8.8 0.0 copy-done.16
  8.8 0.0 copy-done.23
  8.8 59.5 %conditional.3 = (bf16[128,2048]{1,0:T(8,128)(2,1)}, bf16[128,2048]{1,0:T(8,128)(2,1)}, bf16[256,128]{1,0:T(8,128)(2,1)}, f32[8,128]{1,0:T(8,128)}, bf16[32,5120...) conditional(s32[]{:T(128)} %bitcast.10, (s32[24]{0:T(128)S(1)}, ...), branch_computations={%region_0.0_spmd, %region_1.0_spmd, %region_2.0_spmd, %region_3.0_... | conditional | bytes 11403568 | solution.py:557
  8.8 4.1 %collective-permute-start.5 = (bf16[272,1024]{1,0:T(8,128)(2,1)S(1)}, bf16[272,1024]{1,0:T(8,128)(2,1)}, u32[]{:S(2)}, u32[]{:S(2)}) collective-permute-start(bf16[272,1024]{1,0:T(8,128)(2,1)S(1)} %get-tuple-element.530), channel_id=1, source_target_pairs={{0,2},{1,3},{2,0},{3,1},{4,6},{5,7},{6,4},{7,5},{8,10},{9,11},{10,... | collective-permute-start | bytes 1671176 | tf_op jit(solution)/shard_map/cond/branch_1_fun/ppermute | solution.py:26
  12.9 12.3 %collective-permute-done.5.got_ref = bf16[272,1024]{1,0:T(8,128)(2,1)} collective-permute-done((bf16[272,1024]{1,0:T(8,128)(2,1)S(1)}, bf16[272,1024]{1,0:T(8,128)(2,1)}, u32[]{:S(2)}, u32[]{:S(2)}) %collective-permute-start.5) | collective-permute-done | bytes 557088 | tf_op jit(solution)/shard_map/cond/branch_1_fun/ppermute | solution.py:26
  25.3 2.1 %collective-permute-start.6 = (bf16[224,1024]{1,0:T(8,128)(2,1)S(1)}, bf16[224,1024]{1,0:T(8,128)(2,1)}, u32[]{:S(2)}, u32[]{:S(2)}) collective-permute-start(bf16[224,1024]{1,0:T(8,128)(2,1)S(1)} %get-tuple-element.541), channel_id=1, source_target_pairs={{0,2},{1,3},{2,0},{3,1},{4,6},{5,7},{6,4},{7,5},{8,10},{9,11},{10,... | collective-permute-start | bytes 1376264 | tf_op jit(solution)/shard_map/cond/branch_1_fun/ppermute | solution.py:26
  27.4 1.7 %unpack.7 = (bf16[256,128]{1,0:T(8,128)(2,1)}, f32[8,128]{1,0:T(8,128)}) custom-call(bf16[272,1024]{1,0:T(8,128)(2,1)} %collective-permute-done.5.got_ref), custom_call_target="tpu_custom_call" | custom-call | tf_op jit(solution)/shard_map/cond/branch_1_fun/unpack/pallas_call | solution.py:236
  29.1 1.9 %rows.32 = (bf16[192,1024]{1,0:T(8,128)(2,1)S(1)}, bf16[128,1024]{1,0:T(8,128)(2,1)S(1)}, bf16[128,1024]{1,0:T(8,128)(2,1)S(1)}) custom-call(s32[24]{0:T(128)S(1)} %get-tuple-element.543.plan_ref, bf16[128,5120]{1,0:T(8,128)(2,1)S(1)} %get-tuple-element.528.x_ref, bf16[128,5120]{1,0:T(8,128)(2,1)S(1)} %get-tuple-element.529.dy_ref, ...), custom_call_target="tpu_custom_call" | custom-call | tf_op jit(solution)/shard_map/cond/branch_1_fun/rows/pallas_call | solution.py:298
  31.0 3.8 %collective-permute-start.7 = (bf16[192,1024]{1,0:T(8,128)(2,1)S(1)}, bf16[192,1024]{1,0:T(8,128)(2,1)S(1)}, u32[]{:S(2)}, u32[]{:S(2)}) collective-permute-start(bf16[192,1024]{1,0:T(8,128)(2,1)S(1)} %get-tuple-element.538), channel_id=1, source_target_pairs={{0,1},{1,0},{2,3},{3,2},{4,5},{5,4},{6,7},{7,6},{8,9},{9,8},{10,11... | collective-permute-start | bytes 1179656 | tf_op jit(solution)/shard_map/cond/branch_1_fun/ppermute | solution.py:26
  34.7 8.1 %collective-permute-done.7.refs_2_ = bf16[192,1024]{1,0:T(8,128)(2,1)S(1)} collective-permute-done((bf16[192,1024]{1,0:T(8,128)(2,1)S(1)}, bf16[192,1024]{1,0:T(8,128)(2,1)S(1)}, u32[]{:S(2)}, u32[]{:S(2)}) %collective-permute-start.7) | collective-permute-done | bytes 393248 | tf_op jit(solution)/shard_map/cond/branch_1_fun/ppermute | solution.py:26
  42.8 4.4 %collective-permute-done.6.got_ref = bf16[224,1024]{1,0:T(8,128)(2,1)} collective-permute-done((bf16[224,1024]{1,0:T(8,128)(2,1)S(1)}, bf16[224,1024]{1,0:T(8,128)(2,1)}, u32[]{:S(2)}, u32[]{:S(2)}) %collective-permute-start.6) | collective-permute-done | bytes 458784 | tf_op jit(solution)/shard_map/cond/branch_1_fun/ppermute | solution.py:26
  47.3 0.1 collective-permute-start.9
  47.4 1.9 %rows.33 = (bf16[192,1024]{1,0:T(8,128)(2,1)S(1)}, bf16[128,1024]{1,0:T(8,128)(2,1)S(1)}, bf16[128,1024]{1,0:T(8,128)(2,1)S(1)}) custom-call(s32[24]{0:T(128)S(1)} %get-tuple-element.543.plan_ref, bf16[128,5120]{1,0:T(8,128)(2,1)S(1)} %get-tuple-element.528.x_ref, bf16[128,5120]{1,0:T(8,128)(2,1)S(1)} %get-tuple-element.529.dy_ref, ...), custom_call_target="tpu_custom_call" | custom-call | tf_op jit(solution)/shard_map/cond/branch_1_fun/rows/pallas_call | solution.py:298
  49.3 5.3 %collective-permute-start.8 = (bf16[192,1024]{1,0:T(8,128)(2,1)S(1)}, bf16[192,1024]{1,0:T(8,128)(2,1)S(1)}, u32[]{:S(2)}, u32[]{:S(2)}) collective-permute-start(bf16[192,1024]{1,0:T(8,128)(2,1)S(1)} %get-tuple-element.542), channel_id=1, source_target_pairs={{0,1},{1,0},{2,3},{3,2},{4,5},{5,4},{6,7},{7,6},{8,9},{9,8},{10,11... | collective-permute-start | bytes 1179656 | tf_op jit(solution)/shard_map/cond/branch_1_fun/ppermute | solution.py:26
  54.6 1.7 %copy.26 = bf16[32,5120]{1,0:T(8,128)(2,1)} copy(bf16[32,5120]{1,0:T(8,128)(2,1)} %get-tuple-element.1055) | data formatting | bytes 655360 | tf_op jit(solution)/shard_map/cond
  56.3 10.3 %collective-permute-done.8.refs_5_ = bf16[192,1024]{1,0:T(8,128)(2,1)S(1)} collective-permute-done((bf16[192,1024]{1,0:T(8,128)(2,1)S(1)}, bf16[192,1024]{1,0:T(8,128)(2,1)S(1)}, u32[]{:S(2)}, u32[]{:S(2)}) %collective-permute-start.8) | collective-permute-done | bytes 393248 | tf_op jit(solution)/shard_map/cond/branch_1_fun/ppermute | solution.py:26
  66.7 1.6 merge.19
  68.3 0.0 collective-permute-done.9
  68.3 3.3 %collective-permute-start.66 = (bf16[128,2048]{1,0:T(8,128)(2,1)}, bf16[128,2048]{1,0:T(8,128)(2,1)S(1)}, u32[]{:S(2)}, u32[]{:S(2)}) collective-permute-start(bf16[128,2048]{1,0:T(8,128)(2,1)} %get-tuple-element.1027), channel_id=1, source_target_pairs={{28,0},{0,4},{4,8},{8,12},{12,16},{16,20},{20,24},{24,28},{29,1},{... | collective-permute-start | bytes 1572872 | tf_op jit(solution)/shard_map/ppermute | solution.py:21
  71.6 16.8 %collective-permute-start.67 = (bf16[128,2048]{1,0:T(8,128)(2,1)}, bf16[128,2048]{1,0:T(8,128)(2,1)S(1)}, u32[]{:S(2)}, u32[]{:S(2)}) collective-permute-start(bf16[128,2048]{1,0:T(8,128)(2,1)} %get-tuple-element.1028), channel_id=1, source_target_pairs={{4,0},{8,4},{12,8},{16,12},{20,16},{24,20},{28,24},{0,28},{5,1},{9... | collective-permute-start | bytes 1572872 | tf_op jit(solution)/shard_map/ppermute | solution.py:21
  88.4 43.3 %conditional.4 = (bf16[128,2048]{1,0:T(8,128)(2,1)}, bf16[128,2048]{1,0:T(8,128)(2,1)}, bf16[224,1024]{1,0:T(8,128)(2,1)}, bf16[224,1024]{1,0:T(8,128)(2,1)}) conditional(s32[]{:T(128)} %bitcast.10, (s32[24]{0:T(128)S(1)}, bf16[128,5120]{1,0:T(8,128)(2,1)S(1)}, bf16[128,5120]{1,0:T(8,128)(2,1)}, ...), branch_computations={%region_6.0_spmd, %region_7.0_spmd, %region_8.0_spmd, %region_9.0_... | conditional | bytes 25428272 | solution.py:557
  88.4 0.0 collective-permute-start.37
  88.4 0.0 copy-start.11
  88.4 0.0 copy-start.18
  88.4 2.3 %rows.44 = (bf16[192,1024]{1,0:T(8,128)(2,1)S(1)}, bf16[128,1024]{1,0:T(8,128)(2,1)S(1)}, bf16[128,1024]{1,0:T(8,128)(2,1)S(1)}) custom-call(s32[24]{0:T(128)S(1)} %get-tuple-element.704.plan_ref, bf16[128,5120]{1,0:T(8,128)(2,1)S(1)} %get-tuple-element.689.x_ref, bf16[128,5120]{1,0:T(8,128)(2,1)} %get-tuple-element.690.dy_ref, ...), custom_call_target="tpu_custom_call" | custom-call | tf_op jit(solution)/shard_map/cond/branch_1_fun/rows/pallas_call | solution.py:298
  90.7 1.0 collective-permute-start.38
  91.8 12.6 %collective-permute-done.38.refs_2_ = bf16[192,1024]{1,0:T(8,128)(2,1)S(1)} collective-permute-done((bf16[192,1024]{1,0:T(8,128)(2,1)S(1)}, bf16[192,1024]{1,0:T(8,128)(2,1)S(1)}, u32[]{:S(2)}, u32[]{:S(2)}) %collective-permute-start.38) | collective-permute-done | bytes 393248 | tf_op jit(solution)/shard_map/cond/branch_1_fun/ppermute | solution.py:26
  104.3 5.3 %collective-permute-done.37.got_ref = bf16[224,1024]{1,0:T(8,128)(2,1)} collective-permute-done((bf16[224,1024]{1,0:T(8,128)(2,1)}, bf16[224,1024]{1,0:T(8,128)(2,1)}, u32[]{:S(2)}, u32[]{:S(2)}) %collective-permute-start.37) | collective-permute-done | bytes 458784 | tf_op jit(solution)/shard_map/cond/branch_1_fun/ppermute | solution.py:26
  109.6 0.0 collective-permute-start.40
  109.6 0.0 copy-done.11
  109.6 0.0 copy-done.18
  109.7 1.9 %rows.45 = (bf16[192,1024]{1,0:T(8,128)(2,1)S(1)}, bf16[128,1024]{1,0:T(8,128)(2,1)S(1)}, bf16[128,1024]{1,0:T(8,128)(2,1)S(1)}) custom-call(s32[24]{0:T(128)S(1)} %get-tuple-element.704.plan_ref, bf16[128,5120]{1,0:T(8,128)(2,1)S(1)} %get-tuple-element.689.x_ref, bf16[128,5120]{1,0:T(8,128)(2,1)S(1)} %copy-done.4, ...), custom_call_target="tpu_custom_call" | custom-call | tf_op jit(solution)/shard_map/cond/branch_1_fun/rows/pallas_call | solution.py:298
  111.6 2.5 %collective-permute-start.39 = (bf16[192,1024]{1,0:T(8,128)(2,1)S(1)}, bf16[192,1024]{1,0:T(8,128)(2,1)S(1)}, u32[]{:S(2)}, u32[]{:S(2)}) collective-permute-start(bf16[192,1024]{1,0:T(8,128)(2,1)S(1)} %get-tuple-element.703), channel_id=1, source_target_pairs={{0,1},{1,0},{2,3},{3,2},{4,5},{5,4},{6,7},{7,6},{8,9},{9,8},{10,11... | collective-permute-start | bytes 1179656 | tf_op jit(solution)/shard_map/cond/branch_1_fun/ppermute | solution.py:26
  114.0 12.8 %collective-permute-done.39.refs_5_ = bf16[192,1024]{1,0:T(8,128)(2,1)S(1)} collective-permute-done((bf16[192,1024]{1,0:T(8,128)(2,1)S(1)}, bf16[192,1024]{1,0:T(8,128)(2,1)S(1)}, u32[]{:S(2)}, u32[]{:S(2)}) %collective-permute-start.39) | collective-permute-done | bytes 393248 | tf_op jit(solution)/shard_map/cond/branch_1_fun/ppermute | solution.py:26
  126.8 1.6 merge.25
  128.5 3.3 %collective-permute-done.40 = bf16[224,1024]{1,0:T(8,128)(2,1)} collective-permute-done((bf16[224,1024]{1,0:T(8,128)(2,1)S(1)}, bf16[224,1024]{1,0:T(8,128)(2,1)}, u32[]{:S(2)}, u32[]{:S(2)}) %collective-permute-start.40) | collective-permute-done | bytes 458784 | tf_op jit(solution)/shard_map/cond/branch_1_fun/ppermute | solution.py:26
  131.7 0.0 collective-permute-done.66.refs_5_
  131.7 0.0 collective-permute-done.67.refs_7_
  131.8 3.2 %collective-permute-start.69 = (bf16[128,2048]{1,0:T(8,128)(2,1)}, bf16[128,2048]{1,0:T(8,128)(2,1)S(1)}, u32[]{:S(2)}, u32[]{:S(2)}) collective-permute-start(bf16[128,2048]{1,0:T(8,128)(2,1)} %get-tuple-element.1031), channel_id=1, source_target_pairs={{4,0},{8,4},{12,8},{16,12},{20,16},{24,20},{28,24},{0,28},{5,1},{9... | collective-permute-start | bytes 1572872 | tf_op jit(solution)/shard_map/ppermute | solution.py:21
  134.9 0.0 collective-permute-start.68
  134.9 22.4 %conditional.5 = (bf16[128,1024]{1,0:T(8,128)(2,1)S(1)}, bf16[128,1024]{1,0:T(8,128)(2,1)S(1)}, bf16[32,5120]{1,0:T(8,128)(2,1)}, f32[1,1,5120,128]{3,2,1,0:T(8,128)S(1)}) conditional(s32[]{:T(128)} %bitcast.10, (s32[24]{0:T(128)S(1)}, bf16[128,5120]{1,0:T(8,128)(2,1)S(1)}, bf16[128,5120]{1,0:T(8,128)(2,1)}, ...), branch_computations={%region_12.0_spmd, %region_13.0_spmd, %region_14.0_spmd, %region_1... | conditional | bytes 2883696 | solution.py:557
  134.9 2.1 %rows.55 = (bf16[192,1024]{1,0:T(8,128)(2,1)S(1)}, bf16[128,1024]{1,0:T(8,128)(2,1)S(1)}, bf16[128,1024]{1,0:T(8,128)(2,1)S(1)}) custom-call(s32[24]{0:T(128)S(1)} %get-tuple-element.858.plan_ref, bf16[128,5120]{1,0:T(8,128)(2,1)S(1)} %get-tuple-element.865.x_ref, bf16[128,5120]{1,0:T(8,128)(2,1)} %get-tuple-element.848.dy_ref, ...), custom_call_target="tpu_custom_call" | custom-call | tf_op jit(solution)/shard_map/cond/branch_1_fun/rows/pallas_call | solution.py:298
  137.1 0.1 collective-permute-start.59
  137.1 2.4 %collective-permute-start.60 = (bf16[32,5120]{1,0:T(8,128)(2,1)}, bf16[32,5120]{1,0:T(8,128)(2,1)}, u32[]{:S(2)}, u32[]{:S(2)}) collective-permute-start(bf16[32,5120]{1,0:T(8,128)(2,1)} %get-tuple-element.864), channel_id=1, source_target_pairs={{0,2},{1,3},{2,0},{3,1},{4,6},{5,7},{6,4},{7,5},{8,10},{9,11},{10,... | collective-permute-start | bytes 983048 | tf_op jit(solution)/shard_map/cond/branch_1_fun/ppermute | solution.py:26
  139.5 2.7 %grad_down.7 = f32[5120,128]{1,0:T(8,128)S(1)} custom-call(bf16[128,5120]{1,0:T(8,128)(2,1)S(1)} %get-tuple-element.865.x_ref, bf16[256,128]{1,0:T(8,128)(2,1)S(1)} %get-tuple-element.850.low_ref, bf16[256,128]{1,0:T(8,128)(2,1)} %get-tuple-element.851.low2_ref, f32[8,128]{1,0:T(8,128)S(1)} %get-tuple-element.852.high_ref, ...), custom_call_target="tpu_custom_call" | custom-call | tf_op jit(solution)/shard_map/cond/branch_1_fun/grad_down/pallas_call | solution.py:424
  142.3 13.7 %collective-permute-done.59.refs_2_ = bf16[192,1024]{1,0:T(8,128)(2,1)S(1)} collective-permute-done((bf16[192,1024]{1,0:T(8,128)(2,1)S(1)}, bf16[192,1024]{1,0:T(8,128)(2,1)S(1)}, u32[]{:S(2)}, u32[]{:S(2)}) %collective-permute-start.59) | collective-permute-done | bytes 393248 | tf_op jit(solution)/shard_map/cond/branch_1_fun/ppermute | solution.py:26
  155.9 1.4 merge.31
  157.4 0.0 collective-permute-done.60
  157.4 0.0 copy-start.24
  157.4 0.0 collective-permute-done.69.refs_8_
  157.4 0.0 collective-permute-done.68.refs_6_
  157.4 0.2 collective-permute-start.71
  157.6 0.3 collective-permute-start.70
  158.0 5.1 %last.1 = (f32[128,5120]{1,0:T(8,128)}, bf16[128,5120]{1,0:T(8,128)(2,1)}, bf16[128,5120]{1,0:T(8,128)(2,1)}) custom-call(s32[24]{0:T(128)S(1)} %get-tuple-element.1007.plan_ref, bf16[256,128]{1,0:T(8,128)(2,1)S(1)} %get-tuple-element.1008.low_ref, bf16[256,128]{1,0:T(8,128)(2,1)} %get-tuple-element.1015.low2_ref, bf16[128,5120]{1,0:T(8,128)(2,1)} %bitcast.46, ...), custom_call_target="tpu_custom_call" | custom-call | tf_op jit(solution)/shard_map/last/pallas_call | solution.py:488
  163.1 1.2 collective-permute-done.71.refs_3_
  164.2 2.6 %collective-permute-done.70.refs_2_ = bf16[128,1024]{1,0:T(8,128)(2,1)S(1)} collective-permute-done((bf16[128,1024]{1,0:T(8,128)(2,1)S(1)}, bf16[128,1024]{1,0:T(8,128)(2,1)S(1)}, u32[]{:S(2)}, u32[]{:S(2)}) %collective-permute-start.70) | collective-permute-done | bytes 262176 | tf_op jit(solution)/shard_map/ppermute | solution.py:21
  166.8 0.8 join.1
  (10 shorter events, 0.0 us)
Async XLA Ops:
  1.4 0.7 copy-start
  2.1 6.7 %copy-start.1 = (bf16[1,1,128,5120]{3,2,1,0:T(8,128)(2,1)S(1)}, bf16[1,1,128,5120]{3,2,1,0:T(8,128)(2,1)}, u32[]{:S(2)}) copy-start(bf16[1,1,128,5120]{3,2,1,0:T(8,128)(2,1)} %param.25) | copy-start | bytes 3932164
  2.1 6.7 %copy-start.2 = (bf16[1,1,128,5120]{3,2,1,0:T(8,128)(2,1)S(1)}, bf16[1,1,128,5120]{3,2,1,0:T(8,128)(2,1)}, u32[]{:S(2)}) copy-start(bf16[1,1,128,5120]{3,2,1,0:T(8,128)(2,1)} %param.26) | copy-start | bytes 3932164
  2.1 6.7 %copy-start.9 = (bf16[1,5120,128]{2,1,0:T(8,128)(2,1)S(1)}, bf16[1,5120,128]{2,1,0:T(8,128)(2,1)}, u32[]{:S(2)}) copy-start(bf16[1,5120,128]{2,1,0:T(8,128)(2,1)} %param.28) | copy-start | bytes 3932164
  2.1 6.7 %copy-start.16 = (bf16[1,128,5120]{2,1,0:T(8,128)(2,1)S(1)}, bf16[1,128,5120]{2,1,0:T(8,128)(2,1)}, u32[]{:S(2)}) copy-start(bf16[1,128,5120]{2,1,0:T(8,128)(2,1)} %param.29) | copy-start | bytes 3932164
  2.1 6.7 %copy-start.23 = (f32[1,5120]{1,0:T(1,128)S(1)}, f32[1,5120]{1,0:T(1,128)}, u32[]{:S(2)}) copy-start(f32[1,5120]{1,0:T(1,128)} %g_ref.1) | copy-start | bytes 61444
  8.8 16.4 %collective-permute-start.5 = (bf16[272,1024]{1,0:T(8,128)(2,1)S(1)}, bf16[272,1024]{1,0:T(8,128)(2,1)}, u32[]{:S(2)}, u32[]{:S(2)}) collective-permute-start(bf16[272,1024]{1,0:T(8,128)(2,1)S(1)} %get-tuple-element.530), channel_id=1, source_target_pairs={{0,2},{1,3},{2,0},{3,1},{4,6},{5,7},{6,4},{7,5},{8,10},{9,11},{10,... | collective-permute-start | bytes 1671176 | tf_op jit(solution)/shard_map/cond/branch_1_fun/ppermute | solution.py:26
  25.3 22.0 %collective-permute-start.6 = (bf16[224,1024]{1,0:T(8,128)(2,1)S(1)}, bf16[224,1024]{1,0:T(8,128)(2,1)}, u32[]{:S(2)}, u32[]{:S(2)}) collective-permute-start(bf16[224,1024]{1,0:T(8,128)(2,1)S(1)} %get-tuple-element.541), channel_id=1, source_target_pairs={{0,2},{1,3},{2,0},{3,1},{4,6},{5,7},{6,4},{7,5},{8,10},{9,11},{10,... | collective-permute-start | bytes 1376264 | tf_op jit(solution)/shard_map/cond/branch_1_fun/ppermute | solution.py:26
  31.0 11.9 %collective-permute-start.7 = (bf16[192,1024]{1,0:T(8,128)(2,1)S(1)}, bf16[192,1024]{1,0:T(8,128)(2,1)S(1)}, u32[]{:S(2)}, u32[]{:S(2)}) collective-permute-start(bf16[192,1024]{1,0:T(8,128)(2,1)S(1)} %get-tuple-element.538), channel_id=1, source_target_pairs={{0,1},{1,0},{2,3},{3,2},{4,5},{5,4},{6,7},{7,6},{8,9},{9,8},{10,11... | collective-permute-start | bytes 1179656 | tf_op jit(solution)/shard_map/cond/branch_1_fun/ppermute | solution.py:26
  47.3 21.0 %collective-permute-start.9 = (bf16[224,1024]{1,0:T(8,128)(2,1)S(1)}, bf16[224,1024]{1,0:T(8,128)(2,1)}, u32[]{:S(2)}, u32[]{:S(2)}) collective-permute-start(bf16[224,1024]{1,0:T(8,128)(2,1)S(1)} %get-tuple-element.552), channel_id=1, source_target_pairs={{0,2},{1,3},{2,0},{3,1},{4,6},{5,7},{6,4},{7,5},{8,10},{9,11},{10,... | collective-permute-start | bytes 1376264 | tf_op jit(solution)/shard_map/cond/branch_1_fun/ppermute | solution.py:26
  49.3 17.4 %collective-permute-start.8 = (bf16[192,1024]{1,0:T(8,128)(2,1)S(1)}, bf16[192,1024]{1,0:T(8,128)(2,1)S(1)}, u32[]{:S(2)}, u32[]{:S(2)}) collective-permute-start(bf16[192,1024]{1,0:T(8,128)(2,1)S(1)} %get-tuple-element.542), channel_id=1, source_target_pairs={{0,1},{1,0},{2,3},{3,2},{4,5},{5,4},{6,7},{7,6},{8,9},{9,8},{10,11... | collective-permute-start | bytes 1179656 | tf_op jit(solution)/shard_map/cond/branch_1_fun/ppermute | solution.py:26
  68.3 63.4 %collective-permute-start.66 = (bf16[128,2048]{1,0:T(8,128)(2,1)}, bf16[128,2048]{1,0:T(8,128)(2,1)S(1)}, u32[]{:S(2)}, u32[]{:S(2)}) collective-permute-start(bf16[128,2048]{1,0:T(8,128)(2,1)} %get-tuple-element.1027), channel_id=1, source_target_pairs={{28,0},{0,4},{4,8},{8,12},{12,16},{16,20},{20,24},{24,28},{29,1},{... | collective-permute-start | bytes 1572872 | tf_op jit(solution)/shard_map/ppermute | solution.py:21
  71.6 60.2 %collective-permute-start.67 = (bf16[128,2048]{1,0:T(8,128)(2,1)}, bf16[128,2048]{1,0:T(8,128)(2,1)S(1)}, u32[]{:S(2)}, u32[]{:S(2)}) collective-permute-start(bf16[128,2048]{1,0:T(8,128)(2,1)} %get-tuple-element.1028), channel_id=1, source_target_pairs={{4,0},{8,4},{12,8},{16,12},{20,16},{24,20},{28,24},{0,28},{5,1},{9... | collective-permute-start | bytes 1572872 | tf_op jit(solution)/shard_map/ppermute | solution.py:21
  88.4 21.2 %collective-permute-start.37 = (bf16[224,1024]{1,0:T(8,128)(2,1)}, bf16[224,1024]{1,0:T(8,128)(2,1)}, u32[]{:S(2)}, u32[]{:S(2)}) collective-permute-start(bf16[224,1024]{1,0:T(8,128)(2,1)} %get-tuple-element.702), channel_id=1, source_target_pairs={{0,2},{1,3},{2,0},{3,1},{4,6},{5,7},{6,4},{7,5},{8,10},{9,11},{10,... | collective-permute-start | bytes 1376264 | tf_op jit(solution)/shard_map/cond/branch_1_fun/ppermute | solution.py:26
  88.4 21.2 %copy-start.26 = (bf16[224,1024]{1,0:T(8,128)(2,1)S(1)}, bf16[224,1024]{1,0:T(8,128)(2,1)}, u32[]{:S(2)}) copy-start(bf16[224,1024]{1,0:T(8,128)(2,1)} %get-tuple-element.712) | copy-start | bytes 1376260 | tf_op jit(solution)/shard_map/cond
  88.4 21.2 %copy-start.4 = (bf16[128,5120]{1,0:T(8,128)(2,1)S(1)}, bf16[128,5120]{1,0:T(8,128)(2,1)}, u32[]{:S(2)}) copy-start(bf16[128,5120]{1,0:T(8,128)(2,1)} %get-tuple-element.690.dy_ref) | copy-start | bytes 3932164 | tf_op jit(solution)/shard_map/cond
  88.4 21.2 %copy-start.11 = (bf16[5120,128]{1,0:T(8,128)(2,1)S(1)}, bf16[5120,128]{1,0:T(8,128)(2,1)}, u32[]{:S(2)}) copy-start(bf16[5120,128]{1,0:T(8,128)(2,1)} %get-tuple-element.697.down_ref) | copy-start | bytes 3932164 | tf_op jit(solution)/shard_map/cond
  88.4 21.2 %copy-start.18 = (bf16[128,5120]{1,0:T(8,128)(2,1)S(1)}, bf16[128,5120]{1,0:T(8,128)(2,1)}, u32[]{:S(2)}) copy-start(bf16[128,5120]{1,0:T(8,128)(2,1)} %get-tuple-element.696.up_ref) | copy-start | bytes 3932164 | tf_op jit(solution)/shard_map/cond
  90.7 13.6 %collective-permute-start.38 = (bf16[192,1024]{1,0:T(8,128)(2,1)S(1)}, bf16[192,1024]{1,0:T(8,128)(2,1)S(1)}, u32[]{:S(2)}, u32[]{:S(2)}) collective-permute-start(bf16[192,1024]{1,0:T(8,128)(2,1)S(1)} %get-tuple-element.699), channel_id=1, source_target_pairs={{0,1},{1,0},{2,3},{3,2},{4,5},{5,4},{6,7},{7,6},{8,9},{9,8},{10,11... | collective-permute-start | bytes 1179656 | tf_op jit(solution)/shard_map/cond/branch_1_fun/ppermute | solution.py:26
  109.6 22.1 %collective-permute-start.40 = (bf16[224,1024]{1,0:T(8,128)(2,1)S(1)}, bf16[224,1024]{1,0:T(8,128)(2,1)}, u32[]{:S(2)}, u32[]{:S(2)}) collective-permute-start(bf16[224,1024]{1,0:T(8,128)(2,1)S(1)} %copy-done.26), channel_id=1, source_target_pairs={{0,2},{1,3},{2,0},{3,1},{4,6},{5,7},{6,4},{7,5},{8,10},{9,11},{10,... | collective-permute-start | bytes 1376264 | tf_op jit(solution)/shard_map/cond/branch_1_fun/ppermute | solution.py:26
  111.6 15.2 %collective-permute-start.39 = (bf16[192,1024]{1,0:T(8,128)(2,1)S(1)}, bf16[192,1024]{1,0:T(8,128)(2,1)S(1)}, u32[]{:S(2)}, u32[]{:S(2)}) collective-permute-start(bf16[192,1024]{1,0:T(8,128)(2,1)S(1)} %get-tuple-element.703), channel_id=1, source_target_pairs={{0,1},{1,0},{2,3},{3,2},{4,5},{5,4},{6,7},{7,6},{8,9},{9,8},{10,11... | collective-permute-start | bytes 1179656 | tf_op jit(solution)/shard_map/cond/branch_1_fun/ppermute | solution.py:26
  131.8 25.6 %collective-permute-start.69 = (bf16[128,2048]{1,0:T(8,128)(2,1)}, bf16[128,2048]{1,0:T(8,128)(2,1)S(1)}, u32[]{:S(2)}, u32[]{:S(2)}) collective-permute-start(bf16[128,2048]{1,0:T(8,128)(2,1)} %get-tuple-element.1031), channel_id=1, source_target_pairs={{4,0},{8,4},{12,8},{16,12},{20,16},{24,20},{28,24},{0,28},{5,1},{9... | collective-permute-start | bytes 1572872 | tf_op jit(solution)/shard_map/ppermute | solution.py:21
  134.9 22.5 %collective-permute-start.68 = (bf16[128,2048]{1,0:T(8,128)(2,1)}, bf16[128,2048]{1,0:T(8,128)(2,1)S(1)}, u32[]{:S(2)}, u32[]{:S(2)}) collective-permute-start(bf16[128,2048]{1,0:T(8,128)(2,1)} %get-tuple-element.1029), channel_id=1, source_target_pairs={{28,0},{0,4},{4,8},{8,12},{12,16},{16,20},{20,24},{24,28},{29,1},{... | collective-permute-start | bytes 1572872 | tf_op jit(solution)/shard_map/ppermute | solution.py:21
  137.1 18.9 %collective-permute-start.59 = (bf16[192,1024]{1,0:T(8,128)(2,1)S(1)}, bf16[192,1024]{1,0:T(8,128)(2,1)S(1)}, u32[]{:S(2)}, u32[]{:S(2)}) collective-permute-start(bf16[192,1024]{1,0:T(8,128)(2,1)S(1)} %get-tuple-element.857), channel_id=1, source_target_pairs={{0,1},{1,0},{2,3},{3,2},{4,5},{5,4},{6,7},{7,6},{8,9},{9,8},{10,11... | collective-permute-start | bytes 1179656 | tf_op jit(solution)/shard_map/cond/branch_1_fun/ppermute | solution.py:26
  137.1 20.2 %collective-permute-start.60 = (bf16[32,5120]{1,0:T(8,128)(2,1)}, bf16[32,5120]{1,0:T(8,128)(2,1)}, u32[]{:S(2)}, u32[]{:S(2)}) collective-permute-start(bf16[32,5120]{1,0:T(8,128)(2,1)} %get-tuple-element.864), channel_id=1, source_target_pairs={{0,2},{1,3},{2,0},{3,1},{4,6},{5,7},{6,4},{7,5},{8,10},{9,11},{10,... | collective-permute-start | bytes 983048 | tf_op jit(solution)/shard_map/cond/branch_1_fun/ppermute | solution.py:26
  157.4 5.7 %copy-start.24 = (f32[1,1,5120,128]{3,2,1,0:T(8,128)}, f32[1,1,5120,128]{3,2,1,0:T(8,128)S(1)}, u32[]{:S(2)}) copy-start(f32[1,1,5120,128]{3,2,1,0:T(8,128)S(1)} %get-tuple-element.1005) | copy-start | bytes 7864324
  157.4 6.8 %collective-permute-start.71 = (bf16[128,1024]{1,0:T(8,128)(2,1)S(1)}, bf16[128,1024]{1,0:T(8,128)(2,1)S(1)}, u32[]{:S(2)}, u32[]{:S(2)}) collective-permute-start(bf16[128,1024]{1,0:T(8,128)(2,1)S(1)} %get-tuple-element.1034), channel_id=1, source_target_pairs={{4,0},{8,4},{12,8},{16,12},{20,16},{24,20},{28,24},{0,28},{5,1},{9... | collective-permute-start | bytes 786440 | tf_op jit(solution)/shard_map/ppermute | solution.py:21
  157.6 9.2 %collective-permute-start.70 = (bf16[128,1024]{1,0:T(8,128)(2,1)S(1)}, bf16[128,1024]{1,0:T(8,128)(2,1)S(1)}, u32[]{:S(2)}, u32[]{:S(2)}) collective-permute-start(bf16[128,1024]{1,0:T(8,128)(2,1)S(1)} %get-tuple-element.1032), channel_id=1, source_target_pairs={{28,0},{0,4},{4,8},{8,12},{12,16},{16,20},{20,24},{24,28},{29,1},{... | collective-permute-start | bytes 786440 | tf_op jit(solution)/shard_map/ppermute | solution.py:21

commit v3 on v2

--- a/solution.py
+++ b/solution.py
@@ -9,7 +9,7 @@
 
 CAP = 2
 TILE = 512
-CHUNKS = (2, 2, 2, 2, 2)
+CHUNKS = (1, 2, 3, 2, 2)
 STAGES = (((0, 1, 2), (0, 1)), ((3, 4), (2, 3)), ((), (4,)))
 DEPTH, LAG = 1, 2
 F32, BF16 = jnp.float32, jnp.bfloat16

time: 169 us -> 165 us (0.976)
  the two profiles are of different devices: /device:TPU:0 before, /device:TPU:1 now
where the time goes in v3:
time: 165 us; the launch traced here: 164 us
  waiting for transfers between devices  75 us (45%)
  starting transfers between devices  51.9 us (31%)
  Pallas kernels  31.4 us (19%)
  local copies, waits for them, and re-layouts  3.2 us (2%)
    ppermute x11, waiting for transfers between devices, swapped(): lax.ppermute(block, axis, [(i, i ^ mask) for i in range(count) if i ^ mas...  71.5 us
    ppermute x6, starting transfers between devices, passed_along(): return lax.ppermute(block, axis, route)  36.6 us
    ppermute x11, starting transfers between devices, swapped(): lax.ppermute(block, axis, [(i, i ^ mask) for i in range(count) if i ^ mas...  15.3 us
    pallas_call x5, Pallas kernels, make_rows(): pl.pallas_call(functools.partial(rows_kernel, cap, blk), grid=(tiles,), o...  10.6 us
    pallas_call x1, Pallas kernels, make_open(): pl.pallas_call(functools.partial(open_kernel, widths), out_shape=[jax.Sha...  5.97 us
    pallas_call x1, Pallas kernels, make_last(): pl.pallas_call(functools.partial(last_kernel, tuple(places), tuple(starts...  5.06 us
    pallas_call x3, Pallas kernels, make_merge(): pl.pallas_call(functools.partial(merge_kernel, cap, rows // 4, tuple(span...  4.75 us
    ppermute x6, waiting for transfers between devices, passed_along(): return lax.ppermute(block, axis, route)  3.51 us
  transfers between devices with their start and end apart: 17, of which 9 were waited for; matrix products, arithmetic and copies ran while one was open for 1% of the time, Pallas kernels for 15%

profile of v3, /device:TPU:1, one launch (start us, length us, event | category | flops | bytes accessed | tf_op | source)
XLA Modules:
  0.0 163.5 jit_solution(66849018188207332)
XLA Ops:
  0.6 0.8 copy.13.wiring_ref
  1.4 0.7 copy-done
  2.1 0.0 copy-start.17
  2.1 6.0 %open.1 = (s32[24]{0:T(128)S(1)}, s32[1]{0:T(128)}, bf16[256,128]{1,0:T(8,128)(2,1)S(1)}, f32[8,128]{1,0:T(8,128)S(1)}, bf16[304,512]{1,0:T(8,128)(2,1)S(1)}, /*...) custom-call(s32[8,4,4]{2,1,0:T(4,128)S(1)} %copy.13.wiring_ref, ...), custom_call_target="tpu_custom_call" | custom-call | tf_op jit(solution)/shard_map/open/pallas_call | solution.py:198
  8.7 0.0 copy-done.1
  8.7 0.0 copy-done.2
  8.8 0.0 copy-done.3
  8.8 0.0 copy-done.10
  8.8 0.0 copy-done.17
  8.8 56.3 %conditional.3 = (bf16[128,1536]{1,0:T(8,128)(2,1)}, bf16[128,1536]{1,0:T(8,128)(2,1)}, bf16[256,128]{1,0:T(8,128)(2,1)}, f32[8,128]{1,0:T(8,128)}, bf16[32,5120...) conditional(s32[]{:T(128)} %bitcast.10, (s32[24]{0:T(128)S(1)}, ...), branch_computations={%region_0.0_spmd, %region_1.0_spmd, %region_2.0_spmd, %region_3.0_... | conditional | bytes 10289456 | solution.py:557
  8.8 4.2 %collective-permute-start.10 = (bf16[304,512]{1,0:T(8,128)(2,1)S(1)}, bf16[304,512]{1,0:T(8,128)(2,1)}, u32[]{:S(2)}, u32[]{:S(2)}) collective-permute-start(bf16[304,512]{1,0:T(8,128)(2,1)S(1)} %get-tuple-element.557), channel_id=1, source_target_pairs={{0,3},{1,2},{2,1},{3,0},{4,7},{5,6},{6,5},{7,4},{8,11},{9,10},{10,... | collective-permute-start | bytes 933896 | tf_op jit(solution)/shard_map/cond/branch_2_fun/ppermute | solution.py:26
  13.0 6.5 %collective-permute-done.10.got_ref = bf16[304,512]{1,0:T(8,128)(2,1)} collective-permute-done((bf16[304,512]{1,0:T(8,128)(2,1)S(1)}, bf16[304,512]{1,0:T(8,128)(2,1)}, u32[]{:S(2)}, u32[]{:S(2)}) %collective-permute-start.10) | collective-permute-done | bytes 311328 | tf_op jit(solution)/shard_map/cond/branch_2_fun/ppermute | solution.py:26
  19.5 3.6 %collective-permute-start.11 = (bf16[224,1024]{1,0:T(8,128)(2,1)S(1)}, bf16[224,1024]{1,0:T(8,128)(2,1)}, u32[]{:S(2)}, u32[]{:S(2)}) collective-permute-start(bf16[224,1024]{1,0:T(8,128)(2,1)S(1)} %get-tuple-element.568), channel_id=1, source_target_pairs={{0,3},{1,2},{2,1},{3,0},{4,7},{5,6},{6,5},{7,4},{8,11},{9,10},{10,... | collective-permute-start | bytes 1376264 | tf_op jit(solution)/shard_map/cond/branch_2_fun/ppermute | solution.py:26
  23.2 1.6 unpack.8
  24.8 1.4 rows.34
  26.2 0.1 collective-permute-start.12
  26.2 11.3 %collective-permute-done.12.refs_2_ = bf16[192,512]{1,0:T(8,128)(2,1)S(1)} collective-permute-done((bf16[192,512]{1,0:T(8,128)(2,1)S(1)}, bf16[192,512]{1,0:T(8,128)(2,1)S(1)}, u32[]{:S(2)}, u32[]{:S(2)}) %collective-permute-start.12) | collective-permute-done | bytes 196640 | tf_op jit(solution)/shard_map/cond/branch_2_fun/ppermute | solution.py:26
  37.6 0.0 collective-permute-done.11.got_ref
  37.6 2.2 %collective-permute-start.14 = (bf16[224,1536]{1,0:T(8,128)(2,1)S(1)}, bf16[224,1536]{1,0:T(8,128)(2,1)}, u32[]{:S(2)}, u32[]{:S(2)}) collective-permute-start(bf16[224,1536]{1,0:T(8,128)(2,1)S(1)} %get-tuple-element.579), channel_id=1, source_target_pairs={{0,3},{1,2},{2,1},{3,0},{4,7},{5,6},{6,5},{7,4},{8,11},{9,10},{10,... | collective-permute-start | bytes 2064392 | tf_op jit(solution)/shard_map/cond/branch_2_fun/ppermute | solution.py:26
  39.7 1.9 %rows.35 = (bf16[192,1024]{1,0:T(8,128)(2,1)S(1)}, bf16[128,1024]{1,0:T(8,128)(2,1)S(1)}, bf16[128,1024]{1,0:T(8,128)(2,1)S(1)}) custom-call(s32[24]{0:T(128)S(1)} %get-tuple-element.570.plan_ref, bf16[128,5120]{1,0:T(8,128)(2,1)S(1)} %get-tuple-element.555.x_ref, bf16[128,5120]{1,0:T(8,128)(2,1)S(1)} %get-tuple-element.556.dy_ref, ...), custom_call_target="tpu_custom_call" | custom-call | tf_op jit(solution)/shard_map/cond/branch_2_fun/rows/pallas_call | solution.py:298
  41.7 0.1 collective-permute-start.13
  41.7 1.7 %copy.34 = bf16[32,5120]{1,0:T(8,128)(2,1)} copy(bf16[32,5120]{1,0:T(8,128)(2,1)} %get-tuple-element.1063) | data formatting | bytes 655360 | tf_op jit(solution)/shard_map/cond
  43.4 20.0 %collective-permute-done.13.refs_5_ = bf16[192,1024]{1,0:T(8,128)(2,1)S(1)} collective-permute-done((bf16[192,1024]{1,0:T(8,128)(2,1)S(1)}, bf16[192,1024]{1,0:T(8,128)(2,1)S(1)}, u32[]{:S(2)}, u32[]{:S(2)}) %collective-permute-start.13) | collective-permute-done | bytes 393248 | tf_op jit(solution)/shard_map/cond/branch_2_fun/ppermute | solution.py:26
  63.4 1.6 merge.20
  65.1 0.0 collective-permute-done.14
  65.1 16.6 %collective-permute-start.66 = (bf16[128,1536]{1,0:T(8,128)(2,1)}, bf16[128,1536]{1,0:T(8,128)(2,1)S(1)}, u32[]{:S(2)}, u32[]{:S(2)}) collective-permute-start(bf16[128,1536]{1,0:T(8,128)(2,1)} %get-tuple-element.1027), channel_id=1, source_target_pairs={{28,0},{0,4},{4,8},{8,12},{12,16},{16,20},{20,24},{24,28},{29,1},{... | collective-permute-start | bytes 1179656 | tf_op jit(solution)/shard_map/ppermute | solution.py:21
  81.7 0.0 collective-permute-start.67
  81.7 39.7 %conditional.4 = (bf16[128,2560]{1,0:T(8,128)(2,1)}, bf16[128,2560]{1,0:T(8,128)(2,1)}, bf16[224,1024]{1,0:T(8,128)(2,1)}, bf16[224,1024]{1,0:T(8,128)(2,1)}) conditional(s32[]{:T(128)} %bitcast.10, (s32[24]{0:T(128)S(1)}, bf16[128,5120]{1,0:T(8,128)(2,1)S(1)}, bf16[128,5120]{1,0:T(8,128)(2,1)S(1)}, ...), branch_computations={%region_6.0_spmd, %region_7.0_spmd, %region_8.0_spmd, %region_9.0_... | conditional | bytes 23068976 | solution.py:557
  81.7 0.0 copy-start.6
  81.7 0.0 copy-start.13
  81.7 3.3 %rows.46 = (bf16[192,1536]{1,0:T(8,128)(2,1)S(1)}, bf16[128,1536]{1,0:T(8,128)(2,1)S(1)}, bf16[128,1536]{1,0:T(8,128)(2,1)S(1)}) custom-call(s32[24]{0:T(128)S(1)} %get-tuple-element.730.plan_ref, bf16[128,5120]{1,0:T(8,128)(2,1)S(1)} %get-tuple-element.715.x_ref, bf16[128,5120]{1,0:T(8,128)(2,1)S(1)} %get-tuple-element.716.dy_ref, ...), custom_call_target="tpu_custom_call" | custom-call | tf_op jit(solution)/shard_map/cond/branch_2_fun/rows/pallas_call | solution.py:298
  85.0 0.1 collective-permute-start.42
  85.1 0.0 copy-done.21
  85.1 1.0 collective-permute-start.41
  86.1 19.8 %collective-permute-done.41.got_ref = bf16[224,1024]{1,0:T(8,128)(2,1)} collective-permute-done((bf16[224,1024]{1,0:T(8,128)(2,1)S(1)}, bf16[224,1024]{1,0:T(8,128)(2,1)}, u32[]{:S(2)}, u32[]{:S(2)}) %collective-permute-start.41) | collective-permute-done | bytes 458784 | tf_op jit(solution)/shard_map/cond/branch_2_fun/ppermute | solution.py:26
  105.8 0.0 collective-permute-done.42.refs_2_
  105.8 0.0 copy-done.27
  105.9 2.4 %collective-permute-start.44 = (bf16[224,1024]{1,0:T(8,128)(2,1)S(1)}, bf16[224,1024]{1,0:T(8,128)(2,1)}, u32[]{:S(2)}, u32[]{:S(2)}) collective-permute-start(bf16[224,1024]{1,0:T(8,128)(2,1)S(1)} %copy-done.27), channel_id=1, source_target_pairs={{0,3},{1,2},{2,1},{3,0},{4,7},{5,6},{6,5},{7,4},{8,11},{9,10},{10,... | collective-permute-start | bytes 1376264 | tf_op jit(solution)/shard_map/cond/branch_2_fun/ppermute | solution.py:26
  108.2 0.0 copy-done.13
  108.2 1.9 %rows.47 = (bf16[192,1024]{1,0:T(8,128)(2,1)S(1)}, bf16[128,1024]{1,0:T(8,128)(2,1)S(1)}, bf16[128,1024]{1,0:T(8,128)(2,1)S(1)}) custom-call(s32[24]{0:T(128)S(1)} %get-tuple-element.730.plan_ref, bf16[128,5120]{1,0:T(8,128)(2,1)S(1)} %get-tuple-element.715.x_ref, bf16[128,5120]{1,0:T(8,128)(2,1)S(1)} %get-tuple-element.716.dy_ref, ...), custom_call_target="tpu_custom_call" | custom-call | tf_op jit(solution)/shard_map/cond/branch_2_fun/rows/pallas_call | solution.py:298
  110.1 0.1 collective-permute-start.43
  110.2 9.2 %collective-permute-done.43.refs_5_ = bf16[192,1024]{1,0:T(8,128)(2,1)S(1)} collective-permute-done((bf16[192,1024]{1,0:T(8,128)(2,1)S(1)}, bf16[192,1024]{1,0:T(8,128)(2,1)S(1)}, u32[]{:S(2)}, u32[]{:S(2)}) %collective-permute-start.43) | collective-permute-done | bytes 393248 | tf_op jit(solution)/shard_map/cond/branch_2_fun/ppermute | solution.py:26
  119.4 1.7 %merge.26 = (bf16[128,2560]{1,0:T(8,128)(2,1)}, bf16[128,2560]{1,0:T(8,128)(2,1)}) custom-call(s32[24]{0:T(128)S(1)} %get-tuple-element.730.plan_ref, bf16[128,1536]{1,0:T(8,128)(2,1)S(1)} %get-tuple-element.731.refs_0_, bf16[128,1536]{1,0:T(8,128)(2,1)S(1)} %get-tuple-element.732.refs_1_, bf16[192,1536]{1,0:T(8,128)(2,1)S(1)} %collective-permute-done.42.refs_2_, ...), custom_call_target="tpu_custom_call" | custom-call | tf_op jit(solution)/shard_map/cond/branch_2_fun/merge/pallas_call | solution.py:356
  121.1 0.0 collective-permute-done.44
  121.4 0.0 collective-permute-done.66.refs_5_
  121.4 0.0 collective-permute-done.67.refs_7_
  121.4 0.1 collective-permute-start.69
  121.4 13.2 %collective-permute-start.68 = (bf16[128,2560]{1,0:T(8,128)(2,1)}, bf16[128,2560]{1,0:T(8,128)(2,1)S(1)}, u32[]{:S(2)}, u32[]{:S(2)}) collective-permute-start(bf16[128,2560]{1,0:T(8,128)(2,1)} %get-tuple-element.1029), channel_id=1, source_target_pairs={{28,0},{0,4},{4,8},{8,12},{12,16},{16,20},{20,24},{24,28},{29,1},{... | collective-permute-start | bytes 1966088 | tf_op jit(solution)/shard_map/ppermute | solution.py:21
  134.7 12.6 %conditional.5 = (bf16[128,1024]{1,0:T(8,128)(2,1)S(1)}, bf16[128,1024]{1,0:T(8,128)(2,1)S(1)}, bf16[32,5120]{1,0:T(8,128)(2,1)}, f32[1,1,5120,128]{3,2,1,0:T(8,128)S(1)}) conditional(s32[]{:T(128)} %bitcast.10, (s32[24]{0:T(128)S(1)}, bf16[128,5120]{1,0:T(8,128)(2,1)S(1)}, bf16[128,5120]{1,0:T(8,128)(2,1)}, ...), branch_computations={%region_12.0_spmd, %region_13.0_spmd, %region_14.0_spmd, %region_1... | conditional | bytes 2883696 | solution.py:557
  134.7 2.1 %rows.56 = (bf16[192,1024]{1,0:T(8,128)(2,1)S(1)}, bf16[128,1024]{1,0:T(8,128)(2,1)S(1)}, bf16[128,1024]{1,0:T(8,128)(2,1)S(1)}) custom-call(s32[24]{0:T(128)S(1)} %get-tuple-element.883.plan_ref, bf16[128,5120]{1,0:T(8,128)(2,1)S(1)} %get-tuple-element.890.x_ref, bf16[128,5120]{1,0:T(8,128)(2,1)} %get-tuple-element.873.dy_ref, ...), custom_call_target="tpu_custom_call" | custom-call | tf_op jit(solution)/shard_map/cond/branch_2_fun/rows/pallas_call | solution.py:298
  136.8 0.1 collective-permute-start.61
  136.8 1.6 collective-permute-start.62
  138.5 2.7 %grad_down.8 = f32[5120,128]{1,0:T(8,128)S(1)} custom-call(bf16[128,5120]{1,0:T(8,128)(2,1)S(1)} %get-tuple-element.890.x_ref, bf16[256,128]{1,0:T(8,128)(2,1)S(1)} %get-tuple-element.875.low_ref, bf16[256,128]{1,0:T(8,128)(2,1)} %get-tuple-element.876.low2_ref, f32[8,128]{1,0:T(8,128)S(1)} %get-tuple-element.877.high_ref, ...), custom_call_target="tpu_custom_call" | custom-call | tf_op jit(solution)/shard_map/cond/branch_2_fun/grad_down/pallas_call | solution.py:424
  141.1 2.3 %collective-permute-done.61.refs_2_ = bf16[192,1024]{1,0:T(8,128)(2,1)S(1)} collective-permute-done((bf16[192,1024]{1,0:T(8,128)(2,1)S(1)}, bf16[192,1024]{1,0:T(8,128)(2,1)S(1)}, u32[]{:S(2)}, u32[]{:S(2)}) %collective-permute-start.61) | collective-permute-done | bytes 393248 | tf_op jit(solution)/shard_map/cond/branch_2_fun/ppermute | solution.py:26
  143.4 1.4 merge.32
  144.8 2.4 %collective-permute-done.62 = bf16[32,5120]{1,0:T(8,128)(2,1)} collective-permute-done((bf16[32,5120]{1,0:T(8,128)(2,1)}, bf16[32,5120]{1,0:T(8,128)(2,1)}, u32[]{:S(2)}, u32[]{:S(2)}) %collective-permute-start.62) | collective-permute-done | bytes 327712 | tf_op jit(solution)/shard_map/cond/branch_2_fun/ppermute | solution.py:26
  147.3 2.9 %collective-permute-done.69.refs_8_ = bf16[128,2560]{1,0:T(8,128)(2,1)S(1)} collective-permute-done((bf16[128,2560]{1,0:T(8,128)(2,1)}, bf16[128,2560]{1,0:T(8,128)(2,1)S(1)}, u32[]{:S(2)}, u32[]{:S(2)}) %collective-permute-start.69) | collective-permute-done | bytes 655392 | tf_op jit(solution)/shard_map/ppermute | solution.py:21
  150.2 0.0 collective-permute-done.68.refs_6_
  150.2 0.0 collective-permute-start.71
  150.2 6.7 %collective-permute-start.70 = (bf16[128,1024]{1,0:T(8,128)(2,1)S(1)}, bf16[128,1024]{1,0:T(8,128)(2,1)S(1)}, u32[]{:S(2)}, u32[]{:S(2)}) collective-permute-start(bf16[128,1024]{1,0:T(8,128)(2,1)S(1)} %get-tuple-element.1032), channel_id=1, source_target_pairs={{28,0},{0,4},{4,8},{8,12},{12,16},{16,20},{20,24},{24,28},{29,1},{... | collective-permute-start | bytes 786440 | tf_op jit(solution)/shard_map/ppermute | solution.py:21
  156.9 5.1 %last.1 = (f32[128,5120]{1,0:T(8,128)}, bf16[128,5120]{1,0:T(8,128)(2,1)}, bf16[128,5120]{1,0:T(8,128)(2,1)}) custom-call(s32[24]{0:T(128)S(1)} %get-tuple-element.1007.plan_ref, bf16[256,128]{1,0:T(8,128)(2,1)S(1)} %get-tuple-element.1008.low_ref, bf16[256,128]{1,0:T(8,128)(2,1)} %get-tuple-element.1015.low2_ref, bf16[128,5120]{1,0:T(8,128)(2,1)} %bitcast.40, ...), custom_call_target="tpu_custom_call" | custom-call | tf_op jit(solution)/shard_map/last/pallas_call | solution.py:488
  162.0 0.6 collective-permute-done.71.refs_3_
  162.6 0.0 collective-permute-done.70.refs_2_
  162.6 0.8 join.1
  (10 shorter events, 0.0 us)
Async XLA Ops:
  1.4 0.7 copy-start
  2.1 6.7 %copy-start.1 = (bf16[1,1,128,5120]{3,2,1,0:T(8,128)(2,1)S(1)}, bf16[1,1,128,5120]{3,2,1,0:T(8,128)(2,1)}, u32[]{:S(2)}) copy-start(bf16[1,1,128,5120]{3,2,1,0:T(8,128)(2,1)} %param.25) | copy-start | bytes 3932164
  2.1 6.7 %copy-start.2 = (bf16[1,1,128,5120]{3,2,1,0:T(8,128)(2,1)S(1)}, bf16[1,1,128,5120]{3,2,1,0:T(8,128)(2,1)}, u32[]{:S(2)}) copy-start(bf16[1,1,128,5120]{3,2,1,0:T(8,128)(2,1)} %param.26) | copy-start | bytes 3932164
  2.1 6.7 %copy-start.3 = (bf16[1,5120,128]{2,1,0:T(8,128)(2,1)S(1)}, bf16[1,5120,128]{2,1,0:T(8,128)(2,1)}, u32[]{:S(2)}) copy-start(bf16[1,5120,128]{2,1,0:T(8,128)(2,1)} %param.28) | copy-start | bytes 3932164
  2.1 6.7 %copy-start.10 = (bf16[1,128,5120]{2,1,0:T(8,128)(2,1)S(1)}, bf16[1,128,5120]{2,1,0:T(8,128)(2,1)}, u32[]{:S(2)}) copy-start(bf16[1,128,5120]{2,1,0:T(8,128)(2,1)} %param.29) | copy-start | bytes 3932164
  2.1 6.7 %copy-start.17 = (f32[1,5120]{1,0:T(1,128)S(1)}, f32[1,5120]{1,0:T(1,128)}, u32[]{:S(2)}) copy-start(f32[1,5120]{1,0:T(1,128)} %g_ref.1) | copy-start | bytes 61444
  8.8 10.7 %collective-permute-start.10 = (bf16[304,512]{1,0:T(8,128)(2,1)S(1)}, bf16[304,512]{1,0:T(8,128)(2,1)}, u32[]{:S(2)}, u32[]{:S(2)}) collective-permute-start(bf16[304,512]{1,0:T(8,128)(2,1)S(1)} %get-tuple-element.557), channel_id=1, source_target_pairs={{0,3},{1,2},{2,1},{3,0},{4,7},{5,6},{6,5},{7,4},{8,11},{9,10},{10,... | collective-permute-start | bytes 933896 | tf_op jit(solution)/shard_map/cond/branch_2_fun/ppermute | solution.py:26
  19.5 18.0 %collective-permute-start.11 = (bf16[224,1024]{1,0:T(8,128)(2,1)S(1)}, bf16[224,1024]{1,0:T(8,128)(2,1)}, u32[]{:S(2)}, u32[]{:S(2)}) collective-permute-start(bf16[224,1024]{1,0:T(8,128)(2,1)S(1)} %get-tuple-element.568), channel_id=1, source_target_pairs={{0,3},{1,2},{2,1},{3,0},{4,7},{5,6},{6,5},{7,4},{8,11},{9,10},{10,... | collective-permute-start | bytes 1376264 | tf_op jit(solution)/shard_map/cond/branch_2_fun/ppermute | solution.py:26
  26.2 11.4 %collective-permute-start.12 = (bf16[192,512]{1,0:T(8,128)(2,1)S(1)}, bf16[192,512]{1,0:T(8,128)(2,1)S(1)}, u32[]{:S(2)}, u32[]{:S(2)}) collective-permute-start(bf16[192,512]{1,0:T(8,128)(2,1)S(1)} %get-tuple-element.565), channel_id=1, source_target_pairs={{0,1},{1,0},{2,3},{3,2},{4,5},{5,4},{6,7},{7,6},{8,9},{9,8},{10,11... | collective-permute-start | bytes 589832 | tf_op jit(solution)/shard_map/cond/branch_2_fun/ppermute | solution.py:26
  37.6 27.5 %collective-permute-start.14 = (bf16[224,1536]{1,0:T(8,128)(2,1)S(1)}, bf16[224,1536]{1,0:T(8,128)(2,1)}, u32[]{:S(2)}, u32[]{:S(2)}) collective-permute-start(bf16[224,1536]{1,0:T(8,128)(2,1)S(1)} %get-tuple-element.579), channel_id=1, source_target_pairs={{0,3},{1,2},{2,1},{3,0},{4,7},{5,6},{6,5},{7,4},{8,11},{9,10},{10,... | collective-permute-start | bytes 2064392 | tf_op jit(solution)/shard_map/cond/branch_2_fun/ppermute | solution.py:26
  41.7 21.8 %collective-permute-start.13 = (bf16[192,1024]{1,0:T(8,128)(2,1)S(1)}, bf16[192,1024]{1,0:T(8,128)(2,1)S(1)}, u32[]{:S(2)}, u32[]{:S(2)}) collective-permute-start(bf16[192,1024]{1,0:T(8,128)(2,1)S(1)} %get-tuple-element.569), channel_id=1, source_target_pairs={{0,1},{1,0},{2,3},{3,2},{4,5},{5,4},{6,7},{7,6},{8,9},{9,8},{10,11... | collective-permute-start | bytes 1179656 | tf_op jit(solution)/shard_map/cond/branch_2_fun/ppermute | solution.py:26
  65.1 56.3 %collective-permute-start.66 = (bf16[128,1536]{1,0:T(8,128)(2,1)}, bf16[128,1536]{1,0:T(8,128)(2,1)S(1)}, u32[]{:S(2)}, u32[]{:S(2)}) collective-permute-start(bf16[128,1536]{1,0:T(8,128)(2,1)} %get-tuple-element.1027), channel_id=1, source_target_pairs={{28,0},{0,4},{4,8},{8,12},{12,16},{16,20},{20,24},{24,28},{29,1},{... | collective-permute-start | bytes 1179656 | tf_op jit(solution)/shard_map/ppermute | solution.py:21
  81.7 39.7 %collective-permute-start.67 = (bf16[128,1536]{1,0:T(8,128)(2,1)}, bf16[128,1536]{1,0:T(8,128)(2,1)S(1)}, u32[]{:S(2)}, u32[]{:S(2)}) collective-permute-start(bf16[128,1536]{1,0:T(8,128)(2,1)} %get-tuple-element.1028), channel_id=1, source_target_pairs={{4,0},{8,4},{12,8},{16,12},{20,16},{24,20},{28,24},{0,28},{5,1},{9... | collective-permute-start | bytes 1179656 | tf_op jit(solution)/shard_map/ppermute | solution.py:21
  81.7 3.4 %copy-start.21 = (bf16[224,1024]{1,0:T(8,128)(2,1)S(1)}, bf16[224,1024]{1,0:T(8,128)(2,1)}, u32[]{:S(2)}) copy-start(bf16[224,1024]{1,0:T(8,128)(2,1)} %get-tuple-element.728) | copy-start | bytes 1376260 | tf_op jit(solution)/shard_map/cond
  81.7 24.2 %copy-start.27 = (bf16[224,1024]{1,0:T(8,128)(2,1)S(1)}, bf16[224,1024]{1,0:T(8,128)(2,1)}, u32[]{:S(2)}) copy-start(bf16[224,1024]{1,0:T(8,128)(2,1)} %get-tuple-element.738) | copy-start | bytes 1376260 | tf_op jit(solution)/shard_map/cond
  81.7 26.5 %copy-start.6 = (bf16[5120,128]{1,0:T(8,128)(2,1)S(1)}, bf16[5120,128]{1,0:T(8,128)(2,1)}, u32[]{:S(2)}) copy-start(bf16[5120,128]{1,0:T(8,128)(2,1)} %get-tuple-element.723.down_ref) | copy-start | bytes 3932164 | tf_op jit(solution)/shard_map/cond
  81.7 26.5 %copy-start.13 = (bf16[128,5120]{1,0:T(8,128)(2,1)S(1)}, bf16[128,5120]{1,0:T(8,128)(2,1)}, u32[]{:S(2)}) copy-start(bf16[128,5120]{1,0:T(8,128)(2,1)} %get-tuple-element.722.up_ref) | copy-start | bytes 3932164 | tf_op jit(solution)/shard_map/cond
  85.0 20.8 %collective-permute-start.42 = (bf16[192,1536]{1,0:T(8,128)(2,1)S(1)}, bf16[192,1536]{1,0:T(8,128)(2,1)S(1)}, u32[]{:S(2)}, u32[]{:S(2)}) collective-permute-start(bf16[192,1536]{1,0:T(8,128)(2,1)S(1)} %get-tuple-element.725), channel_id=1, source_target_pairs={{0,1},{1,0},{2,3},{3,2},{4,5},{5,4},{6,7},{7,6},{8,9},{9,8},{10,11... | collective-permute-start | bytes 1769480 | tf_op jit(solution)/shard_map/cond/branch_2_fun/ppermute | solution.py:26
  85.1 20.7 %collective-permute-start.41 = (bf16[224,1024]{1,0:T(8,128)(2,1)S(1)}, bf16[224,1024]{1,0:T(8,128)(2,1)}, u32[]{:S(2)}, u32[]{:S(2)}) collective-permute-start(bf16[224,1024]{1,0:T(8,128)(2,1)S(1)} %copy-done.21), channel_id=1, source_target_pairs={{0,3},{1,2},{2,1},{3,0},{4,7},{5,6},{6,5},{7,4},{8,11},{9,10},{10,... | collective-permute-start | bytes 1376264 | tf_op jit(solution)/shard_map/cond/branch_2_fun/ppermute | solution.py:26
  105.9 15.3 %collective-permute-start.44 = (bf16[224,1024]{1,0:T(8,128)(2,1)S(1)}, bf16[224,1024]{1,0:T(8,128)(2,1)}, u32[]{:S(2)}, u32[]{:S(2)}) collective-permute-start(bf16[224,1024]{1,0:T(8,128)(2,1)S(1)} %copy-done.27), channel_id=1, source_target_pairs={{0,3},{1,2},{2,1},{3,0},{4,7},{5,6},{6,5},{7,4},{8,11},{9,10},{10,... | collective-permute-start | bytes 1376264 | tf_op jit(solution)/shard_map/cond/branch_2_fun/ppermute | solution.py:26
  110.1 9.2 %collective-permute-start.43 = (bf16[192,1024]{1,0:T(8,128)(2,1)S(1)}, bf16[192,1024]{1,0:T(8,128)(2,1)S(1)}, u32[]{:S(2)}, u32[]{:S(2)}) collective-permute-start(bf16[192,1024]{1,0:T(8,128)(2,1)S(1)} %get-tuple-element.729), channel_id=1, source_target_pairs={{0,1},{1,0},{2,3},{3,2},{4,5},{5,4},{6,7},{7,6},{8,9},{9,8},{10,11... | collective-permute-start | bytes 1179656 | tf_op jit(solution)/shard_map/cond/branch_2_fun/ppermute | solution.py:26
  121.4 28.8 %collective-permute-start.69 = (bf16[128,2560]{1,0:T(8,128)(2,1)}, bf16[128,2560]{1,0:T(8,128)(2,1)S(1)}, u32[]{:S(2)}, u32[]{:S(2)}) collective-permute-start(bf16[128,2560]{1,0:T(8,128)(2,1)} %get-tuple-element.1031), channel_id=1, source_target_pairs={{4,0},{8,4},{12,8},{16,12},{20,16},{24,20},{28,24},{0,28},{5,1},{9... | collective-permute-start | bytes 1966088 | tf_op jit(solution)/shard_map/ppermute | solution.py:21
  121.4 28.8 %collective-permute-start.68 = (bf16[128,2560]{1,0:T(8,128)(2,1)}, bf16[128,2560]{1,0:T(8,128)(2,1)S(1)}, u32[]{:S(2)}, u32[]{:S(2)}) collective-permute-start(bf16[128,2560]{1,0:T(8,128)(2,1)} %get-tuple-element.1029), channel_id=1, source_target_pairs={{28,0},{0,4},{4,8},{8,12},{12,16},{16,20},{20,24},{24,28},{29,1},{... | collective-permute-start | bytes 1966088 | tf_op jit(solution)/shard_map/ppermute | solution.py:21
  136.8 6.7 %collective-permute-start.61 = (bf16[192,1024]{1,0:T(8,128)(2,1)S(1)}, bf16[192,1024]{1,0:T(8,128)(2,1)S(1)}, u32[]{:S(2)}, u32[]{:S(2)}) collective-permute-start(bf16[192,1024]{1,0:T(8,128)(2,1)S(1)} %get-tuple-element.882), channel_id=1, source_target_pairs={{0,1},{1,0},{2,3},{3,2},{4,5},{5,4},{6,7},{7,6},{8,9},{9,8},{10,11... | collective-permute-start | bytes 1179656 | tf_op jit(solution)/shard_map/cond/branch_2_fun/ppermute | solution.py:26
  136.8 10.4 %collective-permute-start.62 = (bf16[32,5120]{1,0:T(8,128)(2,1)}, bf16[32,5120]{1,0:T(8,128)(2,1)}, u32[]{:S(2)}, u32[]{:S(2)}) collective-permute-start(bf16[32,5120]{1,0:T(8,128)(2,1)} %get-tuple-element.889), channel_id=1, source_target_pairs={{0,3},{1,2},{2,1},{3,0},{4,7},{5,6},{6,5},{7,4},{8,11},{9,10},{10,... | collective-permute-start | bytes 983048 | tf_op jit(solution)/shard_map/cond/branch_2_fun/ppermute | solution.py:26
  147.3 14.7 %copy-start.18 = (f32[1,1,5120,128]{3,2,1,0:T(8,128)}, f32[1,1,5120,128]{3,2,1,0:T(8,128)S(1)}, u32[]{:S(2)}) copy-start(f32[1,1,5120,128]{3,2,1,0:T(8,128)S(1)} %get-tuple-element.1005) | copy-start | bytes 7864324
  150.2 12.3 %collective-permute-start.71 = (bf16[128,1024]{1,0:T(8,128)(2,1)S(1)}, bf16[128,1024]{1,0:T(8,128)(2,1)S(1)}, u32[]{:S(2)}, u32[]{:S(2)}) collective-permute-start(bf16[128,1024]{1,0:T(8,128)(2,1)S(1)} %get-tuple-element.1034), channel_id=1, source_target_pairs={{4,0},{8,4},{12,8},{16,12},{20,16},{24,20},{28,24},{0,28},{5,1},{9... | collective-permute-start | bytes 786440 | tf_op jit(solution)/shard_map/ppermute | solution.py:21
  150.2 12.3 %collective-permute-start.70 = (bf16[128,1024]{1,0:T(8,128)(2,1)S(1)}, bf16[128,1024]{1,0:T(8,128)(2,1)S(1)}, u32[]{:S(2)}, u32[]{:S(2)}) collective-permute-start(bf16[128,1024]{1,0:T(8,128)(2,1)S(1)} %get-tuple-element.1032), channel_id=1, source_target_pairs={{28,0},{0,4},{4,8},{8,12},{12,16},{16,20},{20,24},{24,28},{29,1},{... | collective-permute-start | bytes 786440 | tf_op jit(solution)/shard_map/ppermute | solution.py:21

commit v4 on v3

--- a/solution.py
+++ b/solution.py
@@ -11,7 +11,7 @@
 TILE = 512
 CHUNKS = (1, 2, 3, 2, 2)
 STAGES = (((0, 1, 2), (0, 1)), ((3, 4), (2, 3)), ((), (4,)))
-DEPTH, LAG = 1, 2
+DEPTH, LAG = 2, 3
 F32, BF16 = jnp.float32, jnp.bfloat16
 
 

time: 165 us -> 169 us (1.024); the launches traced: 164 us -> 170 us
  waiting for transfers between devices: 75 us -> 116 us
  starting transfers between devices: 51.9 us -> 17.3 us
    ppermute x11, waiting for transfers between devices: 71.5 us -> 116 us  [swapped(): lax.ppermute(block, axis, [(i, i ^ mask) for i in range(count) if i ^ mas...]
    ppermute x6, starting transfers between devices: 36.6 us -> 5.96 us  [passed_along(): return lax.ppermute(block, axis, route)]
    ppermute x11, starting transfers between devices: 15.3 us -> 11.4 us  [swapped(): lax.ppermute(block, axis, [(i, i ^ mask) for i in range(count) if i ^ mas...]
    ppermute x6, waiting for transfers between devices: 3.51 us -> 0.82 us  [passed_along(): return lax.ppermute(block, axis, route)]
  transfers between devices with their start and end apart: 17 -> 17, of which waited for: 9 -> 8; matrix products, arithmetic and copies ran while one was open for 1% -> 1% of each run, Pallas kernels for 15% -> 14%
where the time goes in v4:
time: 169 us; the launch traced here: 170 us
  waiting for transfers between devices  116 us (69%)
  Pallas kernels  31.4 us (19%)
  starting transfers between devices  17.3 us (10%)
  local copies, waits for them, and re-layouts  3.21 us (2%)
    ppermute x11, waiting for transfers between devices, swapped(): lax.ppermute(block, axis, [(i, i ^ mask) for i in range(count) if i ^ mas...  116 us
    ppermute x11, starting transfers between devices, swapped(): lax.ppermute(block, axis, [(i, i ^ mask) for i in range(count) if i ^ mas...  11.4 us
    pallas_call x5, Pallas kernels, make_rows(): pl.pallas_call(functools.partial(rows_kernel, cap, blk), grid=(tiles,), o...  10.6 us
    pallas_call x1, Pallas kernels, make_open(): pl.pallas_call(functools.partial(open_kernel, widths), out_shape=[jax.Sha...  5.97 us
    ppermute x6, starting transfers between devices, passed_along(): return lax.ppermute(block, axis, route)  5.96 us
    pallas_call x1, Pallas kernels, make_last(): pl.pallas_call(functools.partial(last_kernel, tuple(places), tuple(starts...  5.06 us
    pallas_call x3, Pallas kernels, make_merge(): pl.pallas_call(functools.partial(merge_kernel, cap, rows // 4, tuple(span...  4.73 us
  transfers between devices with their start and end apart: 17, of which 8 were waited for; matrix products, arithmetic and copies ran while one was open for 1% of the time, Pallas kernels for 14%

profile of v4, /device:TPU:1, one launch (start us, length us, event | category | flops | bytes accessed | tf_op | source)
XLA Modules:
  0.0 170.5 jit_solution(17468835009234639747)
XLA Ops:
  0.6 0.8 copy.13.wiring_ref
  1.4 0.7 copy-done
  2.1 0.0 copy-start.17
  2.1 6.0 %open.1 = (s32[24]{0:T(128)S(1)}, s32[1]{0:T(128)}, bf16[256,128]{1,0:T(8,128)(2,1)S(1)}, f32[8,128]{1,0:T(8,128)S(1)}, bf16[304,512]{1,0:T(8,128)(2,1)S(1)}, /*...) custom-call(s32[8,4,4]{2,1,0:T(4,128)S(1)} %copy.13.wiring_ref, ...), custom_call_target="tpu_custom_call" | custom-call | tf_op jit(solution)/shard_map/open/pallas_call | solution.py:198
  8.7 0.0 copy-done.1
  8.7 0.0 copy-done.2
  8.8 0.0 copy-done.3
  8.8 0.0 copy-done.10
  8.8 0.0 copy-done.17
  8.8 81.2 %conditional.3 = (bf16[128,1536]{1,0:T(8,128)(2,1)}, bf16[128,1536]{1,0:T(8,128)(2,1)}, bf16[256,128]{1,0:T(8,128)(2,1)}, f32[8,128]{1,0:T(8,128)}, bf16[32,5120...) conditional(s32[]{:T(128)} %bitcast.10, (s32[24]{0:T(128)S(1)}, ...), branch_computations={%region_0.0_spmd, %region_1.0_spmd, %region_2.0_spmd, %region_3.0_... | conditional | bytes 10289456 | solution.py:557
  8.8 3.2 %collective-permute-start.5 = (bf16[304,512]{1,0:T(8,128)(2,1)S(1)}, bf16[304,512]{1,0:T(8,128)(2,1)}, u32[]{:S(2)}, u32[]{:S(2)}) collective-permute-start(bf16[304,512]{1,0:T(8,128)(2,1)S(1)} %get-tuple-element.535), channel_id=1, source_target_pairs={{0,2},{1,3},{2,0},{3,1},{4,6},{5,7},{6,4},{7,5},{8,10},{9,11},{10,... | collective-permute-start | bytes 933896 | tf_op jit(solution)/shard_map/cond/branch_1_fun/ppermute | solution.py:26
  12.0 0.1 collective-permute-start.6
  12.1 23.6 %collective-permute-done.5.got_ref = bf16[304,512]{1,0:T(8,128)(2,1)} collective-permute-done((bf16[304,512]{1,0:T(8,128)(2,1)S(1)}, bf16[304,512]{1,0:T(8,128)(2,1)}, u32[]{:S(2)}, u32[]{:S(2)}) %collective-permute-start.5) | collective-permute-done | bytes 311328 | tf_op jit(solution)/shard_map/cond/branch_1_fun/ppermute | solution.py:26
  35.7 0.0 collective-permute-start.9
  35.7 1.6 unpack.7
  37.3 1.4 rows.32
  38.7 21.6 %collective-permute-done.6.got_ref = bf16[224,1024]{1,0:T(8,128)(2,1)} collective-permute-done((bf16[224,1024]{1,0:T(8,128)(2,1)S(1)}, bf16[224,1024]{1,0:T(8,128)(2,1)}, u32[]{:S(2)}, u32[]{:S(2)}) %collective-permute-start.6) | collective-permute-done | bytes 458784 | tf_op jit(solution)/shard_map/cond/branch_1_fun/ppermute | solution.py:26
  60.3 1.9 %rows.33 = (bf16[192,1024]{1,0:T(8,128)(2,1)S(1)}, bf16[128,1024]{1,0:T(8,128)(2,1)S(1)}, bf16[128,1024]{1,0:T(8,128)(2,1)S(1)}) custom-call(s32[24]{0:T(128)S(1)} %get-tuple-element.547.plan_ref, bf16[128,5120]{1,0:T(8,128)(2,1)S(1)} %get-tuple-element.533.x_ref, bf16[128,5120]{1,0:T(8,128)(2,1)S(1)} %get-tuple-element.534.dy_ref, ...), custom_call_target="tpu_custom_call" | custom-call | tf_op jit(solution)/shard_map/cond/branch_1_fun/rows/pallas_call | solution.py:298
  62.2 1.1 collective-permute-start.8
  63.3 0.4 collective-permute-start.7
  63.7 1.7 %copy.26 = bf16[32,5120]{1,0:T(8,128)(2,1)} copy(bf16[32,5120]{1,0:T(8,128)(2,1)} %get-tuple-element.1049) | data formatting | bytes 655360 | tf_op jit(solution)/shard_map/cond
  65.4 22.9 %collective-permute-done.7.refs_2_ = bf16[192,512]{1,0:T(8,128)(2,1)S(1)} collective-permute-done((bf16[192,512]{1,0:T(8,128)(2,1)S(1)}, bf16[192,512]{1,0:T(8,128)(2,1)S(1)}, u32[]{:S(2)}, u32[]{:S(2)}) %collective-permute-start.7) | collective-permute-done | bytes 196640 | tf_op jit(solution)/shard_map/cond/branch_1_fun/ppermute | solution.py:26
  88.3 0.0 collective-permute-done.8.refs_5_
  88.3 1.6 merge.19
  89.9 0.0 collective-permute-done.9
  90.0 0.1 collective-permute-start.66
  90.0 0.5 collective-permute-start.67
  90.6 46.8 %conditional.4 = (bf16[128,2560]{1,0:T(8,128)(2,1)}, bf16[128,2560]{1,0:T(8,128)(2,1)}, bf16[224,1024]{1,0:T(8,128)(2,1)}, bf16[224,1024]{1,0:T(8,128)(2,1)}) conditional(s32[]{:T(128)} %bitcast.10, (s32[24]{0:T(128)S(1)}, bf16[128,5120]{1,0:T(8,128)(2,1)S(1)}, bf16[128,5120]{1,0:T(8,128)(2,1)S(1)}, ...), branch_computations={%region_6.0_spmd, %region_7.0_spmd, %region_8.0_spmd, %region_9.0_... | conditional | bytes 21233940 | solution.py:557
  90.6 1.3 collective-permute-start.37
  91.9 3.3 %rows.44 = (bf16[192,1536]{1,0:T(8,128)(2,1)S(1)}, bf16[128,1536]{1,0:T(8,128)(2,1)S(1)}, bf16[128,1536]{1,0:T(8,128)(2,1)S(1)}) custom-call(s32[24]{0:T(128)S(1)} %get-tuple-element.702.plan_ref, bf16[128,5120]{1,0:T(8,128)(2,1)S(1)} %get-tuple-element.688.x_ref, bf16[128,5120]{1,0:T(8,128)(2,1)S(1)} %get-tuple-element.689.dy_ref, ...), custom_call_target="tpu_custom_call" | custom-call | tf_op jit(solution)/shard_map/cond/branch_1_fun/rows/pallas_call | solution.py:298
  95.2 2.3 %collective-permute-start.38 = (bf16[192,1536]{1,0:T(8,128)(2,1)S(1)}, bf16[192,1536]{1,0:T(8,128)(2,1)S(1)}, u32[]{:S(2)}, u32[]{:S(2)}) collective-permute-start(bf16[192,1536]{1,0:T(8,128)(2,1)S(1)} %get-tuple-element.698), channel_id=1, source_target_pairs={{0,1},{1,0},{2,3},{3,2},{4,5},{5,4},{6,7},{7,6},{8,9},{9,8},{10,11... | collective-permute-start | bytes 1769480 | tf_op jit(solution)/shard_map/cond/branch_1_fun/ppermute | solution.py:26
  97.5 0.0 copy-done.20
  97.5 0.0 collective-permute-start.40
  97.5 15.6 %collective-permute-done.37.got_ref = bf16[224,1024]{1,0:T(8,128)(2,1)} collective-permute-done((bf16[224,1024]{1,0:T(8,128)(2,1)}, bf16[224,1024]{1,0:T(8,128)(2,1)}, u32[]{:S(2)}, u32[]{:S(2)}) %collective-permute-start.37) | collective-permute-done | bytes 458784 | tf_op jit(solution)/shard_map/cond/branch_1_fun/ppermute | solution.py:26
  113.1 0.0 copy-done.5
  113.1 0.0 copy-done.12
  113.2 1.9 %rows.45 = (bf16[192,1024]{1,0:T(8,128)(2,1)S(1)}, bf16[128,1024]{1,0:T(8,128)(2,1)S(1)}, bf16[128,1024]{1,0:T(8,128)(2,1)S(1)}) custom-call(s32[24]{0:T(128)S(1)} %get-tuple-element.702.plan_ref, bf16[128,5120]{1,0:T(8,128)(2,1)S(1)} %get-tuple-element.688.x_ref, bf16[128,5120]{1,0:T(8,128)(2,1)S(1)} %get-tuple-element.689.dy_ref, ...), custom_call_target="tpu_custom_call" | custom-call | tf_op jit(solution)/shard_map/cond/branch_1_fun/rows/pallas_call | solution.py:298
  115.1 0.5 collective-permute-start.39
  115.6 5.5 %collective-permute-done.38.refs_2_ = bf16[192,1536]{1,0:T(8,128)(2,1)S(1)} collective-permute-done((bf16[192,1536]{1,0:T(8,128)(2,1)S(1)}, bf16[192,1536]{1,0:T(8,128)(2,1)S(1)}, u32[]{:S(2)}, u32[]{:S(2)}) %collective-permute-start.38) | collective-permute-done | bytes 589856 | tf_op jit(solution)/shard_map/cond/branch_1_fun/ppermute | solution.py:26
  121.0 14.3 %collective-permute-done.39.refs_5_ = bf16[192,1024]{1,0:T(8,128)(2,1)S(1)} collective-permute-done((bf16[192,1024]{1,0:T(8,128)(2,1)S(1)}, bf16[192,1024]{1,0:T(8,128)(2,1)S(1)}, u32[]{:S(2)}, u32[]{:S(2)}) %collective-permute-start.39) | collective-permute-done | bytes 393248 | tf_op jit(solution)/shard_map/cond/branch_1_fun/ppermute | solution.py:26
  135.4 1.7 %merge.25 = (bf16[128,2560]{1,0:T(8,128)(2,1)}, bf16[128,2560]{1,0:T(8,128)(2,1)}) custom-call(s32[24]{0:T(128)S(1)} %get-tuple-element.702.plan_ref, bf16[128,1536]{1,0:T(8,128)(2,1)S(1)} %get-tuple-element.703.refs_0_, bf16[128,1536]{1,0:T(8,128)(2,1)S(1)} %get-tuple-element.704.refs_1_, bf16[192,1536]{1,0:T(8,128)(2,1)S(1)} %collective-permute-done.38.refs_2_, ...), custom_call_target="tpu_custom_call" | custom-call | tf_op jit(solution)/shard_map/cond/branch_1_fun/merge/pallas_call | solution.py:356
  137.1 0.0 collective-permute-done.40
  137.3 0.0 collective-permute-done.66.refs_5_
  137.3 0.0 collective-permute-done.67.refs_7_
  137.4 3.6 %collective-permute-start.69 = (bf16[128,2560]{1,0:T(8,128)(2,1)}, bf16[128,2560]{1,0:T(8,128)(2,1)S(1)}, u32[]{:S(2)}, u32[]{:S(2)}) collective-permute-start(bf16[128,2560]{1,0:T(8,128)(2,1)} %get-tuple-element.1025), channel_id=1, source_target_pairs={{4,0},{8,4},{12,8},{16,12},{20,16},{24,20},{28,24},{0,28},{5,1},{9... | collective-permute-start | bytes 1966088 | tf_op jit(solution)/shard_map/ppermute | solution.py:21
  140.9 0.0 collective-permute-start.68
  140.9 20.8 %conditional.5 = (bf16[128,1024]{1,0:T(8,128)(2,1)S(1)}, bf16[128,1024]{1,0:T(8,128)(2,1)S(1)}, bf16[32,5120]{1,0:T(8,128)(2,1)}, f32[1,1,5120,128]{3,2,1,0:T(8,128)S(1)}) conditional(s32[]{:T(128)} %bitcast.10, (s32[24]{0:T(128)S(1)}, bf16[128,5120]{1,0:T(8,128)(2,1)S(1)}, bf16[128,5120]{1,0:T(8,128)(2,1)}, ...), branch_computations={%region_12.0_spmd, %region_13.0_spmd, %region_14.0_spmd, %region_1... | conditional | bytes 2883696 | solution.py:557
  140.9 2.1 %rows.55 = (bf16[192,1024]{1,0:T(8,128)(2,1)S(1)}, bf16[128,1024]{1,0:T(8,128)(2,1)S(1)}, bf16[128,1024]{1,0:T(8,128)(2,1)S(1)}) custom-call(s32[24]{0:T(128)S(1)} %get-tuple-element.852.plan_ref, bf16[128,5120]{1,0:T(8,128)(2,1)S(1)} %get-tuple-element.859.x_ref, bf16[128,5120]{1,0:T(8,128)(2,1)} %get-tuple-element.842.dy_ref, ...), custom_call_target="tpu_custom_call" | custom-call | tf_op jit(solution)/shard_map/cond/branch_1_fun/rows/pallas_call | solution.py:298
  143.0 0.1 collective-permute-start.59
  143.1 2.4 %collective-permute-start.60 = (bf16[32,5120]{1,0:T(8,128)(2,1)}, bf16[32,5120]{1,0:T(8,128)(2,1)}, u32[]{:S(2)}, u32[]{:S(2)}) collective-permute-start(bf16[32,5120]{1,0:T(8,128)(2,1)} %get-tuple-element.858), channel_id=1, source_target_pairs={{0,2},{1,3},{2,0},{3,1},{4,6},{5,7},{6,4},{7,5},{8,10},{9,11},{10,... | collective-permute-start | bytes 983048 | tf_op jit(solution)/shard_map/cond/branch_1_fun/ppermute | solution.py:26
  145.5 2.7 %grad_down.7 = f32[5120,128]{1,0:T(8,128)S(1)} custom-call(bf16[128,5120]{1,0:T(8,128)(2,1)S(1)} %get-tuple-element.859.x_ref, bf16[256,128]{1,0:T(8,128)(2,1)S(1)} %get-tuple-element.844.low_ref, bf16[256,128]{1,0:T(8,128)(2,1)} %get-tuple-element.845.low2_ref, f32[8,128]{1,0:T(8,128)S(1)} %get-tuple-element.846.high_ref, ...), custom_call_target="tpu_custom_call" | custom-call | tf_op jit(solution)/shard_map/cond/branch_1_fun/grad_down/pallas_call | solution.py:424
  148.2 12.2 %collective-permute-done.59.refs_2_ = bf16[192,1024]{1,0:T(8,128)(2,1)S(1)} collective-permute-done((bf16[192,1024]{1,0:T(8,128)(2,1)S(1)}, bf16[192,1024]{1,0:T(8,128)(2,1)S(1)}, u32[]{:S(2)}, u32[]{:S(2)}) %collective-permute-start.59) | collective-permute-done | bytes 393248 | tf_op jit(solution)/shard_map/cond/branch_1_fun/ppermute | solution.py:26
  160.3 1.4 merge.31
  161.7 0.0 collective-permute-done.60
  161.8 0.0 copy-start.18
  161.8 0.0 collective-permute-done.69.refs_8_
  161.8 0.0 collective-permute-done.68.refs_6_
  161.8 1.4 collective-permute-start.71
  163.2 0.4 collective-permute-start.70
  163.6 5.1 %last.1 = (f32[128,5120]{1,0:T(8,128)}, bf16[128,5120]{1,0:T(8,128)(2,1)}, bf16[128,5120]{1,0:T(8,128)(2,1)}) custom-call(s32[24]{0:T(128)S(1)} %get-tuple-element.1001.plan_ref, bf16[256,128]{1,0:T(8,128)(2,1)S(1)} %get-tuple-element.1002.low_ref, bf16[256,128]{1,0:T(8,128)(2,1)} %get-tuple-element.1009.low2_ref, bf16[128,5120]{1,0:T(8,128)(2,1)} %bitcast.40, ...), custom_call_target="tpu_custom_call" | custom-call | tf_op jit(solution)/shard_map/last/pallas_call | solution.py:488
  168.7 0.0 copy-done.18
  168.7 0.0 collective-permute-done.71.refs_3_
  168.7 0.8 collective-permute-done.70.refs_2_
  169.5 0.8 join.1
  (8 shorter events, 0.0 us)
Async XLA Ops:
  1.4 0.7 copy-start
  2.1 6.7 %copy-start.1 = (bf16[1,1,128,5120]{3,2,1,0:T(8,128)(2,1)S(1)}, bf16[1,1,128,5120]{3,2,1,0:T(8,128)(2,1)}, u32[]{:S(2)}) copy-start(bf16[1,1,128,5120]{3,2,1,0:T(8,128)(2,1)} %param.25) | copy-start | bytes 3932164
  2.1 6.7 %copy-start.2 = (bf16[1,1,128,5120]{3,2,1,0:T(8,128)(2,1)S(1)}, bf16[1,1,128,5120]{3,2,1,0:T(8,128)(2,1)}, u32[]{:S(2)}) copy-start(bf16[1,1,128,5120]{3,2,1,0:T(8,128)(2,1)} %param.26) | copy-start | bytes 3932164
  2.1 6.7 %copy-start.3 = (bf16[1,5120,128]{2,1,0:T(8,128)(2,1)S(1)}, bf16[1,5120,128]{2,1,0:T(8,128)(2,1)}, u32[]{:S(2)}) copy-start(bf16[1,5120,128]{2,1,0:T(8,128)(2,1)} %param.28) | copy-start | bytes 3932164
  2.1 6.7 %copy-start.10 = (bf16[1,128,5120]{2,1,0:T(8,128)(2,1)S(1)}, bf16[1,128,5120]{2,1,0:T(8,128)(2,1)}, u32[]{:S(2)}) copy-start(bf16[1,128,5120]{2,1,0:T(8,128)(2,1)} %param.29) | copy-start | bytes 3932164
  2.1 6.7 %copy-start.17 = (f32[1,5120]{1,0:T(1,128)S(1)}, f32[1,5120]{1,0:T(1,128)}, u32[]{:S(2)}) copy-start(f32[1,5120]{1,0:T(1,128)} %g_ref.1) | copy-start | bytes 61444
  8.8 26.9 %collective-permute-start.5 = (bf16[304,512]{1,0:T(8,128)(2,1)S(1)}, bf16[304,512]{1,0:T(8,128)(2,1)}, u32[]{:S(2)}, u32[]{:S(2)}) collective-permute-start(bf16[304,512]{1,0:T(8,128)(2,1)S(1)} %get-tuple-element.535), channel_id=1, source_target_pairs={{0,2},{1,3},{2,0},{3,1},{4,6},{5,7},{6,4},{7,5},{8,10},{9,11},{10,... | collective-permute-start | bytes 933896 | tf_op jit(solution)/shard_map/cond/branch_1_fun/ppermute | solution.py:26
  12.0 48.3 %collective-permute-start.6 = (bf16[224,1024]{1,0:T(8,128)(2,1)S(1)}, bf16[224,1024]{1,0:T(8,128)(2,1)}, u32[]{:S(2)}, u32[]{:S(2)}) collective-permute-start(bf16[224,1024]{1,0:T(8,128)(2,1)S(1)} %get-tuple-element.545), channel_id=1, source_target_pairs={{0,2},{1,3},{2,0},{3,1},{4,6},{5,7},{6,4},{7,5},{8,10},{9,11},{10,... | collective-permute-start | bytes 1376264 | tf_op jit(solution)/shard_map/cond/branch_1_fun/ppermute | solution.py:26
  35.7 54.2 %collective-permute-start.9 = (bf16[224,1536]{1,0:T(8,128)(2,1)S(1)}, bf16[224,1536]{1,0:T(8,128)(2,1)}, u32[]{:S(2)}, u32[]{:S(2)}) collective-permute-start(bf16[224,1536]{1,0:T(8,128)(2,1)S(1)} %get-tuple-element.556), channel_id=1, source_target_pairs={{0,2},{1,3},{2,0},{3,1},{4,6},{5,7},{6,4},{7,5},{8,10},{9,11},{10,... | collective-permute-start | bytes 2064392 | tf_op jit(solution)/shard_map/cond/branch_1_fun/ppermute | solution.py:26
  62.2 26.1 %collective-permute-start.8 = (bf16[192,1024]{1,0:T(8,128)(2,1)S(1)}, bf16[192,1024]{1,0:T(8,128)(2,1)S(1)}, u32[]{:S(2)}, u32[]{:S(2)}) collective-permute-start(bf16[192,1024]{1,0:T(8,128)(2,1)S(1)} %get-tuple-element.546), channel_id=1, source_target_pairs={{0,1},{1,0},{2,3},{3,2},{4,5},{5,4},{6,7},{7,6},{8,9},{9,8},{10,11... | collective-permute-start | bytes 1179656 | tf_op jit(solution)/shard_map/cond/branch_1_fun/ppermute | solution.py:26
  63.3 25.0 %collective-permute-start.7 = (bf16[192,512]{1,0:T(8,128)(2,1)S(1)}, bf16[192,512]{1,0:T(8,128)(2,1)S(1)}, u32[]{:S(2)}, u32[]{:S(2)}) collective-permute-start(bf16[192,512]{1,0:T(8,128)(2,1)S(1)} %get-tuple-element.543), channel_id=1, source_target_pairs={{0,1},{1,0},{2,3},{3,2},{4,5},{5,4},{6,7},{7,6},{8,9},{9,8},{10,11... | collective-permute-start | bytes 589832 | tf_op jit(solution)/shard_map/cond/branch_1_fun/ppermute | solution.py:26
  90.0 47.4 %collective-permute-start.66 = (bf16[128,1536]{1,0:T(8,128)(2,1)}, bf16[128,1536]{1,0:T(8,128)(2,1)S(1)}, u32[]{:S(2)}, u32[]{:S(2)}) collective-permute-start(bf16[128,1536]{1,0:T(8,128)(2,1)} %get-tuple-element.1021), channel_id=1, source_target_pairs={{28,0},{0,4},{4,8},{8,12},{12,16},{16,20},{20,24},{24,28},{29,1},{... | collective-permute-start | bytes 1179656 | tf_op jit(solution)/shard_map/ppermute | solution.py:21
  90.0 47.3 %collective-permute-start.67 = (bf16[128,1536]{1,0:T(8,128)(2,1)}, bf16[128,1536]{1,0:T(8,128)(2,1)S(1)}, u32[]{:S(2)}, u32[]{:S(2)}) collective-permute-start(bf16[128,1536]{1,0:T(8,128)(2,1)} %get-tuple-element.1022), channel_id=1, source_target_pairs={{4,0},{8,4},{12,8},{16,12},{20,16},{24,20},{28,24},{0,28},{5,1},{9... | collective-permute-start | bytes 1179656 | tf_op jit(solution)/shard_map/ppermute | solution.py:21
  90.6 22.6 %collective-permute-start.37 = (bf16[224,1024]{1,0:T(8,128)(2,1)}, bf16[224,1024]{1,0:T(8,128)(2,1)}, u32[]{:S(2)}, u32[]{:S(2)}) collective-permute-start(bf16[224,1024]{1,0:T(8,128)(2,1)} %get-tuple-element.700), channel_id=1, source_target_pairs={{0,2},{1,3},{2,0},{3,1},{4,6},{5,7},{6,4},{7,5},{8,10},{9,11},{10,... | collective-permute-start | bytes 1376264 | tf_op jit(solution)/shard_map/cond/branch_1_fun/ppermute | solution.py:26
  91.9 5.6 %copy-start.20 = (bf16[224,1024]{1,0:T(8,128)(2,1)S(1)}, bf16[224,1024]{1,0:T(8,128)(2,1)}, u32[]{:S(2)}) copy-start(bf16[224,1024]{1,0:T(8,128)(2,1)} %get-tuple-element.710) | copy-start | bytes 1376260 | tf_op jit(solution)/shard_map/cond
  91.9 21.2 %copy-start.5 = (bf16[5120,128]{1,0:T(8,128)(2,1)S(1)}, bf16[5120,128]{1,0:T(8,128)(2,1)}, u32[]{:S(2)}) copy-start(bf16[5120,128]{1,0:T(8,128)(2,1)} %get-tuple-element.696.down_ref) | copy-start | bytes 3932164 | tf_op jit(solution)/shard_map/cond
  91.9 21.2 %copy-start.12 = (bf16[128,5120]{1,0:T(8,128)(2,1)S(1)}, bf16[128,5120]{1,0:T(8,128)(2,1)}, u32[]{:S(2)}) copy-start(bf16[128,5120]{1,0:T(8,128)(2,1)} %get-tuple-element.695.up_ref) | copy-start | bytes 3932164 | tf_op jit(solution)/shard_map/cond
  95.2 25.8 %collective-permute-start.38 = (bf16[192,1536]{1,0:T(8,128)(2,1)S(1)}, bf16[192,1536]{1,0:T(8,128)(2,1)S(1)}, u32[]{:S(2)}, u32[]{:S(2)}) collective-permute-start(bf16[192,1536]{1,0:T(8,128)(2,1)S(1)} %get-tuple-element.698), channel_id=1, source_target_pairs={{0,1},{1,0},{2,3},{3,2},{4,5},{5,4},{6,7},{7,6},{8,9},{9,8},{10,11... | collective-permute-start | bytes 1769480 | tf_op jit(solution)/shard_map/cond/branch_1_fun/ppermute | solution.py:26
  97.5 39.6 %collective-permute-start.40 = (bf16[224,1024]{1,0:T(8,128)(2,1)S(1)}, bf16[224,1024]{1,0:T(8,128)(2,1)}, u32[]{:S(2)}, u32[]{:S(2)}) collective-permute-start(bf16[224,1024]{1,0:T(8,128)(2,1)S(1)} %copy-done.20), channel_id=1, source_target_pairs={{0,2},{1,3},{2,0},{3,1},{4,6},{5,7},{6,4},{7,5},{8,10},{9,11},{10,... | collective-permute-start | bytes 1376264 | tf_op jit(solution)/shard_map/cond/branch_1_fun/ppermute | solution.py:26
  115.1 20.3 %collective-permute-start.39 = (bf16[192,1024]{1,0:T(8,128)(2,1)S(1)}, bf16[192,1024]{1,0:T(8,128)(2,1)S(1)}, u32[]{:S(2)}, u32[]{:S(2)}) collective-permute-start(bf16[192,1024]{1,0:T(8,128)(2,1)S(1)} %get-tuple-element.701), channel_id=1, source_target_pairs={{0,1},{1,0},{2,3},{3,2},{4,5},{5,4},{6,7},{7,6},{8,9},{9,8},{10,11... | collective-permute-start | bytes 1179656 | tf_op jit(solution)/shard_map/cond/branch_1_fun/ppermute | solution.py:26
  137.4 24.4 %collective-permute-start.69 = (bf16[128,2560]{1,0:T(8,128)(2,1)}, bf16[128,2560]{1,0:T(8,128)(2,1)S(1)}, u32[]{:S(2)}, u32[]{:S(2)}) collective-permute-start(bf16[128,2560]{1,0:T(8,128)(2,1)} %get-tuple-element.1025), channel_id=1, source_target_pairs={{4,0},{8,4},{12,8},{16,12},{20,16},{24,20},{28,24},{0,28},{5,1},{9... | collective-permute-start | bytes 1966088 | tf_op jit(solution)/shard_map/ppermute | solution.py:21
  140.9 20.9 %collective-permute-start.68 = (bf16[128,2560]{1,0:T(8,128)(2,1)}, bf16[128,2560]{1,0:T(8,128)(2,1)S(1)}, u32[]{:S(2)}, u32[]{:S(2)}) collective-permute-start(bf16[128,2560]{1,0:T(8,128)(2,1)} %get-tuple-element.1023), channel_id=1, source_target_pairs={{28,0},{0,4},{4,8},{8,12},{12,16},{16,20},{20,24},{24,28},{29,1},{... | collective-permute-start | bytes 1966088 | tf_op jit(solution)/shard_map/ppermute | solution.py:21
  143.0 17.3 %collective-permute-start.59 = (bf16[192,1024]{1,0:T(8,128)(2,1)S(1)}, bf16[192,1024]{1,0:T(8,128)(2,1)S(1)}, u32[]{:S(2)}, u32[]{:S(2)}) collective-permute-start(bf16[192,1024]{1,0:T(8,128)(2,1)S(1)} %get-tuple-element.851), channel_id=1, source_target_pairs={{0,1},{1,0},{2,3},{3,2},{4,5},{5,4},{6,7},{7,6},{8,9},{9,8},{10,11... | collective-permute-start | bytes 1179656 | tf_op jit(solution)/shard_map/cond/branch_1_fun/ppermute | solution.py:26
  143.1 18.6 %collective-permute-start.60 = (bf16[32,5120]{1,0:T(8,128)(2,1)}, bf16[32,5120]{1,0:T(8,128)(2,1)}, u32[]{:S(2)}, u32[]{:S(2)}) collective-permute-start(bf16[32,5120]{1,0:T(8,128)(2,1)} %get-tuple-element.858), channel_id=1, source_target_pairs={{0,2},{1,3},{2,0},{3,1},{4,6},{5,7},{6,4},{7,5},{8,10},{9,11},{10,... | collective-permute-start | bytes 983048 | tf_op jit(solution)/shard_map/cond/branch_1_fun/ppermute | solution.py:26
  161.8 6.9 %copy-start.18 = (f32[1,1,5120,128]{3,2,1,0:T(8,128)}, f32[1,1,5120,128]{3,2,1,0:T(8,128)S(1)}, u32[]{:S(2)}) copy-start(f32[1,1,5120,128]{3,2,1,0:T(8,128)S(1)} %get-tuple-element.999) | copy-start | bytes 7864324
  161.8 6.9 %collective-permute-start.71 = (bf16[128,1024]{1,0:T(8,128)(2,1)S(1)}, bf16[128,1024]{1,0:T(8,128)(2,1)S(1)}, u32[]{:S(2)}, u32[]{:S(2)}) collective-permute-start(bf16[128,1024]{1,0:T(8,128)(2,1)S(1)} %get-tuple-element.1028), channel_id=1, source_target_pairs={{4,0},{8,4},{12,8},{16,12},{20,16},{24,20},{28,24},{0,28},{5,1},{9... | collective-permute-start | bytes 786440 | tf_op jit(solution)/shard_map/ppermute | solution.py:21
  163.2 6.3 %collective-permute-start.70 = (bf16[128,1024]{1,0:T(8,128)(2,1)S(1)}, bf16[128,1024]{1,0:T(8,128)(2,1)S(1)}, u32[]{:S(2)}, u32[]{:S(2)}) collective-permute-start(bf16[128,1024]{1,0:T(8,128)(2,1)S(1)} %get-tuple-element.1026), channel_id=1, source_target_pairs={{28,0},{0,4},{4,8},{8,12},{12,16},{16,20},{20,24},{24,28},{29,1},{... | collective-permute-start | bytes 786440 | tf_op jit(solution)/shard_map/ppermute | solution.py:21
